TPU v7x, 512 devices: a whole 4x8x8 slice. The times are simulated.
512 devices in a mesh: dp: 8 (over z_lo, core), feat: 64 (over y, x, z_hi).
Axes of the slice: x: 4, y: 8, z: 8 (z_hi: 2, z_lo: 4; z = z_hi * 4 + z_lo), core: 2. Of those that a mesh axis runs over, the one named last changes fastest.
Arguments:
- samples: bfloat16 [8192, 128], P('dp'), may hold values from -6 to 6
- projection: bfloat16 [128, 131072], P(None, ('dp', 'feat')), may hold values from -0.5 to 0.5
- phase_shift: bfloat16 [1, 131072], P(None, ('dp', 'feat')), may hold values from 0 to 6.28125
- solution: float32 [131072, 128], P(('dp', 'feat')), may hold values from -6 to 6
- residual: float32 [131072, 128], P(('dp', 'feat')), may hold values from -6 to 6
- direction: float32 [131072, 128], P(('dp', 'feat')), may hold values from -6 to 6
Outputs:
- solution_next: float32 [131072, 128], P(('dp', 'feat'))
- residual_next: float32 [131072, 128], P(('dp', 'feat'))
- direction_next: float32 [131072, 128], P(('dp', 'feat'))
All inputs are finite; a program needn't handle non-finite values.
Results may differ from a plain program's by a relative error of at most 0.0015.
The roundings to bfloat16 on the way count: a program that leaves them out, or rounds other values in their place, can miss the bound.
Values may be sent and summed in bfloat16 or wider, within the bound.
No kernel may reach another device: no remote copies, remote signals or barrier semaphores. Data moves between devices by JAX's collectives and lax.ppermute only.
A program may use at most 64 MiB of HBM per device.

v0:
```python
import math

import jax
import jax.numpy as jnp
from jax import lax
from jax.sharding import PartitionSpec as P

FEATURES = 131072


penalty = 0.1
highest = lax.Precision.HIGHEST


def features(rows, proj_cols, shift_cols):
    phase = jnp.dot(rows, proj_cols, preferred_element_type=jnp.float32) + shift_cols.astype(
        jnp.float32
    )
    return (math.sqrt(2.0 / FEATURES) * jnp.cos(phase)).astype(jnp.bfloat16)


def symmetric(matrix):
    return 0.5 * (matrix + matrix.T)


def definite_solve(matrix, rhs):
    lower = jnp.linalg.cholesky(matrix)
    middle = lax.linalg.triangular_solve(lower, rhs, left_side=True, lower=True)
    return lax.linalg.triangular_solve(lower, middle, left_side=True, lower=True, transpose_a=True)


def local_gram(left, right):
    return jnp.dot(left.T, right, precision=highest, preferred_element_type=jnp.float32)


def local(samples, projection, phase_shift, solution, residual, direction):
    proj_cols, shift_cols = (
        lax.all_gather(projection, "dp", axis=1, tiled=True),
        lax.all_gather(phase_shift, "dp", axis=1, tiled=True),
    )
    dir_rows = lax.all_gather(direction.astype(jnp.bfloat16), "dp", axis=0, tiled=True)
    row_count = samples.shape[0]
    in_width = samples.shape[1]
    targets = direction.shape[1]
    slab_count = samples.shape[0]
    block_size = math.gcd(slab_count, 256)
    row_blocks = samples.reshape(slab_count // block_size, block_size, in_width)

    def one_block(row_block):
        return jnp.dot(
            features(row_block, proj_cols, shift_cols), dir_rows, preferred_element_type=jnp.float32
        )

    stacked = lax.map(one_block, row_blocks)
    row_low = lax.psum(stacked.reshape(slab_count, targets), "feat").astype(jnp.bfloat16)
    block_size = math.gcd(row_count, 256)
    sample_blocks = samples.reshape(row_count // block_size, block_size, in_width)
    sum_blocks = row_low.reshape(row_count // block_size, block_size, targets)

    def advance(running, items):
        row_block, sum_block = items
        feats = features(row_block, proj_cols, shift_cols)
        return (
            running
            + lax.dot_general(
                feats, sum_block, (((0,), (0,)), ((), ())), preferred_element_type=jnp.float32
            ),
            None,
        )

    running, unused = lax.scan(
        advance,
        jnp.zeros((direction.shape[0] * lax.axis_size("dp"), targets), jnp.float32),
        (sample_blocks, sum_blocks),
    )
    applied = lax.psum_scatter(running, "dp", scatter_dimension=0, tiled=True) + penalty * direction
    res_gram = lax.psum(local_gram(residual, residual), ("dp", "feat"))
    dir_gram = lax.psum(local_gram(direction, applied), ("dp", "feat"))
    res_gram = symmetric(res_gram)
    dir_gram = symmetric(dir_gram)
    step_coef = definite_solve(dir_gram, res_gram)
    solution_next = solution + jnp.dot(
        direction, step_coef, precision=highest, preferred_element_type=jnp.float32
    )
    residual_next = residual - jnp.dot(
        applied, step_coef, precision=highest, preferred_element_type=jnp.float32
    )
    res_gram_next = symmetric(lax.psum(local_gram(residual_next, residual_next), ("dp", "feat")))
    mix_coef = definite_solve(res_gram, res_gram_next)
    direction_next = residual_next + jnp.dot(
        direction, mix_coef, precision=highest, preferred_element_type=jnp.float32
    )
    return (solution_next, residual_next, direction_next)


def solution(mesh):
    in_specs = (
        P("dp", None),
        P(None, ("dp", "feat")),
        P(None, ("dp", "feat")),
        P(("dp", "feat"), None),
        P(("dp", "feat"), None),
        P(("dp", "feat"), None),
    )
    out_specs = (P(("dp", "feat"), None), P(("dp", "feat"), None), P(("dp", "feat"), None))
    return jax.shard_map(local, mesh=mesh, in_specs=in_specs, out_specs=out_specs, check_vma=False)
```

profile of v0, /device:TPU:1, one launch (start us, length us, event | category | flops | bytes accessed | tf_op | source)
XLA Modules:
  0.0 1157.0 jit_solution(4294634282219274461)
XLA Ops:
  7.2 21.8 %all_gather.9 = bf16[128,2048]{1,0:T(8,128)(2,1)S(1)} all-gather(bf16[128,256]{1,0:T(8,128)(2,1)} %param.16), channel_id=1, replica_groups=mesh['dp'=8,'feat'=64] {'dp'}, dimensions={1}, use_global_device_ids=true | all-gather | bytes 589824 | tf_op jit(solution)/shard_map/all_gather | solution.py:38
  29.1 9.3 all_gather.10
  39.3 14.7 %all_gather.11 = bf16[2048,128]{1,0:T(8,128)(2,1)S(1)} all-gather(bf16[256,128]{1,0:T(8,128)(2,1)S(1)} %convert_element_type.34), channel_id=1, replica_groups=mesh['dp'=8,'feat'=64] {'dp'}, dimensions={0}, use_global_device_ids=true | all-gather | bytes 589824 | tf_op jit(solution)/shard_map/all_gather | solution.py:41
  54.0 29.0 %while.21 = (s32[]{:T(128)}, f32[4,256,128]{2,1,0:T(8,128)S(1)}, bf16[4,256,128]{2,1,0:T(8,128)(2,1)S(1)}, bf16[128,2048]{1,0:T(8,128)(2,1)S(1)}, bf16[1,2048]{1...) while((s32[]{:T(128)}, f32[4,256,128]{2,1,0:T(8,128)S(1)}, ...), condition=%wide.region_1.2_spmd, body=%wide.region_0.1_spmd.sunk | while | flops 270010368 | bytes 1266765 | solution.py:54
  54.0 7.2 fusion.81
  61.3 7.2 fusion.81
  68.5 7.2 fusion.81
  75.8 7.2 fusion.81
  83.0 388.5 %all-reduce.8 = bf16[1024,128]{1,0:T(8,128)(2,1)S(1)} all-reduce(f32[1024,128]{1,0:T(8,128)S(1)} %bitcast.103), channel_id=1, replica_groups=mesh['dp'=8,'feat'=64] {'feat'}, use_global_device_ids=true, to_apply=%region_2.3 | all-reduce | flops 131072 | bytes 786432 | tf_op jit(solution)/shard_map/psum | solution.py:55
  471.5 29.8 %while.22 = (s32[]{:T(128)}, f32[2048,128]{1,0:T(8,128)S(1)}, bf16[4,256,128]{2,1,0:T(8,128)(2,1)S(1)}, bf16[128,2048]{1,0:T(8,128)(2,1)S(1)}, bf16[1,2048]{1,0:...) while((s32[]{:T(128)}, f32[2048,128]{1,0:T(8,128)S(1)}, ...), condition=%wide.region_4.5_spmd.clone, body=%wide.region_3.4_spmd.clone.sunk | while | flops 270534656 | bytes 2774111 | solution.py:71
  471.5 7.4 convolution_add_fusion.4
  478.9 7.4 convolution_add_fusion.4
  486.4 7.4 convolution_add_fusion.4
  493.8 7.4 convolution_add_fusion.4
  502.3 1.0 fusion.53
  503.3 81.6 %reduce-scatter.2.cloned.1.call-done = f32[256,128]{1,0:T(8,128)} async-done(((f32[2048,128]{1,0:T(8,128)}), f32[256,128]{1,0:T(8,128)}) %reduce-scatter.2.cloned.1.call-update) | async-done | bytes 131088 | tf_op jit(solution)/shard_map/reduce_scatter | solution.py:76
  584.9 1.9 convolution_bitcast_fusion.2
  587.2 267.4 %all-reduce.7.cloned.1.call-done = (f32[128,128]{1,0:T(8,128)}, f32[128,128]{1,0:T(8,128)}) async-done(((f32[128,128]{1,0:T(8,128)}, f32[128,128]{1,0:T(8,128)}), (f32[128,128]{1,0:T(8,128)}, f32[128,128]{1,0:T(8,128)})) %all-reduce.7.cloned.1.call-update) | async-done | bytes 131088 | tf_op jit(solution)/shard_map/psum | solution.py:77
  857.5 11.7 %cholesky.55 = f32[128,128]{1,0:T(8,128)S(1)} custom-call(f32[128,128]{1,0:T(8,128)S(1)} %fusion.39), custom_call_target="Cholesky" | custom-call | tf_op jit(solution)/shard_map/jit(cholesky)/cholesky | solution.py:27
  870.0 11.7 %cholesky.44 = f32[128,128]{1,0:T(8,128)S(1)} custom-call(f32[128,128]{1,0:T(8,128)S(1)} %fusion.45), custom_call_target="Cholesky" | custom-call | tf_op jit(solution)/shard_map/jit(cholesky)/cholesky | solution.py:27
  883.0 9.8 custom-call.12
  895.7 9.8 custom-call.14
  906.3 241.0 %all-reduce.5.cloned.1.call-done = f32[128,128]{1,0:T(8,128)} async-done(((f32[128,128]{1,0:T(8,128)}), f32[128,128]{1,0:T(8,128)}) %all-reduce.5.cloned.1.call-update) | async-done | bytes 65552 | tf_op jit(solution)/shard_map/psum | solution.py:88
  1148.2 1.1 fusion.34
  (54 shorter events, 13.0 us)
Async XLA Ops:
  7.2 46.8 %copy-start.6 = (bf16[1024,128]{1,0:T(8,128)(2,1)S(1)}, bf16[1024,128]{1,0:T(8,128)(2,1)}, u32[]{:S(2)}) copy-start(bf16[1024,128]{1,0:T(8,128)(2,1)} %param.15) | copy-start | bytes 786436
  7.2 577.7 %reduce-scatter.2.cloned.1.call-start = ((), (), s32[]{:S(2)}) async-start(), calls=%async_computation.1 | async-start | bytes 1179648 | tf_op jit(solution)/shard_map/reduce_scatter | solution.py:76
  501.2 1.0 copy-start.3
  501.2 1.1 copy-start.2
  501.2 83.6 %copy-start = (f32[256,128]{1,0:T(8,128)S(1)}, f32[256,128]{1,0:T(8,128)}, u32[]{:S(2)}) copy-start(f32[256,128]{1,0:T(8,128)} %param.20) | copy-start | bytes 393220
  501.3 85.8 %copy-start.5 = (f32[256,128]{1,0:T(8,128)S(1)}, f32[256,128]{1,0:T(8,128)}, u32[]{:S(2)}) copy-start(f32[256,128]{1,0:T(8,128)} %param.18) | copy-start | bytes 393220
  502.2 352.4 %all-reduce.7.cloned.1.call-start = ((), (), s32[]{:S(2)}) async-start(), calls=%async_computation.3 | async-start | bytes 262144 | tf_op jit(solution)/shard_map/psum | solution.py:77
  586.8 560.4 %all-reduce.5.cloned.1.call-start = ((), (), s32[]{:S(2)}) async-start(), calls=%async_computation.2 | async-start | bytes 131072 | tf_op jit(solution)/shard_map/psum | solution.py:88
  587.2 306.2 %copy-start.4 = (f32[256,128]{1,0:T(8,128)S(1)}, f32[256,128]{1,0:T(8,128)}, u32[]{:S(2)}) copy-start(f32[256,128]{1,0:T(8,128)} %reduce-scatter.2.cloned.1.call-done) | copy-start | bytes 393220
  893.6 256.8 %copy-start.1 = (f32[256,128]{1,0:T(8,128)}, f32[256,128]{1,0:T(8,128)S(1)}, u32[]{:S(2)}) copy-start(f32[256,128]{1,0:T(8,128)S(1)} %convolution_subtract_fusion) | copy-start | bytes 393220
Sparse Core Ops, SparseCore 0:
  502.4 82.4 reduce-scatter.1
  590.7 263.8 all-reduce.6
  894.8 252.3 all-reduce.4
where the time goes:
time: 1160 us
  waiting for transfers between devices  590 us (51%)
  blocking collectives  434 us (37%)
  matrix products  65.7 us (6%)
  other arithmetic  47.6 us (4%)
  between operations  14 us (1%)
    psum x1, blocking collectives, local(): lax.psum(stacked.reshape(slab_count, targets), 'feat').astype(jnp.bfloat16)  388 us
    psum x1, waiting for transfers between devices, local(): res_gram = lax.psum(local_gram(residual, residual), ('dp', 'feat'))  267 us
    psum x1, waiting for transfers between devices, local(): lax.psum(local_gram(residual_next, residual_next), ('dp', 'feat'))  241 us
    reduce_scatter x1, waiting for transfers between devices, local(): lax.psum_scatter(running, 'dp', scatter_dimension=0, tiled=True)  81.6 us
    dot_general x4, matrix products, advance(): lax.dot_general(feats, sum_block, (((0,), (0,)), ((), ())), preferred_ele...  29.6 us
    dot_general x4, matrix products, one_block(): jnp.dot(features(row_block, proj_cols, shift_cols), dir_rows, preferred_e...  28.8 us
    another operation x6, other arithmetic, definite_solve(): lower = jnp.linalg.cholesky(matrix)  24.8 us
  transfers between devices with their start and end apart: 3, of which 3 were waited for; matrix products, arithmetic and copies ran while one was open for 1% of the time, Pallas kernels for 0%

commit v1 on v0

v1 whole, which is shorter than its diff:
```python
import math

import jax
import jax.numpy as jnp
from jax import lax
from jax.experimental import pallas as pl
from jax.experimental.pallas import tpu as pltpu
from jax.sharding import Mesh, PartitionSpec as P

FEATURES = 131072
penalty = 0.1
highest = lax.Precision.HIGHEST
f32 = jnp.float32
bf16 = jnp.bfloat16

SINE = (6.283164044300415, -41.33714237083587, 81.34076887919463, -70.99343319457358)
SCALE = math.sqrt(2.0 / FEATURES)
ROUNDER = 12582912.0
PACK = 272
KDIM = 144
GRAM = 384

AXES = ("z2", "z1", "core", "y4", "y2", "y1", "x2", "x1", "zhi")
DP = ("z2", "z1", "core")
Z = ("z2", "z1")
ROW_NEAR = ("x2", "x1", "y1")
ROW_FAR = ("y4", "y2", "zhi")
GRAM_A = ("core", "x1", "y1")
GRAM_B = ("y4", "zhi", "x2")
GRAM_C = ("y2", "z2", "z1")


def vmem():
    return pl.BlockSpec(memory_space=pltpu.VMEM)


def call(kernel, outs, *args, scratch=(), flops=0, nbytes=0):
    return pl.pallas_call(
        kernel,
        out_shape=outs,
        in_specs=[vmem()] * len(args),
        out_specs=jax.tree.map(lambda _: vmem(), outs),
        scratch_shapes=list(scratch),
        compiler_params=pltpu.CompilerParams(vmem_limit_bytes=16 * 1024 * 1024),
        cost_estimate=pl.CostEstimate(flops=flops, bytes_accessed=nbytes, transcendentals=0),
    )(*args)


def struct(shape, dtype=f32):
    return jax.ShapeDtypeStruct(shape, dtype)


def pack_kernel(proj_ref, shift_ref, dir_ref, out_ref):
    shift = jnp.broadcast_to(shift_ref[...].astype(f32), (16, 256))
    first = lax.broadcasted_iota(jnp.int32, (16, 256), 0) == 0
    shift = jnp.where(first, shift, 0.0).astype(bf16)
    low = dir_ref[...].T.astype(bf16)
    for z in range(4):
        out_ref[z, 0:128, :] = proj_ref[...]
        out_ref[z, 128:144, :] = shift
        out_ref[z, 144:272, :] = low


def scaled_cos(phase):
    turns = phase * (1.0 / (2.0 * math.pi))
    turns = turns - ((turns + ROUNDER) - ROUNDER)
    w = 0.25 - jnp.abs(turns)
    z = w * w
    acc = SINE[3] * SCALE
    for c in (SINE[2], SINE[1], SINE[0]):
        acc = acc * z + c * SCALE
    return acc * w


def feature_steps(rows_t, pack_ref, feats_ref, acc):
    @pl.loop(0, 4)
    def _(s):
        piece = pack_ref.at[s]
        dir_t = piece[144:272, :]
        for r in range(4):
            cols = slice(r * 256, (r + 1) * 256)
            phase = lax.dot_general(
                piece[0:KDIM, :], rows_t[:, cols], (((0,), (0,)), ((), ())), preferred_element_type=f32
            )
            feats = scaled_cos(phase).astype(bf16)
            feats_ref[s, :, cols] = feats
            acc[:, cols] += jnp.dot(dir_t, feats, preferred_element_type=f32)


def own_features(samples_ref, pack_ref, feats_ref, acc, rows_t):
    rows_t[0:128, :] = samples_ref[...].T
    one = lax.broadcasted_iota(jnp.int32, (16, 1024), 0) == 0
    rows_t[128:144, :] = jnp.where(one, 1.0, 0.0).astype(bf16)
    acc[...] = jnp.zeros_like(acc)
    feature_steps(rows_t, pack_ref, feats_ref, acc)


def other_features(rows_t, acc_in, pack_ref, feats_ref, sums_ref, acc):
    acc[...] = acc_in[...]
    feature_steps(rows_t, pack_ref, feats_ref, acc)
    sums_ref[...] = acc[...].T


def sum_low_kernel(in_ref, out_ref):
    total = in_ref[0]
    for i in range(1, 8):
        total = total + in_ref[i]
    low = total.astype(bf16)
    for i in range(8):
        out_ref[i] = low


def sum_kernel(in_ref, out_ref):
    total = in_ref[0]
    for i in range(1, 8):
        total = total + in_ref[i]
    out_ref[...] = total


def sum_copies_kernel(in_ref, out_ref):
    total = in_ref[0]
    for i in range(1, 8):
        total = total + in_ref[i]
    for i in range(8):
        out_ref[i] = total


def back_kernel(feats_ref, low_ref, out_ref):
    for s in range(4):
        out_ref[s] = jnp.dot(feats_ref[s], low_ref[...], preferred_element_type=f32)


def fdot(a, b):
    return jnp.dot(a, b, precision=highest, preferred_element_type=f32)


def sym(m):
    return 0.5 * (m + m.T)


def places():
    n = 128
    return lax.broadcasted_iota(jnp.int32, (n, n), 0), lax.broadcasted_iota(jnp.int32, (n, n), 1)


def gram_kernel(parts_ref, dir_ref, res_ref, applied_ref, gram_ref):
    total = (parts_ref[0] + parts_ref[1]) + (parts_ref[2] + parts_ref[3])
    applied = total + penalty * dir_ref[...]
    applied_ref[...] = applied
    applied_t = applied.T
    dir_gram = sym(fdot(applied_t, dir_ref[...]))
    applied_gram = fdot(applied_t, applied)
    res_gram = sym(fdot(res_ref[...].T, res_ref[...]))
    at_row, at_col = places()
    diag = jnp.sum(jnp.where(at_row == at_col, applied_gram, 0.0), axis=1, keepdims=True)
    gram_ref[0:128, :] = jnp.where(at_col >= at_row, dir_gram, applied_gram)
    gram_ref[128:256, :] = fdot(applied_t, res_ref[...])
    gram_ref[256:384, :] = jnp.where(
        at_col >= at_row, res_gram, jnp.where(at_col == 0, diag, diag[0:1, 0:1])
    )


def lower_inverses(mats):
    n = 128
    lane = lax.broadcasted_iota(jnp.int32, (8, n), 1)
    sub = lax.broadcasted_iota(jnp.int32, (8, n), 0)
    lane1 = lane[0:1]
    tiles = [[m[8 * i : 8 * i + 8, :] for i in range(16)] for m in mats]
    for k in range(0, n, 2):
        home, at = divmod(k, 8)
        pair = (lane == k) | (lane == k + 1)
        for t in tiles:
            row_a = t[home][at : at + 1, :]
            row_b = t[home][at + 1 : at + 2, :]
            inv_a = 1.0 / row_a[:, k : k + 1]
            cross = row_b[:, k : k + 1]
            ratio = row_a[:, k + 1 : k + 2] * inv_a
            inv_b = 1.0 / (row_b[:, k + 1 : k + 2] - cross * ratio)
            low_a = jnp.where(lane1 == k, inv_a, row_a * inv_a)
            new_b = jnp.where(lane1 == k, 0.0, row_b) - cross * low_a
            low_b = jnp.where(lane1 == k + 1, inv_b, new_b * inv_b)
            low_a8 = jnp.broadcast_to(jnp.where(lane1 == k + 1, 0.0, low_a), (8, n))
            low_b8 = jnp.broadcast_to(low_b, (8, n))
            for i in range(home, 16):
                if i == home and at == 6:
                    t[i] = jnp.where(sub == at + 1, jnp.broadcast_to(new_b, (8, n)), t[i])
                    continue
                old = t[i]
                col_a = jnp.broadcast_to(old[:, k : k + 1], (8, n))
                col_b = jnp.broadcast_to(old[:, k + 1 : k + 2], (8, n)) - col_a * ratio
                new = jnp.where(pair, 0.0, old) - col_a * low_a8 - col_b * low_b8
                if i == home:
                    new = jnp.where(sub > at + 1, new, old)
                    new = jnp.where(sub == at + 1, jnp.broadcast_to(new_b, (8, n)), new)
                t[i] = new
    out = []
    at_row, at_col = places()
    for t in tiles:
        full = jnp.concatenate(t, axis=0)
        diag = jnp.sum(jnp.where(at_row == at_col, full, 0.0), axis=1, keepdims=True)
        inv = jnp.where(at_row > at_col, full, jnp.where(at_row == at_col, 1.0, 0.0))
        out.append((inv, 1.0 / diag))
    return out


def final_kernel(gram_ref, applied_ref, dir_ref, res_ref, sol_ref, sol_out, res_out, dir_out):
    at_row, at_col = places()
    first, cross, third = (gram_ref[128 * i : 128 * i + 128, :] for i in range(3))
    first_t, third_t = first.T, third.T
    dir_gram = jnp.where(at_col >= at_row, first, first_t)
    res_gram = jnp.where(at_col >= at_row, third, third_t)
    diag = jnp.where(at_row == 0, third[127:128, 1:2], third[:, 0:1])
    applied_gram = jnp.where(at_col < at_row, first, jnp.where(at_col == at_row, diag, first_t))
    (inv_d, scale_d), (inv_r, scale_r) = lower_inverses([dir_gram, res_gram])
    step = fdot(inv_d.T, scale_d * fdot(inv_d, res_gram))
    step_t = step.T
    sol_out[...] = sol_ref[...] + fdot(dir_ref[...], step)
    res_next = res_ref[...] - fdot(applied_ref[...], step)
    res_out[...] = res_next
    both = fdot(step_t, cross)
    gram_next = sym(res_gram - both - both.T + fdot(step_t, fdot(applied_gram, step)))
    mix = fdot(inv_r.T, scale_r * fdot(inv_r, gram_next))
    dir_out[...] = res_next + fdot(dir_ref[...], mix)


def swap_core(value):
    return lax.ppermute(value, "core", [(0, 1), (1, 0)])


def exchange(value, axes):
    return lax.all_to_all(value, axes, 0, 0)


def local(samples, projection, phase_shift, solution, residual, direction):
    pack = call(pack_kernel, struct((4, PACK, 256), bf16), projection, phase_shift, direction)
    own = exchange(pack, Z)
    other = swap_core(own)
    work = 2 * 2 * 1024 * 1024 * 128
    own_feats, acc, rows_t = call(
        own_features,
        [struct((4, 256, 1024), bf16), struct((128, 1024)), struct((KDIM, 1024), bf16)],
        samples,
        own,
        flops=10 * work,
    )
    other_feats, sums = call(
        other_features,
        [struct((4, 256, 1024), bf16), struct((1024, 128))],
        rows_t,
        acc,
        other,
        scratch=[pltpu.VMEM((128, 1024), f32)],
        flops=10 * work,
    )
    near = exchange(sums.reshape(8, 128, 128), ROW_NEAR)
    near = call(sum_kernel, struct((128, 128)), near)
    far = exchange(near.reshape(8, 16, 128), ROW_FAR)
    far = call(sum_low_kernel, struct((8, 16, 128), bf16), far)
    low = exchange(far, ROW_FAR).reshape(128, 128)
    low = exchange(jnp.broadcast_to(low[None], (8, 128, 128)), ROW_NEAR).reshape(1024, 128)
    theirs = call(back_kernel, struct((4, 256, 128)), other_feats, low, flops=work // 2)
    theirs = swap_core(theirs)
    mine = call(back_kernel, struct((4, 256, 128)), own_feats, low, flops=work // 2)
    parts = exchange(mine + theirs, Z)
    applied, gram = call(
        gram_kernel, [struct((256, 128)), struct((GRAM, 128))], parts, direction, residual
    )
    chunk = GRAM // 8
    piece = exchange(gram.reshape(8, chunk, 128), GRAM_A)
    for axes in (GRAM_B, GRAM_C, GRAM_A):
        piece = call(sum_copies_kernel, struct((8, chunk, 128)), piece)
        piece = exchange(piece, axes)
    return call(
        final_kernel,
        [struct((256, 128))] * 3,
        piece.reshape(GRAM, 128),
        applied,
        direction,
        residual,
        solution,
    )


def solution(mesh):
    fine = Mesh(mesh.devices.reshape((2,) * 9), AXES)
    rows, cols, state = P(DP, None), P(None, AXES), P(AXES, None)
    return jax.shard_map(
        local,
        mesh=fine,
        in_specs=(rows, cols, cols, state, state, state),
        out_specs=(state, state, state),
        check_vma=False,
    )
```

time: 1160 us -> 201 us (0.17)
  waiting for transfers between devices: 590 us -> 0.79 us
  blocking collectives: 434 us -> 150 us
  matrix products: 65.7 us -> 0 us
  other arithmetic: 47.6 us -> 0.05 us
  Pallas kernels: 0 us -> 34.9 us
  between operations: 14 us -> 0.77 us
    psum x2 -> x0, waiting for transfers between devices: 508 us -> none  [the longest x1 267 us: local(): res_gram = lax.psum(local_gram(residual, residual), ('dp', 'feat'))]
    psum x1 -> x0, blocking collectives: 388 us -> none  [local(): lax.psum(stacked.reshape(slab_count, targets), 'feat').astype(jnp.bfloat16)]
    all_to_all x0 -> x10, blocking collectives: none -> 150 us  [exchange(): return lax.all_to_all(value, axes, 0, 0)]
    reduce_scatter x1 -> x0, waiting for transfers between devices: 81.6 us -> none  [local(): lax.psum_scatter(running, 'dp', scatter_dimension=0, tiled=True)]
    dot_general x14 -> x0, matrix products: 63.9 us -> none  [the longest x4 29.6 us: advance(): lax.dot_general(feats, sum_block, (((0,), (0,)), ((), ())), preferred_ele...]
    all_gather x3 -> x0, blocking collectives: 45.8 us -> none  [the longest x1 21.8 us: local(): lax.all_gather(projection, 'dp', axis=1, tiled=True)]
    another operation x10 -> x0, other arithmetic: 45.7 us -> none  [the longest x6 24.8 us: definite_solve(): lower = jnp.linalg.cholesky(matrix)]
    pallas_call x0 -> x12, Pallas kernels: none -> 34.9 us  [call(): pl.pallas_call(kernel, out_shape=outs, in_specs=[vmem()] * len(args), out...]
  transfers between devices with their start and end apart: 3 -> 2, of which waited for: 3 -> 1; matrix products, arithmetic and copies ran while one was open for 1% -> 0% of each run, Pallas kernels for 0% -> 3%
where the time goes in v1:
time: 201 us; the launch traced here: 200 us
  blocking collectives  150 us (75%)
  Pallas kernels  34.9 us (17%)
  starting transfers between devices  10.7 us (5%)
  local copies, waits for them, and re-layouts  3.42 us (2%)
    all_to_all x10, blocking collectives, exchange(): return lax.all_to_all(value, axes, 0, 0)  150 us
    pallas_call x12, Pallas kernels, call(): pl.pallas_call(kernel, out_shape=outs, in_specs=[vmem()] * len(args), out...  34.9 us
    ppermute x2, starting transfers between devices, swap_core(): return lax.ppermute(value, 'core', [(0, 1), (1, 0)])  10.7 us
  transfers between devices with their start and end apart: 2, of which 1 were waited for; matrix products, arithmetic and copies ran while one was open for 0% of the time, Pallas kernels for 3%

profile of v1, /device:TPU:1, one launch (start us, length us, event | category | flops | bytes accessed | tf_op | source)
XLA Modules:
  0.0 200.3 jit_solution(17758295300898383363)
XLA Ops:
  0.6 0.9 copy-done
  1.5 0.8 copy-done.4
  2.4 0.7 copy-done.5
  3.1 0.1 shard_map.85
  3.2 21.7 %all_to_all.50.pack_ref = bf16[4,272,256]{2,1,0:T(8,128)(2,1)S(1)} all-to-all(bf16[4,272,256]{2,1,0:T(8,128)(2,1)S(1)} %shard_map.85), channel_id=1, replica_groups=mesh['z2'=2,'z1'=2,'core'=2,'y4'=2,'y2'=2,'y1'=2,'x2'=2,'x1'=2,'zhi'=2] ..., dimensions={0} | all-to-all | bytes 1114112 | tf_op jit(solution)/shard_map/all_to_all | solution.py:231
  24.9 3.9 %collective-permute-start = (bf16[4,272,256]{2,1,0:T(8,128)(2,1)S(1)}, bf16[4,272,256]{2,1,0:T(8,128)(2,1)S(1)}, u32[]{:S(2)}, u32[]{:S(2)}) collective-permute-start(bf16[4,272,256]{2,1,0:T(8,128)(2,1)S(1)} %all_to_all.50.pack_ref), channel_id=1, source_target_pairs={{0,64},{64,0},{1,65},{65,1},{2,66},{66,2},{3,67},{67,3},{4,68},{68... | collective-permute-start | bytes 1671176 | tf_op jit(solution)/shard_map/ppermute | solution.py:227
  28.8 0.9 copy-done.6
  29.8 5.5 %shard_map.86 = (bf16[4,256,1024]{2,1,0:T(8,128)(2,1)S(1)}, f32[128,1024]{1,0:T(8,128)S(1)}, bf16[144,1024]{1,0:T(8,128)(2,1)S(1)}) custom-call(bf16[1024,128]{1,0:T(8,128)(2,1)S(1)} %copy-done.6, bf16[4,272,256]{2,1,0:T(8,128)(2,1)S(1)} %all_to_all.50.pack_ref), custom_call_target="tpu_custom_call" | custom-call | flops 5368709120 | tf_op jit(solution)/shard_map/pallas_call | solution.py:38
  35.4 5.6 %shard_map.87 = (bf16[4,256,1024]{2,1,0:T(8,128)(2,1)S(1)}, f32[1024,128]{1,0:T(8,128)S(1)}) custom-call(bf16[144,1024]{1,0:T(8,128)(2,1)S(1)} %get-tuple-element.11.rows_t, f32[128,1024]{1,0:T(8,128)S(1)} %get-tuple-element.12.acc_in, bf16[4,272,256]{2,1,0:T(8,128)(2,1)S(1)} %collective-permute-done.pack_ref), custom_call_target="tpu_custom_call" | custom-call | flops 5368709120 | tf_op jit(solution)/shard_map/pallas_call | solution.py:38
  41.0 14.8 %all_to_all.51.in_ref = f32[8,128,128]{2,1,0:T(8,128)S(1)} all-to-all(f32[8,128,128]{2,1,0:T(8,128)S(1)} %bitcast.9), channel_id=1, replica_groups=mesh['z2'=2,'z1'=2,'core'=2,'y4'=2,'y2'=2,'y1'=2,'x2'=2,'x1'=2,'zhi'=2] ..., dimensions={0} | all-to-all | bytes 1048576 | tf_op jit(solution)/shard_map/all_to_all | solution.py:231
  55.8 23.0 %all_to_all.52.in_ref = f32[8,16,128]{2,1,0:T(8,128)S(1)} all-to-all(f32[8,16,128]{2,1,0:T(8,128)S(1)} %bitcast.10), channel_id=1, replica_groups=mesh['z2'=2,'z1'=2,'core'=2,'y4'=2,'y2'=2,'y1'=2,'x2'=2,'x1'=2,'zhi'=2] ..., dimensions={0} | all-to-all | bytes 131072 | tf_op jit(solution)/shard_map/all_to_all | solution.py:231
  78.8 13.8 %all_to_all.53 = bf16[8,16,128]{2,1,0:T(8,128)(2,1)S(1)} all-to-all(bf16[8,16,128]{2,1,0:T(8,128)(2,1)S(1)} %shard_map.89), channel_id=1, replica_groups=mesh['z2'=2,'z1'=2,'core'=2,'y4'=2,'y2'=2,'y1'=2,'x2'=2,'x1'=2,'zhi'=2] ..., dimensions={0} | all-to-all | bytes 65536 | tf_op jit(solution)/shard_map/all_to_all | solution.py:231
  92.6 8.5 %all_to_all.54 = bf16[8,128,128]{2,1,0:T(8,128)(2,1)S(1)} all-to-all(bf16[8,128,128]{2,1,0:T(8,128)(2,1)S(1)} %broadcast_in_dim.8), channel_id=1, replica_groups=mesh['z2'=2,'z1'=2,'core'=2,'y4'=2,'y2'=2,'y1'=2,'x2'=2,'x1'=2,'zhi'=2] ..., dimensions={0} | all-to-all | bytes 524288 | tf_op jit(solution)/shard_map/all_to_all | solution.py:231
  101.1 0.7 shard_map.91
  101.8 6.8 %collective-permute-start.1 = (f32[4,256,128]{2,1,0:T(8,128)S(1)}, f32[4,256,128]{2,1,0:T(8,128)S(1)}, u32[]{:S(2)}, u32[]{:S(2)}) collective-permute-start(f32[4,256,128]{2,1,0:T(8,128)S(1)} %shard_map.91), channel_id=1, source_target_pairs={{0,64},{64,0},{1,65},{65,1},{2,66},{66,2},{3,67},{67,3},{4,68},{68... | collective-permute-start | bytes 1572872 | tf_op jit(solution)/shard_map/ppermute | solution.py:227
  108.6 0.7 shard_map.90
  109.3 0.8 collective-permute-done.1
  110.2 16.6 %all_to_all.55.parts_ref = f32[4,256,128]{2,1,0:T(8,128)S(1)} all-to-all(f32[4,256,128]{2,1,0:T(8,128)S(1)} %add.3), channel_id=1, replica_groups=mesh['z2'=2,'z1'=2,'core'=2,'y4'=2,'y2'=2,'y1'=2,'x2'=2,'x1'=2,'zhi'=2] ..., dimensions={0} | all-to-all | bytes 1048576 | tf_op jit(solution)/shard_map/all_to_all | solution.py:231
  126.8 0.6 shard_map.92
  127.5 9.3 %all_to_all.56.in_ref = f32[8,48,128]{2,1,0:T(8,128)S(1)} all-to-all(f32[8,48,128]{2,1,0:T(8,128)S(1)} %bitcast.11), channel_id=1, replica_groups=mesh['z2'=2,'z1'=2,'core'=2,'y4'=2,'y2'=2,'y1'=2,'x2'=2,'x1'=2,'zhi'=2] ..., dimensions={0} | all-to-all | bytes 393216 | tf_op jit(solution)/shard_map/all_to_all | solution.py:231
  136.8 17.2 %all_to_all.57.in_ref = f32[8,48,128]{2,1,0:T(8,128)S(1)} all-to-all(f32[8,48,128]{2,1,0:T(8,128)S(1)} %shard_map.93), channel_id=1, replica_groups=mesh['z2'=2,'z1'=2,'core'=2,'y4'=2,'y2'=2,'y1'=2,'x2'=2,'x1'=2,'zhi'=2] ..., dimensions={0} | all-to-all | bytes 393216 | tf_op jit(solution)/shard_map/all_to_all | solution.py:231
  154.1 15.2 %all_to_all.58.in_ref = f32[8,48,128]{2,1,0:T(8,128)S(1)} all-to-all(f32[8,48,128]{2,1,0:T(8,128)S(1)} %shard_map.94), channel_id=1, replica_groups=mesh['z2'=2,'z1'=2,'core'=2,'y4'=2,'y2'=2,'y1'=2,'x2'=2,'x1'=2,'zhi'=2] ..., dimensions={0} | all-to-all | bytes 393216 | tf_op jit(solution)/shard_map/all_to_all | solution.py:231
  169.3 9.5 %all_to_all.59 = f32[8,48,128]{2,1,0:T(8,128)S(1)} all-to-all(f32[8,48,128]{2,1,0:T(8,128)S(1)} %shard_map.95), channel_id=1, replica_groups=mesh['z2'=2,'z1'=2,'core'=2,'y4'=2,'y2'=2,'y1'=2,'x2'=2,'x1'=2,'zhi'=2] ..., dimensions={0} | all-to-all | bytes 393216 | tf_op jit(solution)/shard_map/all_to_all | solution.py:231
  178.7 21.5 %shard_map.96 = (f32[256,128]{1,0:T(8,128)}, f32[256,128]{1,0:T(8,128)}, f32[256,128]{1,0:T(8,128)}) custom-call(f32[384,128]{1,0:T(8,128)S(1)} %bitcast.8, f32[256,128]{1,0:T(8,128)S(1)} %get-tuple-element.16.applied_ref, f32[256,128]{1,0:T(8,128)S(1)} %copy-done.1, f32[256,128]{1,0:T(8,128)S(1)} %copy-done.2, f32[256,128]{1,0:T(8,128)S(1)} %copy-done.3), custom_call_target="tpu_custom_call" | custom-call | tf_op jit(solution)/shard_map/pallas_call | solution.py:38
  (18 shorter events, 0.2 us)
Async XLA Ops:
  0.6 0.9 copy-start
  1.5 0.8 copy-start.4
  2.4 0.7 copy-start.5
  24.9 10.4 %collective-permute-start = (bf16[4,272,256]{2,1,0:T(8,128)(2,1)S(1)}, bf16[4,272,256]{2,1,0:T(8,128)(2,1)S(1)}, u32[]{:S(2)}, u32[]{:S(2)}) collective-permute-start(bf16[4,272,256]{2,1,0:T(8,128)(2,1)S(1)} %all_to_all.50.pack_ref), channel_id=1, source_target_pairs={{0,64},{64,0},{1,65},{65,1},{2,66},{66,2},{3,67},{67,3},{4,68},{68... | collective-permute-start | bytes 1671176 | tf_op jit(solution)/shard_map/ppermute | solution.py:227
  28.8 1.0 copy-start.6
  101.8 8.3 %collective-permute-start.1 = (f32[4,256,128]{2,1,0:T(8,128)S(1)}, f32[4,256,128]{2,1,0:T(8,128)S(1)}, u32[]{:S(2)}, u32[]{:S(2)}) collective-permute-start(f32[4,256,128]{2,1,0:T(8,128)S(1)} %shard_map.91), channel_id=1, source_target_pairs={{0,64},{64,0},{1,65},{65,1},{2,66},{66,2},{3,67},{67,3},{4,68},{68... | collective-permute-start | bytes 1572872 | tf_op jit(solution)/shard_map/ppermute | solution.py:227
  108.6 18.2 %copy-start.1 = (f32[256,128]{1,0:T(8,128)S(1)}, f32[256,128]{1,0:T(8,128)}, u32[]{:S(2)}) copy-start(f32[256,128]{1,0:T(8,128)} %dir_ref.5) | copy-start | bytes 393220
  108.6 18.2 %copy-start.2 = (f32[256,128]{1,0:T(8,128)S(1)}, f32[256,128]{1,0:T(8,128)}, u32[]{:S(2)}) copy-start(f32[256,128]{1,0:T(8,128)} %res_ref.3) | copy-start | bytes 393220
  110.2 68.5 %copy-start.3 = (f32[256,128]{1,0:T(8,128)S(1)}, f32[256,128]{1,0:T(8,128)}, u32[]{:S(2)}) copy-start(f32[256,128]{1,0:T(8,128)} %sol_ref.1) | copy-start | bytes 393220

commit v2 on v1

v2 whole, which is shorter than its diff:
```python
import math

import jax
import jax.numpy as jnp
from jax import lax
from jax.experimental import pallas as pl
from jax.experimental.pallas import tpu as pltpu
from jax.sharding import Mesh, PartitionSpec as P

FEATURES = 131072
penalty = 0.1
highest = lax.Precision.HIGHEST
f32 = jnp.float32
bf16 = jnp.bfloat16

SINE = (6.283164044300415, -41.33714237083587, 81.34076887919463, -70.99343319457358)
SCALE = math.sqrt(2.0 / FEATURES)
ROUNDER = 12582912.0
PACK = 272
GRAM = 384

AXES = ("z2", "z1", "core", "y4", "y2", "y1", "x2", "x1", "zhi")
DP = ("z2", "z1", "core")
RING_X = ("x2", "x1")
RING_Y = ("y4", "y2", "y1")
RING_Z = ("zhi", "z2", "z1")
CHIP_X = ("x2", "x1", "core")


def vmem():
    return pl.BlockSpec(memory_space=pltpu.VMEM)


def call(kernel, outs, *args, scratch=(), flops=0, nbytes=0):
    return pl.pallas_call(
        kernel,
        out_shape=outs,
        in_specs=[vmem()] * len(args),
        out_specs=jax.tree.map(lambda _: vmem(), outs),
        scratch_shapes=list(scratch),
        compiler_params=pltpu.CompilerParams(vmem_limit_bytes=16 * 1024 * 1024),
        cost_estimate=pl.CostEstimate(flops=flops, bytes_accessed=nbytes, transcendentals=0),
    )(*args)


def struct(shape, dtype=f32):
    return jax.ShapeDtypeStruct(shape, dtype)


def pack_kernel(proj_in, shift_in, dir_in, out_ref, proj_ref, shift_ref, dir_ref, sems):
    copies = [
        pltpu.make_async_copy(src, dst, sems.at[i])
        for i, (src, dst) in enumerate(
            ((dir_in, dir_ref), (proj_in, proj_ref), (shift_in, shift_ref))
        )
    ]
    for c in copies:
        c.start()
    for c in copies:
        c.wait()
    proj_t = proj_ref[...].astype(f32).T.astype(bf16)
    out_ref[0:128, 0:128] = proj_t[0:128]
    out_ref[0:128, 128:256] = proj_t[128:256]
    out_ref[128:144, :] = jnp.broadcast_to(shift_ref[...].astype(f32), (16, 256)).astype(bf16)
    out_ref[144:272, :] = dir_ref[...].T.astype(bf16)


def scaled_cos(phase):
    turns = phase * (1.0 / (2.0 * math.pi))
    turns = turns - ((turns + ROUNDER) - ROUNDER)
    w = 0.25 - jnp.abs(turns)
    z = w * w
    acc = SINE[3] * SCALE
    for c in (SINE[2], SINE[1], SINE[0]):
        acc = acc * z + c * SCALE
    return acc * w


def feature_step(rows_t, piece, feats_ref, acc):
    proj_t = jnp.concatenate([piece[0:128, 0:128], piece[0:128, 128:256]], axis=0)
    shift = piece[128:144, :].astype(f32).T[:, 0:1]
    dir_t = piece[144:272, :]
    for r in range(4):
        cols = slice(r * 256, (r + 1) * 256)
        phase = jnp.dot(proj_t, rows_t[:, cols], preferred_element_type=f32)
        for i in range(0, 256, 32):
            strip = phase[i : i + 32] + shift[i : i + 32]
            feats_ref[i : i + 32, cols] = scaled_cos(strip).astype(bf16)
        acc[:, cols] += jnp.dot(dir_t, feats_ref[:, cols], preferred_element_type=f32)


def own_features(samples_ref, pack_ref, feats_ref, acc, rows_t):
    rows_t[...] = samples_ref[...].T
    acc[...] = jnp.zeros_like(acc)
    feature_step(rows_t, pack_ref, feats_ref.at[0], acc)


def more_features(rows_t, acc_in, *refs):
    packs, feats_ref, acc = refs[:-2], refs[-2], refs[-1]
    acc[...] = acc_in[...]
    for s, p in enumerate(packs):
        feature_step(rows_t, p, feats_ref.at[s], acc)


def stack_kernel(a_ref, b_ref, c_ref, after_ref, out_ref):
    for s, r in enumerate((a_ref, b_ref, c_ref)):
        out_ref[s] = r[...]


def last_features(rows_t, acc_in, pack_ref, feats_ref, sums_ref, acc):
    acc[...] = acc_in[...]

    @pl.loop(0, 3)
    def _(s):
        feature_step(rows_t, pack_ref.at[s], feats_ref.at[s], acc)

    sums_ref[...] = acc[...].T


def total_of(in_ref):
    total = in_ref[0]
    for i in range(1, in_ref.shape[0]):
        total = total + in_ref[i]
    return total


def sum_kernel(in_ref, out_ref):
    out_ref[...] = total_of(in_ref)


def sum_copies_kernel(in_ref, out_ref):
    total = total_of(in_ref)
    for i in range(8):
        out_ref[i] = total


def low_copies_kernel(a_ref, b_ref, out_ref):
    low = (a_ref[...] + b_ref[...]).astype(bf16)
    for i in range(8):
        out_ref[i] = low


def add_kernel(a_ref, b_ref, *outs):
    for i in range(4):
        outs[i][...] = a_ref[i] + b_ref[i]


def back_kernel(near_ref, far_ref, low_ref, out_ref):
    out_ref[0] = jnp.dot(near_ref[0], low_ref[...], preferred_element_type=f32)
    for s in range(3):
        out_ref[s + 1] = jnp.dot(far_ref[s], low_ref[...], preferred_element_type=f32)


def fdot(a, b):
    return jnp.dot(a, b, precision=highest, preferred_element_type=f32)


def sym(m):
    return 0.5 * (m + m.T)


def places():
    n = 128
    return lax.broadcasted_iota(jnp.int32, (n, n), 0), lax.broadcasted_iota(jnp.int32, (n, n), 1)


def gram_kernel(p0, p1, p2, p3, dir_ref, res_ref, applied_ref, gram_ref):
    total = (p0[...] + p1[...]) + (p2[...] + p3[...])
    applied = total + penalty * dir_ref[...]
    applied_ref[...] = applied
    applied_t = applied.T
    dir_gram = sym(fdot(applied_t, dir_ref[...]))
    applied_gram = fdot(applied_t, applied)
    res_gram = sym(fdot(res_ref[...].T, res_ref[...]))
    at_row, at_col = places()
    diag = jnp.sum(jnp.where(at_row == at_col, applied_gram, 0.0), axis=1, keepdims=True)
    gram_ref[0:128, :] = jnp.where(at_col >= at_row, dir_gram, applied_gram)
    gram_ref[128:256, :] = fdot(applied_t, res_ref[...])
    gram_ref[256:384, :] = jnp.where(
        at_col >= at_row, res_gram, jnp.where(at_col == 0, diag, diag[0:1, 0:1])
    )


def inverse_factors(mats):
    n, w = 128, 8
    lane = lax.broadcasted_iota(jnp.int32, (w, n), 1)
    sub = lax.broadcasted_iota(jnp.int32, (w, n), 0)

    def row(tile, i):
        return jnp.broadcast_to(tile[i : i + 1, :], (w, n))

    def col(tile, i):
        return jnp.broadcast_to(tile[:, i : i + 1], (w, n))

    tiles = [[m[w * i : w * i + w, :] for i in range(n // w)] for m in mats]
    outs = [([], []) for _ in mats]
    for h in range(n // w):
        k = w * h
        inside = (lane >= k) & (lane < k + w)
        for t, (ms, ns) in zip(tiles, outs):
            home = t[h]
            rows = [row(home, i) for i in range(w)]
            p = {(i, j): col(rows[i], k + j) for i in range(w) for j in range(i + 1)}
            r = [jnp.where(inside, jnp.where(lane == k + i, 1.0, 0.0), rows[i]) for i in range(w)]
            inv, low = [], {}
            for j in range(w):
                inv.append(1.0 / p[j, j])
                for i in range(j + 1, w):
                    low[i, j] = p[i, j] * inv[j]
                for i in range(j + 1, w):
                    for m in range(j + 1, i + 1):
                        p[i, m] = p[i, m] - low[i, j] * p[m, j]
                    r[i] = r[i] - low[i, j] * r[j]
            x = [None] * w
            for j in reversed(range(w)):
                x[j] = r[j] * inv[j]
                for i in range(j + 1, w):
                    x[j] = x[j] - low[i, j] * x[i]
            for i in range(h + 1, n // w):
                old = t[i]
                new = jnp.where(inside, 0.0, old)
                for j in range(w):
                    new = new - col(old, k + j) * x[j]
                t[i] = new
            whole = x[0]
            for j in range(1, w):
                whole = jnp.where(sub == j, x[j], whole)
            ms.append(jnp.where(lane < k, home, jnp.where(lane == sub + k, 1.0, 0.0)))
            ns.append(jnp.where(lane < k + w, whole, 0.0))
    return [(jnp.concatenate(ms, axis=0), jnp.concatenate(ns, axis=0)) for ms, ns in outs]


def final_kernel(gram_ref, applied_ref, dir_ref, res_ref, sol_ref, sol_out, res_out, dir_out):
    at_row, at_col = places()
    first, cross, third = (gram_ref[128 * i : 128 * i + 128, :] for i in range(3))
    first_t, third_t = first.T, third.T
    dir_gram = jnp.where(at_col >= at_row, first, first_t)
    res_gram = jnp.where(at_col >= at_row, third, third_t)
    diag = jnp.where(at_row == 0, third[127:128, 1:2], third[:, 0:1])
    applied_gram = jnp.where(at_col < at_row, first, jnp.where(at_col == at_row, diag, first_t))
    (m_d, n_d), (m_r, n_r) = inverse_factors([dir_gram, res_gram])
    step = fdot(m_d.T, fdot(n_d, res_gram))
    step_t = step.T
    sol_out[...] = sol_ref[...] + fdot(dir_ref[...], step)
    res_next = res_ref[...] - fdot(applied_ref[...], step)
    res_out[...] = res_next
    both = fdot(step_t, cross)
    gram_next = sym(res_gram - both - both.T + fdot(step_t, fdot(applied_gram, step)))
    mix = fdot(m_r.T, fdot(n_r, gram_next))
    dir_out[...] = res_next + fdot(dir_ref[...], mix)


def swap(value, axes, s):
    n = 2 ** len(axes)
    return lax.ppermute(value, axes, [(i, i ^ s) for i in range(n)])


def exchange(value, axes):
    return lax.all_to_all(value, axes, 0, 0)


def local(samples, projection, phase_shift, solution, residual, direction):
    z_lo = ("z2", "z1")
    core = ("core",)
    pack = pl.pallas_call(
        pack_kernel,
        out_shape=struct((PACK, 256), bf16),
        in_specs=[pl.BlockSpec(memory_space=pltpu.HBM)] * 3,
        out_specs=vmem(),
        scratch_shapes=[
            pltpu.VMEM((128, 256), bf16),
            pltpu.VMEM((1, 256), bf16),
            pltpu.VMEM((256, 128), f32),
            pltpu.SemaphoreType.DMA((3,)),
        ],
        compiler_params=pltpu.CompilerParams(vmem_limit_bytes=63000000),
    )(projection, phase_shift, direction)
    along = [swap(pack, z_lo, s) for s in (1, 2, 3)]
    across = swap(pack, core, 1)
    work = 2 * 2 * 1024 * 256 * 128 * 10

    def feats_of(n):
        return struct((n, 256, 1024), bf16)

    acc_of = struct((128, 1024))
    own, acc, rows_t = call(
        own_features, [feats_of(1), acc_of, struct((128, 1024), bf16)], samples, pack, flops=work
    )
    other, acc = call(more_features, [feats_of(1), acc_of], rows_t, acc, across, flops=work)
    stacked = pl.pallas_call(
        stack_kernel,
        out_shape=struct((3, PACK, 256), bf16),
        in_specs=[vmem()] * 3 + [pl.BlockSpec(memory_space=pl.ANY)],
        out_specs=vmem(),
        compiler_params=pltpu.CompilerParams(vmem_limit_bytes=16 * 1024 * 1024),
    )(*along, acc)
    across_far = swap(stacked, core, 1)
    own_far, acc = call(more_features, [feats_of(3), acc_of], rows_t, acc, *along, flops=3 * work)
    other_far, sums = call(
        last_features,
        [feats_of(3), struct((1024, 128))],
        rows_t,
        acc,
        across_far,
        scratch=[pltpu.VMEM((128, 1024), f32)],
        flops=3 * work,
    )
    by_x = call(sum_kernel, struct((256, 128)), exchange(sums.reshape(4, 256, 128), RING_X))
    by_y = call(sum_kernel, struct((32, 128)), exchange(by_x.reshape(8, 32, 128), RING_Y))
    low = call(low_copies_kernel, struct((8, 32, 128), bf16), by_y, swap(by_y, ("zhi",), 1))
    low = exchange(low, RING_Y).reshape(256, 128)
    low = exchange(jnp.broadcast_to(low[None], (4, 256, 128)), RING_X).reshape(1024, 128)
    theirs = call(back_kernel, struct((4, 256, 128)), other, other_far, low, flops=work // 5)
    theirs = swap(theirs, core, 1)
    mine = call(back_kernel, struct((4, 256, 128)), own, own_far, low, flops=work // 5)
    parts = call(add_kernel, [struct((256, 128))] * 4, mine, theirs)
    parts = [parts[0]] + [swap(parts[s], z_lo, s) for s in (1, 2, 3)]
    applied, gram = call(
        gram_kernel, [struct((256, 128)), struct((GRAM, 128))], *parts, direction, residual
    )
    chunk = GRAM // 8
    piece = exchange(gram.reshape(8, chunk, 128), CHIP_X)
    for axes in (RING_Y, RING_Z, CHIP_X):
        piece = call(sum_copies_kernel, struct((8, chunk, 128)), piece)
        piece = exchange(piece, axes)
    return call(
        final_kernel,
        [struct((256, 128))] * 3,
        piece.reshape(GRAM, 128),
        applied,
        direction,
        residual,
        solution,
    )


def solution(mesh):
    fine = Mesh(mesh.devices.reshape((2,) * 9), AXES)
    rows, cols, state = P(DP, None), P(None, AXES), P(AXES, None)
    return jax.shard_map(
        local,
        mesh=fine,
        in_specs=(rows, cols, cols, state, state, state),
        out_specs=(state, state, state),
        check_vma=False,
    )
```

time: 201 us -> 179 us (0.89)
  blocking collectives: 150 us -> 95.3 us
  starting transfers between devices: 10.7 us -> 45.8 us
  Pallas kernels: 34.9 us -> 25.9 us
  waiting for transfers between devices: 0.79 us -> 8.36 us
    all_to_all x10 -> x8, blocking collectives: 150 us -> 95.3 us  [exchange(): return lax.all_to_all(value, axes, 0, 0)]
    ppermute x2 -> x10, starting transfers between devices: 10.7 us -> 45.8 us  [swap(): return lax.ppermute(value, axes, [(i, i ^ s) for i in range(n)])]
    pallas_call x12 -> x15, Pallas kernels: 34.9 us -> 24.2 us  [call(): pl.pallas_call(kernel, out_shape=outs, in_specs=[vmem()] * len(args), out...]
    ppermute x2 -> x10, waiting for transfers between devices: 0.79 us -> 8.36 us  [swap(): return lax.ppermute(value, axes, [(i, i ^ s) for i in range(n)])]
  transfers between devices with their start and end apart: 2 -> 10, of which waited for: 1 -> 6; matrix products, arithmetic and copies ran while one was open for 0% -> 0% of each run, Pallas kernels for 3% -> 4%
where the time goes in v2:
time: 179 us; the launch traced here: 178 us
  blocking collectives  95.3 us (53%)
  starting transfers between devices  45.8 us (26%)
  Pallas kernels  25.9 us (14%)
  waiting for transfers between devices  8.36 us (5%)
  local copies, waits for them, and re-layouts  1.91 us (1%)
    all_to_all x8, blocking collectives, exchange(): return lax.all_to_all(value, axes, 0, 0)  95.3 us
    ppermute x10, starting transfers between devices, swap(): return lax.ppermute(value, axes, [(i, i ^ s) for i in range(n)])  45.8 us
    pallas_call x15, Pallas kernels, call(): pl.pallas_call(kernel, out_shape=outs, in_specs=[vmem()] * len(args), out...  24.2 us
    ppermute x10, waiting for transfers between devices, swap(): return lax.ppermute(value, axes, [(i, i ^ s) for i in range(n)])  8.36 us
  transfers between devices with their start and end apart: 10, of which 6 were waited for; matrix products, arithmetic and copies ran while one was open for 0% of the time, Pallas kernels for 4%

profile of v2, /device:TPU:1, one launch (start us, length us, event | category | flops | bytes accessed | tf_op | source)
XLA Modules:
  0.0 178.1 jit_solution(6873892074259098545)
XLA Ops:
  0.6 1.7 shard_map.85.pack_ref
  2.3 8.8 %collective-permute-start = (bf16[272,256]{1,0:T(8,128)(2,1)}, bf16[272,256]{1,0:T(8,128)(2,1)S(1)}, u32[]{:S(2)}, u32[]{:S(2)}) collective-permute-start(bf16[272,256]{1,0:T(8,128)(2,1)} %shard_map.85.pack_ref), channel_id=1, source_target_pairs={{0,64},{64,0},{1,65},{65,1},{2,66},{66,2},{3,67},{67,3},{4,68},{68... | collective-permute-start | bytes 417800 | tf_op jit(solution)/shard_map/ppermute | solution.py:255
  11.1 2.2 %collective-permute-start.3 = (bf16[272,256]{1,0:T(8,128)(2,1)}, bf16[272,256]{1,0:T(8,128)(2,1)S(1)}, u32[]{:S(2)}, u32[]{:S(2)}) collective-permute-start(bf16[272,256]{1,0:T(8,128)(2,1)} %shard_map.85.pack_ref), channel_id=1, source_target_pairs={{0,384},{128,256},{256,128},{384,0},{1,385},{129,257},{257,129},{3... | collective-permute-start | bytes 417800 | tf_op jit(solution)/shard_map/ppermute | solution.py:255
  13.4 1.9 %collective-permute-start.2 = (bf16[272,256]{1,0:T(8,128)(2,1)}, bf16[272,256]{1,0:T(8,128)(2,1)S(1)}, u32[]{:S(2)}, u32[]{:S(2)}) collective-permute-start(bf16[272,256]{1,0:T(8,128)(2,1)} %shard_map.85.pack_ref), channel_id=1, source_target_pairs={{0,256},{128,384},{256,0},{384,128},{1,257},{129,385},{257,1},{385... | collective-permute-start | bytes 417800 | tf_op jit(solution)/shard_map/ppermute | solution.py:255
  15.3 5.1 %collective-permute-start.1 = (bf16[272,256]{1,0:T(8,128)(2,1)}, bf16[272,256]{1,0:T(8,128)(2,1)S(1)}, u32[]{:S(2)}, u32[]{:S(2)}) collective-permute-start(bf16[272,256]{1,0:T(8,128)(2,1)} %shard_map.85.pack_ref), channel_id=1, source_target_pairs={{0,128},{128,0},{256,384},{384,256},{1,129},{129,1},{257,385},{385... | collective-permute-start | bytes 417800 | tf_op jit(solution)/shard_map/ppermute | solution.py:255
  25.1 1.6 collective-permute-done.2.refs_1_.b_ref
  27.0 3.0 %collective-permute-start.4 = (bf16[3,272,256]{2,1,0:T(8,128)(2,1)S(1)}, bf16[3,272,256]{2,1,0:T(8,128)(2,1)S(1)}, u32[]{:S(2)}, u32[]{:S(2)}) collective-permute-start(bf16[3,272,256]{2,1,0:T(8,128)(2,1)S(1)} %shard_map.89), channel_id=1, source_target_pairs={{0,64},{64,0},{1,65},{65,1},{2,66},{66,2},{3,67},{67,3},{4,68},{68... | collective-permute-start | bytes 1253384 | tf_op jit(solution)/shard_map/ppermute | solution.py:255
  30.1 3.7 %shard_map.88 = (bf16[3,256,1024]{2,1,0:T(8,128)(2,1)S(1)}, f32[128,1024]{1,0:T(8,128)S(1)}) custom-call(bf16[128,1024]{1,0:T(8,128)(2,1)S(1)} %get-tuple-element.19.rows_t, f32[128,1024]{1,0:T(8,128)S(1)} %get-tuple-element.21.acc_in.after_ref, bf16[272,256]{1,0:T(8,128)(2,1)S(1)} %collective-permute-done.1.refs_0_.a_ref, ...), custom_call_target="tpu_custom_call" | custom-call | flops 4026531840 | tf_op jit(solution)/shard_map/pallas_call | solution.py:35
  33.8 4.3 %shard_map.90 = (bf16[3,256,1024]{2,1,0:T(8,128)(2,1)S(1)}, f32[1024,128]{1,0:T(8,128)S(1)}) custom-call(bf16[128,1024]{1,0:T(8,128)(2,1)S(1)} %get-tuple-element.19.rows_t, f32[128,1024]{1,0:T(8,128)S(1)} %get-tuple-element.23.acc_in, bf16[3,272,256]{2,1,0:T(8,128)(2,1)S(1)} %collective-permute-done.4.pack_ref), custom_call_target="tpu_custom_call" | custom-call | flops 4026531840 | tf_op jit(solution)/shard_map/pallas_call | solution.py:35
  38.2 11.7 %all_to_all.40.in_ref = f32[4,256,128]{2,1,0:T(8,128)S(1)} all-to-all(f32[4,256,128]{2,1,0:T(8,128)S(1)} %bitcast.10), channel_id=1, replica_groups=mesh['z2'=2,'z1'=2,'core'=2,'y4'=2,'y2'=2,'y1'=2,'x2'=2,'x1'=2,'zhi'=2] ..., dimensions={0} | all-to-all | bytes 1048576 | tf_op jit(solution)/shard_map/all_to_all | solution.py:259
  49.9 14.4 %all_to_all.41.in_ref = f32[8,32,128]{2,1,0:T(8,128)S(1)} all-to-all(f32[8,32,128]{2,1,0:T(8,128)S(1)} %bitcast.9), channel_id=1, replica_groups=mesh['z2'=2,'z1'=2,'core'=2,'y4'=2,'y2'=2,'y1'=2,'x2'=2,'x1'=2,'zhi'=2] ..., dimensions={0} | all-to-all | bytes 262144 | tf_op jit(solution)/shard_map/all_to_all | solution.py:259
  64.3 8.0 %collective-permute-start.5 = (f32[32,128]{1,0:T(8,128)S(1)}, f32[32,128]{1,0:T(8,128)S(1)}, u32[]{:S(2)}, u32[]{:S(2)}) collective-permute-start(f32[32,128]{1,0:T(8,128)S(1)} %shard_map.92.a_ref), channel_id=1, source_target_pairs={{0,1},{1,0},{2,3},{3,2},{4,5},{5,4},{6,7},{7,6},{8,9},{9,8},{10,11... | collective-permute-start | bytes 49160 | tf_op jit(solution)/shard_map/ppermute | solution.py:255
  73.4 9.6 %all_to_all.42 = bf16[8,32,128]{2,1,0:T(8,128)(2,1)S(1)} all-to-all(bf16[8,32,128]{2,1,0:T(8,128)(2,1)S(1)} %shard_map.93), channel_id=1, replica_groups=mesh['z2'=2,'z1'=2,'core'=2,'y4'=2,'y2'=2,'y1'=2,'x2'=2,'x1'=2,'zhi'=2] ..., dimensions={0} | all-to-all | bytes 131072 | tf_op jit(solution)/shard_map/all_to_all | solution.py:259
  83.1 7.9 %all_to_all.43 = bf16[4,256,128]{2,1,0:T(8,128)(2,1)S(1)} all-to-all(bf16[4,256,128]{2,1,0:T(8,128)(2,1)S(1)} %broadcast_in_dim.8), channel_id=1, replica_groups=mesh['z2'=2,'z1'=2,'core'=2,'y4'=2,'y2'=2,'y1'=2,'x2'=2,'x1'=2,'zhi'=2] ..., dimensions={0} | all-to-all | bytes 524288 | tf_op jit(solution)/shard_map/all_to_all | solution.py:259
  91.7 7.5 %collective-permute-start.6 = (f32[4,256,128]{2,1,0:T(8,128)S(1)}, f32[4,256,128]{2,1,0:T(8,128)S(1)}, u32[]{:S(2)}, u32[]{:S(2)}) collective-permute-start(f32[4,256,128]{2,1,0:T(8,128)S(1)} %shard_map.95), channel_id=1, source_target_pairs={{0,64},{64,0},{1,65},{65,1},{2,66},{66,2},{3,67},{67,3},{4,68},{68... | collective-permute-start | bytes 1572872 | tf_op jit(solution)/shard_map/ppermute | solution.py:255
  100.8 1.9 %collective-permute-start.7 = (f32[256,128]{1,0:T(8,128)S(1)}, f32[256,128]{1,0:T(8,128)S(1)}, u32[]{:S(2)}, u32[]{:S(2)}) collective-permute-start(f32[256,128]{1,0:T(8,128)S(1)} %get-tuple-element.28), channel_id=1, source_target_pairs={{0,128},{128,0},{256,384},{384,256},{1,129},{129,1},{257,385},{385... | collective-permute-start | bytes 393224 | tf_op jit(solution)/shard_map/ppermute | solution.py:255
  102.7 4.3 %collective-permute-start.8 = (f32[256,128]{1,0:T(8,128)S(1)}, f32[256,128]{1,0:T(8,128)S(1)}, u32[]{:S(2)}, u32[]{:S(2)}) collective-permute-start(f32[256,128]{1,0:T(8,128)S(1)} %get-tuple-element.29), channel_id=1, source_target_pairs={{0,256},{128,384},{256,0},{384,128},{1,257},{129,385},{257,1},{385... | collective-permute-start | bytes 393224 | tf_op jit(solution)/shard_map/ppermute | solution.py:255
  107.0 3.1 %collective-permute-start.9 = (f32[256,128]{1,0:T(8,128)S(1)}, f32[256,128]{1,0:T(8,128)S(1)}, u32[]{:S(2)}, u32[]{:S(2)}) collective-permute-start(f32[256,128]{1,0:T(8,128)S(1)} %get-tuple-element.30), channel_id=1, source_target_pairs={{0,384},{128,256},{256,128},{384,0},{1,385},{129,257},{257,129},{3... | collective-permute-start | bytes 393224 | tf_op jit(solution)/shard_map/ppermute | solution.py:255
  110.1 2.9 %collective-permute-done.8.p2 = f32[256,128]{1,0:T(8,128)S(1)} collective-permute-done((f32[256,128]{1,0:T(8,128)S(1)}, f32[256,128]{1,0:T(8,128)S(1)}, u32[]{:S(2)}, u32[]{:S(2)}) %collective-permute-start.8) | collective-permute-done | bytes 131104 | tf_op jit(solution)/shard_map/ppermute | solution.py:255
  115.3 11.7 %all_to_all.44.in_ref = f32[8,48,128]{2,1,0:T(8,128)S(1)} all-to-all(f32[8,48,128]{2,1,0:T(8,128)S(1)} %bitcast.11), channel_id=1, replica_groups=mesh['z2'=2,'z1'=2,'core'=2,'y4'=2,'y2'=2,'y1'=2,'x2'=2,'x1'=2,'zhi'=2] ..., dimensions={0} | all-to-all | bytes 393216 | tf_op jit(solution)/shard_map/all_to_all | solution.py:259
  127.0 11.0 %all_to_all.45.in_ref = f32[8,48,128]{2,1,0:T(8,128)S(1)} all-to-all(f32[8,48,128]{2,1,0:T(8,128)S(1)} %shard_map.98), channel_id=1, replica_groups=mesh['z2'=2,'z1'=2,'core'=2,'y4'=2,'y2'=2,'y1'=2,'x2'=2,'x1'=2,'zhi'=2] ..., dimensions={0} | all-to-all | bytes 393216 | tf_op jit(solution)/shard_map/all_to_all | solution.py:259
  138.0 16.6 %all_to_all.46.in_ref = f32[8,48,128]{2,1,0:T(8,128)S(1)} all-to-all(f32[8,48,128]{2,1,0:T(8,128)S(1)} %shard_map.99), channel_id=1, replica_groups=mesh['z2'=2,'z1'=2,'core'=2,'y4'=2,'y2'=2,'y1'=2,'x2'=2,'x1'=2,'zhi'=2] ..., dimensions={0} | all-to-all | bytes 393216 | tf_op jit(solution)/shard_map/all_to_all | solution.py:259
  154.6 12.4 %all_to_all.47 = f32[8,48,128]{2,1,0:T(8,128)S(1)} all-to-all(f32[8,48,128]{2,1,0:T(8,128)S(1)} %shard_map.100), channel_id=1, replica_groups=mesh['z2'=2,'z1'=2,'core'=2,'y4'=2,'y2'=2,'y1'=2,'x2'=2,'x1'=2,'zhi'=2] ..., dimensions={0} | all-to-all | bytes 393216 | tf_op jit(solution)/shard_map/all_to_all | solution.py:259
  167.0 11.1 %shard_map.101 = (f32[256,128]{1,0:T(8,128)}, f32[256,128]{1,0:T(8,128)}, f32[256,128]{1,0:T(8,128)}) custom-call(f32[384,128]{1,0:T(8,128)S(1)} %bitcast.8, f32[256,128]{1,0:T(8,128)S(1)} %get-tuple-element.32.applied_ref, f32[256,128]{1,0:T(8,128)S(1)} %copy-done, f32[256,128]{1,0:T(8,128)S(1)} %copy-done.1, f32[256,128]{1,0:T(8,128)S(1)} %copy-done.3), custom_call_target="tpu_custom_call" | custom-call | tf_op jit(solution)/shard_map/pallas_call | solution.py:35
  (32 shorter events, 10.7 us)
Async XLA Ops:
  2.3 21.3 %collective-permute-start = (bf16[272,256]{1,0:T(8,128)(2,1)}, bf16[272,256]{1,0:T(8,128)(2,1)S(1)}, u32[]{:S(2)}, u32[]{:S(2)}) collective-permute-start(bf16[272,256]{1,0:T(8,128)(2,1)} %shard_map.85.pack_ref), channel_id=1, source_target_pairs={{0,64},{64,0},{1,65},{65,1},{2,66},{66,2},{3,67},{67,3},{4,68},{68... | collective-permute-start | bytes 417800 | tf_op jit(solution)/shard_map/ppermute | solution.py:255
  11.1 14.0 %collective-permute-start.3 = (bf16[272,256]{1,0:T(8,128)(2,1)}, bf16[272,256]{1,0:T(8,128)(2,1)S(1)}, u32[]{:S(2)}, u32[]{:S(2)}) collective-permute-start(bf16[272,256]{1,0:T(8,128)(2,1)} %shard_map.85.pack_ref), channel_id=1, source_target_pairs={{0,384},{128,256},{256,128},{384,0},{1,385},{129,257},{257,129},{3... | collective-permute-start | bytes 417800 | tf_op jit(solution)/shard_map/ppermute | solution.py:255
  13.4 13.3 %collective-permute-start.2 = (bf16[272,256]{1,0:T(8,128)(2,1)}, bf16[272,256]{1,0:T(8,128)(2,1)S(1)}, u32[]{:S(2)}, u32[]{:S(2)}) collective-permute-start(bf16[272,256]{1,0:T(8,128)(2,1)} %shard_map.85.pack_ref), channel_id=1, source_target_pairs={{0,256},{128,384},{256,0},{384,128},{1,257},{129,385},{257,1},{385... | collective-permute-start | bytes 417800 | tf_op jit(solution)/shard_map/ppermute | solution.py:255
  15.3 11.7 %collective-permute-start.1 = (bf16[272,256]{1,0:T(8,128)(2,1)}, bf16[272,256]{1,0:T(8,128)(2,1)S(1)}, u32[]{:S(2)}, u32[]{:S(2)}) collective-permute-start(bf16[272,256]{1,0:T(8,128)(2,1)} %shard_map.85.pack_ref), channel_id=1, source_target_pairs={{0,128},{128,0},{256,384},{384,256},{1,129},{129,1},{257,385},{385... | collective-permute-start | bytes 417800 | tf_op jit(solution)/shard_map/ppermute | solution.py:255
  20.4 0.9 copy-start.2
  21.3 0.9 copy-start.4
  27.0 6.8 %collective-permute-start.4 = (bf16[3,272,256]{2,1,0:T(8,128)(2,1)S(1)}, bf16[3,272,256]{2,1,0:T(8,128)(2,1)S(1)}, u32[]{:S(2)}, u32[]{:S(2)}) collective-permute-start(bf16[3,272,256]{2,1,0:T(8,128)(2,1)S(1)} %shard_map.89), channel_id=1, source_target_pairs={{0,64},{64,0},{1,65},{65,1},{2,66},{66,2},{3,67},{67,3},{4,68},{68... | collective-permute-start | bytes 1253384 | tf_op jit(solution)/shard_map/ppermute | solution.py:255
  64.3 9.1 %collective-permute-start.5 = (f32[32,128]{1,0:T(8,128)S(1)}, f32[32,128]{1,0:T(8,128)S(1)}, u32[]{:S(2)}, u32[]{:S(2)}) collective-permute-start(f32[32,128]{1,0:T(8,128)S(1)} %shard_map.92.a_ref), channel_id=1, source_target_pairs={{0,1},{1,0},{2,3},{3,2},{4,5},{5,4},{6,7},{7,6},{8,9},{9,8},{10,11... | collective-permute-start | bytes 49160 | tf_op jit(solution)/shard_map/ppermute | solution.py:255
  91.7 9.0 %collective-permute-start.6 = (f32[4,256,128]{2,1,0:T(8,128)S(1)}, f32[4,256,128]{2,1,0:T(8,128)S(1)}, u32[]{:S(2)}, u32[]{:S(2)}) collective-permute-start(f32[4,256,128]{2,1,0:T(8,128)S(1)} %shard_map.95), channel_id=1, source_target_pairs={{0,64},{64,0},{1,65},{65,1},{2,66},{66,2},{3,67},{67,3},{4,68},{68... | collective-permute-start | bytes 1572872 | tf_op jit(solution)/shard_map/ppermute | solution.py:255
  99.2 15.4 %copy-start = (f32[256,128]{1,0:T(8,128)S(1)}, f32[256,128]{1,0:T(8,128)}, u32[]{:S(2)}) copy-start(f32[256,128]{1,0:T(8,128)} %dir_ref.3) | copy-start | bytes 393220
  99.2 15.4 %copy-start.1 = (f32[256,128]{1,0:T(8,128)S(1)}, f32[256,128]{1,0:T(8,128)}, u32[]{:S(2)}) copy-start(f32[256,128]{1,0:T(8,128)} %res_ref.3) | copy-start | bytes 393220
  100.8 9.3 %collective-permute-start.7 = (f32[256,128]{1,0:T(8,128)S(1)}, f32[256,128]{1,0:T(8,128)S(1)}, u32[]{:S(2)}, u32[]{:S(2)}) collective-permute-start(f32[256,128]{1,0:T(8,128)S(1)} %get-tuple-element.28), channel_id=1, source_target_pairs={{0,128},{128,0},{256,384},{384,256},{1,129},{129,1},{257,385},{385... | collective-permute-start | bytes 393224 | tf_op jit(solution)/shard_map/ppermute | solution.py:255
  102.7 10.3 %collective-permute-start.8 = (f32[256,128]{1,0:T(8,128)S(1)}, f32[256,128]{1,0:T(8,128)S(1)}, u32[]{:S(2)}, u32[]{:S(2)}) collective-permute-start(f32[256,128]{1,0:T(8,128)S(1)} %get-tuple-element.29), channel_id=1, source_target_pairs={{0,256},{128,384},{256,0},{384,128},{1,257},{129,385},{257,1},{385... | collective-permute-start | bytes 393224 | tf_op jit(solution)/shard_map/ppermute | solution.py:255
  107.0 7.6 %collective-permute-start.9 = (f32[256,128]{1,0:T(8,128)S(1)}, f32[256,128]{1,0:T(8,128)S(1)}, u32[]{:S(2)}, u32[]{:S(2)}) collective-permute-start(f32[256,128]{1,0:T(8,128)S(1)} %get-tuple-element.30), channel_id=1, source_target_pairs={{0,384},{128,256},{256,128},{384,0},{1,385},{129,257},{257,129},{3... | collective-permute-start | bytes 393224 | tf_op jit(solution)/shard_map/ppermute | solution.py:255
  115.3 51.7 %copy-start.3 = (f32[256,128]{1,0:T(8,128)S(1)}, f32[256,128]{1,0:T(8,128)}, u32[]{:S(2)}) copy-start(f32[256,128]{1,0:T(8,128)} %sol_ref.1) | copy-start | bytes 393220

commit v3 on v2

--- a/solution.py
+++ b/solution.py
@@ -1,3 +1,4 @@
+import functools
 import math
 
 import jax
@@ -31,15 +32,19 @@
     return pl.BlockSpec(memory_space=pltpu.VMEM)
 
 
-def call(kernel, outs, *args, scratch=(), flops=0, nbytes=0):
+def call(kernel, outs, *args, scratch=(), flops=0, ids=(), after=None):
+    args = (*ids, *args)
+    specs = [pl.BlockSpec(memory_space=pltpu.SMEM)] * len(ids) + [vmem()] * (len(args) - len(ids))
+    if after is not None:
+        args, specs = (*args, after), [*specs, pl.BlockSpec(memory_space=pl.ANY)]
     return pl.pallas_call(
         kernel,
         out_shape=outs,
-        in_specs=[vmem()] * len(args),
+        in_specs=specs,
         out_specs=jax.tree.map(lambda _: vmem(), outs),
         scratch_shapes=list(scratch),
         compiler_params=pltpu.CompilerParams(vmem_limit_bytes=16 * 1024 * 1024),
-        cost_estimate=pl.CostEstimate(flops=flops, bytes_accessed=nbytes, transcendentals=0),
+        cost_estimate=pl.CostEstimate(flops=flops, bytes_accessed=0, transcendentals=0),
     )(*args)
 
 
@@ -76,45 +81,60 @@
     return acc * w
 
 
-def feature_step(rows_t, piece, feats_ref, acc):
+def feature_step(rows_t, piece, feats_ref, acc, quarters, base):
     proj_t = jnp.concatenate([piece[0:128, 0:128], piece[0:128, 128:256]], axis=0)
     shift = piece[128:144, :].astype(f32).T[:, 0:1]
     dir_t = piece[144:272, :]
-    for r in range(4):
-        cols = slice(r * 256, (r + 1) * 256)
-        phase = jnp.dot(proj_t, rows_t[:, cols], preferred_element_type=f32)
+    for q in quarters:
+        rows = slice(q * 256, (q + 1) * 256)
+        cols = slice((q - base) * 256, (q - base + 1) * 256)
+        phase = jnp.dot(proj_t, rows_t[:, rows], preferred_element_type=f32)
         for i in range(0, 256, 32):
             strip = phase[i : i + 32] + shift[i : i + 32]
             feats_ref[i : i + 32, cols] = scaled_cos(strip).astype(bf16)
         acc[:, cols] += jnp.dot(dir_t, feats_ref[:, cols], preferred_element_type=f32)
 
 
-def own_features(samples_ref, pack_ref, feats_ref, acc, rows_t):
-    rows_t[...] = samples_ref[...].T
+def first_features(ids_ref, samples_ref, pack_ref, feats_ref, acc, rows_t):
+    for q in range(4):
+        start = pl.multiple_of((ids_ref[0] ^ q) * 256, 256)
+        rows_t[:, q * 256 : (q + 1) * 256] = samples_ref[pl.ds(start, 256), :].T
     acc[...] = jnp.zeros_like(acc)
-    feature_step(rows_t, pack_ref, feats_ref.at[0], acc)
-
-
-def more_features(rows_t, acc_in, *refs):
-    packs, feats_ref, acc = refs[:-2], refs[-2], refs[-1]
+    feature_step(rows_t, pack_ref, feats_ref, acc, range(4), 0)
+
+
+def their_near_features(rows_t, acc_in, p1, after_ref, feats_ref, acc):
     acc[...] = acc_in[...]
-    for s, p in enumerate(packs):
-        feature_step(rows_t, p, feats_ref.at[s], acc)
-
-
-def stack_kernel(a_ref, b_ref, c_ref, after_ref, out_ref):
-    for s, r in enumerate((a_ref, b_ref, c_ref)):
-        out_ref[s] = r[...]
-
-
-def last_features(rows_t, acc_in, pack_ref, feats_ref, sums_ref, acc):
+    feature_step(rows_t, p1, feats_ref, acc, range(4), 0)
+
+
+def their_far_features(rows_t, acc_in, p2, p3, feats_ref, sums_ref, acc):
     acc[...] = acc_in[...]
-
-    @pl.loop(0, 3)
-    def _(s):
-        feature_step(rows_t, pack_ref.at[s], feats_ref.at[s], acc)
-
+    for s, p in enumerate((p2, p3)):
+        feature_step(rows_t, p, feats_ref.at[s], acc, range(4), 0)
     sums_ref[...] = acc[...].T
+
+
+def own_quarter(q, rows_t, acc_in, p1, p2, p3, *refs):
+    feats_ref, sums_ref, acc = refs[-3:]
+    acc[...] = acc_in[:, q * 256 : (q + 1) * 256]
+    for s, p in enumerate((p1, p2, p3)):
+        feature_step(rows_t, p, feats_ref.at[s], acc, (q,), q)
+    total = acc[...].T
+    if len(refs) == 5:
+        total = total + refs[0][q * 256 : (q + 1) * 256, :]
+    sums_ref[...] = total
+
+
+def add_quarter(q, own_ref, other_ref, out_ref):
+    out_ref[...] = own_ref[...] + other_ref[q * 256 : (q + 1) * 256, :]
+
+
+def four_sum(a, b, c, d, out_ref):
+    total = (a[...] + b[...]) + (c[...] + d[...])
+    for y in range(8):
+        for z in range(2):
+            out_ref[2 * y + z] = total[32 * y : 32 * y + 32]
 
 
 def total_of(in_ref):
@@ -124,31 +144,36 @@
     return total
 
 
-def sum_kernel(in_ref, out_ref):
-    out_ref[...] = total_of(in_ref)
-
-
 def sum_copies_kernel(in_ref, out_ref):
     total = total_of(in_ref)
     for i in range(8):
         out_ref[i] = total
 
 
-def low_copies_kernel(a_ref, b_ref, out_ref):
-    low = (a_ref[...] + b_ref[...]).astype(bf16)
-    for i in range(8):
+def low_copies_kernel(in_ref, out_ref):
+    low = total_of(in_ref).astype(bf16)
+    for i in range(32):
         out_ref[i] = low
 
 
-def add_kernel(a_ref, b_ref, *outs):
-    for i in range(4):
-        outs[i][...] = a_ref[i] + b_ref[i]
-
-
-def back_kernel(near_ref, far_ref, low_ref, out_ref):
-    out_ref[0] = jnp.dot(near_ref[0], low_ref[...], preferred_element_type=f32)
-    for s in range(3):
-        out_ref[s + 1] = jnp.dot(far_ref[s], low_ref[...], preferred_element_type=f32)
+def own_back(ids_ref, first_ref, f0, f1, f2, f3, low_ref, *outs):
+    quarters = (f0, f1, f2, f3)
+    for s in range(4):
+        total = jnp.zeros((256, 128), f32)
+        for q in range(4):
+            feats = first_ref[:, q * 256 : (q + 1) * 256] if s == 0 else quarters[q][s - 1]
+            total += jnp.dot(feats, low_ref[ids_ref[0] ^ q], preferred_element_type=f32)
+        outs[s][...] = total
+
+
+def their_back(ids_ref, first_ref, near_ref, far_ref, low_ref, a0, a1, a2, a3, *outs):
+    for s, part in enumerate((a0, a1, a2, a3)):
+        total = part[...]
+        for q in range(4):
+            cols = slice(q * 256, (q + 1) * 256)
+            feats = (first_ref, near_ref, far_ref.at[0], far_ref.at[1])[s][:, cols]
+            total += jnp.dot(feats, low_ref[ids_ref[0] ^ q], preferred_element_type=f32)
+        outs[s][...] = total
 
 
 def fdot(a, b):
@@ -216,15 +241,21 @@
                 x[j] = r[j] * inv[j]
                 for i in range(j + 1, w):
                     x[j] = x[j] - low[i, j] * x[i]
-            for i in range(h + 1, n // w):
-                old = t[i]
+            whole = x[0]
+            for j in range(1, w):
+                whole = jnp.where(sub == j, x[j], whole)
+            if h + 1 < n // w:
+                right = jnp.where(lane >= k + w, home, 0.0)
+                change = lax.dot_general(
+                    right, whole, (((0,), (0,)), ((), ())), precision=highest, preferred_element_type=f32
+                )
+                for i in range(h + 2, n // w):
+                    t[i] = jnp.where(inside, 0.0, t[i]) - change[w * i : w * i + w]
+                old = t[h + 1]
                 new = jnp.where(inside, 0.0, old)
                 for j in range(w):
                     new = new - col(old, k + j) * x[j]
-                t[i] = new
-            whole = x[0]
-            for j in range(1, w):
-                whole = jnp.where(sub == j, x[j], whole)
+                t[h + 1] = new
             ms.append(jnp.where(lane < k, home, jnp.where(lane == sub + k, 1.0, 0.0)))
             ns.append(jnp.where(lane < k + w, whole, 0.0))
     return [(jnp.concatenate(ms, axis=0), jnp.concatenate(ns, axis=0)) for ms, ns in outs]
@@ -276,44 +307,62 @@
         compiler_params=pltpu.CompilerParams(vmem_limit_bytes=63000000),
     )(projection, phase_shift, direction)
     along = [swap(pack, z_lo, s) for s in (1, 2, 3)]
-    across = swap(pack, core, 1)
+    other_samples = swap(samples, core, 1)
+    ids = (lax.axis_index(RING_X).astype(jnp.int32).reshape(1),)
     work = 2 * 2 * 1024 * 256 * 128 * 10
-
-    def feats_of(n):
-        return struct((n, 256, 1024), bf16)
-
-    acc_of = struct((128, 1024))
-    own, acc, rows_t = call(
-        own_features, [feats_of(1), acc_of, struct((128, 1024), bf16)], samples, pack, flops=work
-    )
-    other, acc = call(more_features, [feats_of(1), acc_of], rows_t, acc, across, flops=work)
-    stacked = pl.pallas_call(
-        stack_kernel,
-        out_shape=struct((3, PACK, 256), bf16),
-        in_specs=[vmem()] * 3 + [pl.BlockSpec(memory_space=pl.ANY)],
-        out_specs=vmem(),
-        compiler_params=pltpu.CompilerParams(vmem_limit_bytes=16 * 1024 * 1024),
-    )(*along, acc)
-    across_far = swap(stacked, core, 1)
-    own_far, acc = call(more_features, [feats_of(3), acc_of], rows_t, acc, *along, flops=3 * work)
-    other_far, sums = call(
-        last_features,
-        [feats_of(3), struct((1024, 128))],
-        rows_t,
-        acc,
-        across_far,
+    acc_of, rows_of = struct((128, 1024)), struct((128, 1024), bf16)
+    feats_of = struct((256, 1024), bf16)
+    part, low_part = struct((256, 128)), struct((3, 256, 256), bf16)
+    firsts = [feats_of, acc_of, rows_of]
+    own_first, own_acc, own_rows = call(first_features, firsts, samples, pack, flops=work, ids=ids)
+    their_first, their_acc, their_rows = call(
+        first_features, firsts, other_samples, pack, flops=work, ids=ids
+    )
+    their_near, their_acc = call(
+        their_near_features,
+        [feats_of, acc_of],
+        their_rows,
+        their_acc,
+        along[0],
+        after=own_acc,
+        flops=work,
+    )
+    their_far, their_sums = call(
+        their_far_features,
+        [struct((2, 256, 1024), bf16), struct((1024, 128))],
+        their_rows,
+        their_acc,
+        *along[1:],
         scratch=[pltpu.VMEM((128, 1024), f32)],
-        flops=3 * work,
-    )
-    by_x = call(sum_kernel, struct((256, 128)), exchange(sums.reshape(4, 256, 128), RING_X))
-    by_y = call(sum_kernel, struct((32, 128)), exchange(by_x.reshape(8, 32, 128), RING_Y))
-    low = call(low_copies_kernel, struct((8, 32, 128), bf16), by_y, swap(by_y, ("zhi",), 1))
-    low = exchange(low, RING_Y).reshape(256, 128)
-    low = exchange(jnp.broadcast_to(low[None], (4, 256, 128)), RING_X).reshape(1024, 128)
-    theirs = call(back_kernel, struct((4, 256, 128)), other, other_far, low, flops=work // 5)
-    theirs = swap(theirs, core, 1)
-    mine = call(back_kernel, struct((4, 256, 128)), own, own_far, low, flops=work // 5)
-    parts = call(add_kernel, [struct((256, 128))] * 4, mine, theirs)
+        flops=2 * work,
+    )
+    from_other = swap(their_sums, core, 1)
+    own_rest, sums, last = [None] * 4, [None] * 4, their_sums
+    for q in (2, 1, 3, 0):
+        own_rest[q], sums[q] = call(
+            functools.partial(own_quarter, q),
+            [low_part, part],
+            own_rows,
+            own_acc,
+            *along,
+            *(() if q == 2 else (from_other,)),
+            after=last,
+            scratch=[pltpu.VMEM((128, 256), f32)],
+            flops=3 * work // 4,
+        )
+        last = sums[q]
+        if q == 2:
+            last = sums[q] = call(functools.partial(add_quarter, q), part, sums[q], from_other)
+        if q:
+            sums[q] = swap(sums[q], RING_X, q)
+    pieces = exchange(call(four_sum, struct((16, 32, 128)), *sums), RING_Y + ("zhi",))
+    low = call(low_copies_kernel, struct((32, 32, 128), bf16), pieces)
+    low = exchange(low, RING_X + RING_Y).reshape(4, 256, 128)
+    other_low = swap(low, core, 1)
+    parts = call(own_back, [part] * 4, own_first, *own_rest, low, flops=work // 5, ids=ids)
+    parts = call(
+        their_back, [part] * 4, their_first, their_near, their_far, other_low, *parts, flops=work // 5, ids=ids
+    )
     parts = [parts[0]] + [swap(parts[s], z_lo, s) for s in (1, 2, 3)]
     applied, gram = call(
         gram_kernel, [struct((256, 128)), struct((GRAM, 128))], *parts, direction, residual

time: 179 us -> 168 us (0.939)
  blocking collectives: 95.3 us -> 84.6 us
  waiting for transfers between devices: 8.36 us -> 13.1 us
  Pallas kernels: 25.9 us -> 22.4 us
    all_to_all x8 -> x6, blocking collectives: 95.3 us -> 84.6 us  [exchange(): return lax.all_to_all(value, axes, 0, 0)]
    ppermute x10 -> x12, waiting for transfers between devices: 8.36 us -> 13.1 us  [swap(): return lax.ppermute(value, axes, [(i, i ^ s) for i in range(n)])]
    pallas_call x16 -> x18, Pallas kernels: 24.2 us -> 20.6 us  [call(): pl.pallas_call(kernel, out_shape=outs, in_specs=specs, out_specs=jax.tree...]
    ppermute x10 -> x12, starting transfers between devices: 45.8 us -> 45.3 us  [swap(): return lax.ppermute(value, axes, [(i, i ^ s) for i in range(n)])]
  transfers between devices with their start and end apart: 10 -> 12, of which waited for: 6 -> 5; matrix products, arithmetic and copies ran while one was open for 0% -> 0% of each run, Pallas kernels for 4% -> 6%
where the time goes in v3:
time: 168 us; the launch traced here: 167 us
  blocking collectives  84.6 us (50%)
  starting transfers between devices  45.3 us (27%)
  Pallas kernels  22.4 us (13%)
  waiting for transfers between devices  13.1 us (8%)
    all_to_all x6, blocking collectives, exchange(): return lax.all_to_all(value, axes, 0, 0)  84.6 us
    ppermute x12, starting transfers between devices, swap(): return lax.ppermute(value, axes, [(i, i ^ s) for i in range(n)])  45.3 us
    pallas_call x18, Pallas kernels, call(): pl.pallas_call(kernel, out_shape=outs, in_specs=specs, out_specs=jax.tree...  20.6 us
    ppermute x12, waiting for transfers between devices, swap(): return lax.ppermute(value, axes, [(i, i ^ s) for i in range(n)])  13.1 us
  transfers between devices with their start and end apart: 12, of which 5 were waited for; matrix products, arithmetic and copies ran while one was open for 0% of the time, Pallas kernels for 6%

profile of v3, /device:TPU:1, one launch (start us, length us, event | category | flops | bytes accessed | tf_op | source)
XLA Modules:
  0.0 167.3 jit_solution(14670566738742507089)
XLA Ops:
  0.6 8.9 %collective-permute-start = (bf16[1024,128]{1,0:T(8,128)(2,1)}, bf16[1024,128]{1,0:T(8,128)(2,1)S(1)}, u32[]{:S(2)}, u32[]{:S(2)}) collective-permute-start(bf16[1024,128]{1,0:T(8,128)(2,1)} %samples_ref.1), channel_id=1, source_target_pairs={{0,64},{64,0},{1,65},{65,1},{2,66},{66,2},{3,67},{67,3},{4,68},{68... | collective-permute-start | bytes 786440 | tf_op jit(solution)/shard_map/ppermute | solution.py:286
  9.6 1.7 %shard_map.85.pack_ref = bf16[272,256]{1,0:T(8,128)(2,1)} custom-call(bf16[128,256]{1,0:T(8,128)(2,1)} %proj_in.1, bf16[1,256]{1,0:T(2,128)(2,1)} %shift_in.1, f32[256,128]{1,0:T(8,128)} %dir_ref.3), custom_call_target="tpu_custom_call" | custom-call | tf_op jit(solution)/shard_map/pallas_call | solution.py:296
  11.3 2.2 %collective-permute-start.3 = (bf16[272,256]{1,0:T(8,128)(2,1)}, bf16[272,256]{1,0:T(8,128)(2,1)S(1)}, u32[]{:S(2)}, u32[]{:S(2)}) collective-permute-start(bf16[272,256]{1,0:T(8,128)(2,1)} %shard_map.85.pack_ref), channel_id=1, source_target_pairs={{0,384},{128,256},{256,128},{384,0},{1,385},{129,257},{257,129},{3... | collective-permute-start | bytes 417800 | tf_op jit(solution)/shard_map/ppermute | solution.py:286
  13.5 1.9 %collective-permute-start.2 = (bf16[272,256]{1,0:T(8,128)(2,1)}, bf16[272,256]{1,0:T(8,128)(2,1)S(1)}, u32[]{:S(2)}, u32[]{:S(2)}) collective-permute-start(bf16[272,256]{1,0:T(8,128)(2,1)} %shard_map.85.pack_ref), channel_id=1, source_target_pairs={{0,256},{128,384},{256,0},{384,128},{1,257},{129,385},{257,1},{385... | collective-permute-start | bytes 417800 | tf_op jit(solution)/shard_map/ppermute | solution.py:286
  15.5 5.1 %collective-permute-start.1 = (bf16[272,256]{1,0:T(8,128)(2,1)}, bf16[272,256]{1,0:T(8,128)(2,1)S(1)}, u32[]{:S(2)}, u32[]{:S(2)}) collective-permute-start(bf16[272,256]{1,0:T(8,128)(2,1)} %shard_map.85.pack_ref), channel_id=1, source_target_pairs={{0,128},{128,0},{256,384},{384,256},{1,129},{129,1},{257,385},{385... | collective-permute-start | bytes 417800 | tf_op jit(solution)/shard_map/ppermute | solution.py:286
  24.3 2.8 %collective-permute-done.1.p1 = bf16[272,256]{1,0:T(8,128)(2,1)S(1)} collective-permute-done((bf16[272,256]{1,0:T(8,128)(2,1)}, bf16[272,256]{1,0:T(8,128)(2,1)S(1)}, u32[]{:S(2)}, u32[]{:S(2)}) %collective-permute-start.1) | collective-permute-done | bytes 139296 | tf_op jit(solution)/shard_map/ppermute | solution.py:286
  28.6 2.6 %shard_map.89 = (bf16[2,256,1024]{2,1,0:T(8,128)(2,1)S(1)}, f32[1024,128]{1,0:T(8,128)S(1)}) custom-call(bf16[128,1024]{1,0:T(8,128)(2,1)S(1)} %get-tuple-element.32.rows_t, f32[128,1024]{1,0:T(8,128)S(1)} %get-tuple-element.36.acc_in, bf16[272,256]{1,0:T(8,128)(2,1)S(1)} %collective-permute-done.2.p2, bf16[272,256]{1,0:T(8,128)(2,1)S(1)} %collective-permute-done.3.p3), custom_call_target="tpu_custom_call" | custom-call | flops 2684354560 | tf_op jit(solution)/shard_map/pallas_call | solution.py:40
  31.2 3.0 %collective-permute-start.4 = (f32[1024,128]{1,0:T(8,128)S(1)}, f32[1024,128]{1,0:T(8,128)S(1)}, u32[]{:S(2)}, u32[]{:S(2)}) collective-permute-start(f32[1024,128]{1,0:T(8,128)S(1)} %get-tuple-element.39.refs_0_), channel_id=1, source_target_pairs={{0,64},{64,0},{1,65},{65,1},{2,66},{66,2},{3,67},{67,3},{4,68},{68... | collective-permute-start | bytes 1572872 | tf_op jit(solution)/shard_map/ppermute | solution.py:286
  35.7 3.0 %collective-permute-start.6 = (f32[256,128]{1,0:T(8,128)S(1)}, f32[256,128]{1,0:T(8,128)S(1)}, u32[]{:S(2)}, u32[]{:S(2)}) collective-permute-start(f32[256,128]{1,0:T(8,128)S(1)} %shard_map.91.refs_1_), channel_id=1, source_target_pairs={{0,4},{2,6},{4,0},{6,2},{1,5},{3,7},{5,1},{7,3},{8,12},{10,14},{12... | collective-permute-start | bytes 393224 | tf_op jit(solution)/shard_map/ppermute | solution.py:286
  39.8 2.2 %collective-permute-start.5 = (f32[256,128]{1,0:T(8,128)S(1)}, f32[256,128]{1,0:T(8,128)S(1)}, u32[]{:S(2)}, u32[]{:S(2)}) collective-permute-start(f32[256,128]{1,0:T(8,128)S(1)} %get-tuple-element.41.refs_1_), channel_id=1, source_target_pairs={{0,2},{2,0},{4,6},{6,4},{1,3},{3,1},{5,7},{7,5},{8,10},{10,8},{12,... | collective-permute-start | bytes 393224 | tf_op jit(solution)/shard_map/ppermute | solution.py:286
  43.0 3.8 %collective-permute-start.7 = (f32[256,128]{1,0:T(8,128)S(1)}, f32[256,128]{1,0:T(8,128)S(1)}, u32[]{:S(2)}, u32[]{:S(2)}) collective-permute-start(f32[256,128]{1,0:T(8,128)S(1)} %get-tuple-element.42.refs_1_), channel_id=1, source_target_pairs={{0,6},{2,4},{4,2},{6,0},{1,7},{3,5},{5,3},{7,1},{8,14},{10,12},{12... | collective-permute-start | bytes 393224 | tf_op jit(solution)/shard_map/ppermute | solution.py:286
  47.8 2.1 %collective-permute-done.7.d = f32[256,128]{1,0:T(8,128)S(1)} collective-permute-done((f32[256,128]{1,0:T(8,128)S(1)}, f32[256,128]{1,0:T(8,128)S(1)}, u32[]{:S(2)}, u32[]{:S(2)}) %collective-permute-start.7) | collective-permute-done | bytes 131104 | tf_op jit(solution)/shard_map/ppermute | solution.py:286
  49.9 24.7 %all_to_all.30.in_ref = f32[16,32,128]{2,1,0:T(8,128)S(1)} all-to-all(f32[16,32,128]{2,1,0:T(8,128)S(1)} %shard_map.95), channel_id=1, replica_groups=mesh['z2'=2,'z1'=2,'core'=2,'y4'=2,'y2'=2,'y1'=2,'x2'=2,'x1'=2,'zhi'=2] ..., dimensions={0} | all-to-all | bytes 524288 | tf_op jit(solution)/shard_map/all_to_all | solution.py:290
  74.7 14.3 %all_to_all.31 = bf16[32,32,128]{2,1,0:T(8,128)(2,1)S(1)} all-to-all(bf16[32,32,128]{2,1,0:T(8,128)(2,1)S(1)} %shard_map.96), channel_id=1, replica_groups=mesh['z2'=2,'z1'=2,'core'=2,'y4'=2,'y2'=2,'y1'=2,'x2'=2,'x1'=2,'zhi'=2] ..., dimensions={0} | all-to-all | bytes 524288 | tf_op jit(solution)/shard_map/all_to_all | solution.py:290
  88.9 5.9 %collective-permute-start.8 = (bf16[4,256,128]{2,1,0:T(8,128)(2,1)S(1)}, bf16[4,256,128]{2,1,0:T(8,128)(2,1)S(1)}, u32[]{:S(2)}, u32[]{:S(2)}) collective-permute-start(bf16[4,256,128]{2,1,0:T(8,128)(2,1)S(1)} %bitcast.4), channel_id=1, source_target_pairs={{0,64},{64,0},{1,65},{65,1},{2,66},{66,2},{3,67},{67,3},{4,68},{68... | collective-permute-start | bytes 786440 | tf_op jit(solution)/shard_map/ppermute | solution.py:286
  96.6 2.9 %collective-permute-start.9 = (f32[256,128]{1,0:T(8,128)S(1)}, f32[256,128]{1,0:T(8,128)S(1)}, u32[]{:S(2)}, u32[]{:S(2)}) collective-permute-start(f32[256,128]{1,0:T(8,128)S(1)} %get-tuple-element.54), channel_id=1, source_target_pairs={{0,128},{128,0},{256,384},{384,256},{1,129},{129,1},{257,385},{385... | collective-permute-start | bytes 393224 | tf_op jit(solution)/shard_map/ppermute | solution.py:286
  99.5 3.3 %collective-permute-start.10 = (f32[256,128]{1,0:T(8,128)S(1)}, f32[256,128]{1,0:T(8,128)S(1)}, u32[]{:S(2)}, u32[]{:S(2)}) collective-permute-start(f32[256,128]{1,0:T(8,128)S(1)} %get-tuple-element.55), channel_id=1, source_target_pairs={{0,256},{128,384},{256,0},{384,128},{1,257},{129,385},{257,1},{385... | collective-permute-start | bytes 393224 | tf_op jit(solution)/shard_map/ppermute | solution.py:286
  102.8 3.1 %collective-permute-start.11 = (f32[256,128]{1,0:T(8,128)S(1)}, f32[256,128]{1,0:T(8,128)S(1)}, u32[]{:S(2)}, u32[]{:S(2)}) collective-permute-start(f32[256,128]{1,0:T(8,128)S(1)} %get-tuple-element.56), channel_id=1, source_target_pairs={{0,384},{128,256},{256,128},{384,0},{1,385},{129,257},{257,129},{3... | collective-permute-start | bytes 393224 | tf_op jit(solution)/shard_map/ppermute | solution.py:286
  105.9 7.2 %collective-permute-done.10.p2 = f32[256,128]{1,0:T(8,128)S(1)} collective-permute-done((f32[256,128]{1,0:T(8,128)S(1)}, f32[256,128]{1,0:T(8,128)S(1)}, u32[]{:S(2)}, u32[]{:S(2)}) %collective-permute-start.10) | collective-permute-done | bytes 131104 | tf_op jit(solution)/shard_map/ppermute | solution.py:286
  113.8 9.5 %all_to_all.32.in_ref = f32[8,48,128]{2,1,0:T(8,128)S(1)} all-to-all(f32[8,48,128]{2,1,0:T(8,128)S(1)} %bitcast.7), channel_id=1, replica_groups=mesh['z2'=2,'z1'=2,'core'=2,'y4'=2,'y2'=2,'y1'=2,'x2'=2,'x1'=2,'zhi'=2] ..., dimensions={0} | all-to-all | bytes 393216 | tf_op jit(solution)/shard_map/all_to_all | solution.py:290
  123.3 11.0 %all_to_all.33.in_ref = f32[8,48,128]{2,1,0:T(8,128)S(1)} all-to-all(f32[8,48,128]{2,1,0:T(8,128)S(1)} %shard_map.100), channel_id=1, replica_groups=mesh['z2'=2,'z1'=2,'core'=2,'y4'=2,'y2'=2,'y1'=2,'x2'=2,'x1'=2,'zhi'=2] ..., dimensions={0} | all-to-all | bytes 393216 | tf_op jit(solution)/shard_map/all_to_all | solution.py:290
  134.4 12.7 %all_to_all.34.in_ref = f32[8,48,128]{2,1,0:T(8,128)S(1)} all-to-all(f32[8,48,128]{2,1,0:T(8,128)S(1)} %shard_map.101), channel_id=1, replica_groups=mesh['z2'=2,'z1'=2,'core'=2,'y4'=2,'y2'=2,'y1'=2,'x2'=2,'x1'=2,'zhi'=2] ..., dimensions={0} | all-to-all | bytes 393216 | tf_op jit(solution)/shard_map/all_to_all | solution.py:290
  147.1 12.5 %all_to_all.35 = f32[8,48,128]{2,1,0:T(8,128)S(1)} all-to-all(f32[8,48,128]{2,1,0:T(8,128)S(1)} %shard_map.102), channel_id=1, replica_groups=mesh['z2'=2,'z1'=2,'core'=2,'y4'=2,'y2'=2,'y1'=2,'x2'=2,'x1'=2,'zhi'=2] ..., dimensions={0} | all-to-all | bytes 393216 | tf_op jit(solution)/shard_map/all_to_all | solution.py:290
  159.6 7.7 %shard_map.103 = (f32[256,128]{1,0:T(8,128)}, f32[256,128]{1,0:T(8,128)}, f32[256,128]{1,0:T(8,128)}) custom-call(f32[384,128]{1,0:T(8,128)S(1)} %bitcast.6, f32[256,128]{1,0:T(8,128)S(1)} %get-tuple-element.58.applied_ref, f32[256,128]{1,0:T(8,128)S(1)} %copy-done, f32[256,128]{1,0:T(8,128)S(1)} %copy-done.1, f32[256,128]{1,0:T(8,128)S(1)} %copy-done.4), custom_call_target="tpu_custom_call" | custom-call | tf_op jit(solution)/shard_map/pallas_call | solution.py:40
  (37 shorter events, 12.2 us)
Async XLA Ops:
  0.6 20.0 %copy-start.5 = (bf16[1024,128]{1,0:T(8,128)(2,1)S(1)}, bf16[1024,128]{1,0:T(8,128)(2,1)}, u32[]{:S(2)}) copy-start(bf16[1024,128]{1,0:T(8,128)(2,1)} %samples_ref.1) | copy-start | bytes 786436
  0.6 22.3 %collective-permute-start = (bf16[1024,128]{1,0:T(8,128)(2,1)}, bf16[1024,128]{1,0:T(8,128)(2,1)S(1)}, u32[]{:S(2)}, u32[]{:S(2)}) collective-permute-start(bf16[1024,128]{1,0:T(8,128)(2,1)} %samples_ref.1), channel_id=1, source_target_pairs={{0,64},{64,0},{1,65},{65,1},{2,66},{66,2},{3,67},{67,3},{4,68},{68... | collective-permute-start | bytes 786440 | tf_op jit(solution)/shard_map/ppermute | solution.py:286
  11.3 17.3 %collective-permute-start.3 = (bf16[272,256]{1,0:T(8,128)(2,1)}, bf16[272,256]{1,0:T(8,128)(2,1)S(1)}, u32[]{:S(2)}, u32[]{:S(2)}) collective-permute-start(bf16[272,256]{1,0:T(8,128)(2,1)} %shard_map.85.pack_ref), channel_id=1, source_target_pairs={{0,384},{128,256},{256,128},{384,0},{1,385},{129,257},{257,129},{3... | collective-permute-start | bytes 417800 | tf_op jit(solution)/shard_map/ppermute | solution.py:286
  13.5 15.0 %collective-permute-start.2 = (bf16[272,256]{1,0:T(8,128)(2,1)}, bf16[272,256]{1,0:T(8,128)(2,1)S(1)}, u32[]{:S(2)}, u32[]{:S(2)}) collective-permute-start(bf16[272,256]{1,0:T(8,128)(2,1)} %shard_map.85.pack_ref), channel_id=1, source_target_pairs={{0,256},{128,384},{256,0},{384,128},{1,257},{129,385},{257,1},{385... | collective-permute-start | bytes 417800 | tf_op jit(solution)/shard_map/ppermute | solution.py:286
  15.5 11.7 %collective-permute-start.1 = (bf16[272,256]{1,0:T(8,128)(2,1)}, bf16[272,256]{1,0:T(8,128)(2,1)S(1)}, u32[]{:S(2)}, u32[]{:S(2)}) collective-permute-start(bf16[272,256]{1,0:T(8,128)(2,1)} %shard_map.85.pack_ref), channel_id=1, source_target_pairs={{0,128},{128,0},{256,384},{384,256},{1,129},{129,1},{257,385},{385... | collective-permute-start | bytes 417800 | tf_op jit(solution)/shard_map/ppermute | solution.py:286
  20.6 0.9 copy-start.2
  21.5 1.4 copy-start.3
  31.2 4.5 %collective-permute-start.4 = (f32[1024,128]{1,0:T(8,128)S(1)}, f32[1024,128]{1,0:T(8,128)S(1)}, u32[]{:S(2)}, u32[]{:S(2)}) collective-permute-start(f32[1024,128]{1,0:T(8,128)S(1)} %get-tuple-element.39.refs_0_), channel_id=1, source_target_pairs={{0,64},{64,0},{1,65},{65,1},{2,66},{66,2},{3,67},{67,3},{4,68},{68... | collective-permute-start | bytes 1572872 | tf_op jit(solution)/shard_map/ppermute | solution.py:286
  35.7 12.0 %collective-permute-start.6 = (f32[256,128]{1,0:T(8,128)S(1)}, f32[256,128]{1,0:T(8,128)S(1)}, u32[]{:S(2)}, u32[]{:S(2)}) collective-permute-start(f32[256,128]{1,0:T(8,128)S(1)} %shard_map.91.refs_1_), channel_id=1, source_target_pairs={{0,4},{2,6},{4,0},{6,2},{1,5},{3,7},{5,1},{7,3},{8,12},{10,14},{12... | collective-permute-start | bytes 393224 | tf_op jit(solution)/shard_map/ppermute | solution.py:286
  39.8 8.0 %collective-permute-start.5 = (f32[256,128]{1,0:T(8,128)S(1)}, f32[256,128]{1,0:T(8,128)S(1)}, u32[]{:S(2)}, u32[]{:S(2)}) collective-permute-start(f32[256,128]{1,0:T(8,128)S(1)} %get-tuple-element.41.refs_1_), channel_id=1, source_target_pairs={{0,2},{2,0},{4,6},{6,4},{1,3},{3,1},{5,7},{7,5},{8,10},{10,8},{12,... | collective-permute-start | bytes 393224 | tf_op jit(solution)/shard_map/ppermute | solution.py:286
  43.0 6.9 %collective-permute-start.7 = (f32[256,128]{1,0:T(8,128)S(1)}, f32[256,128]{1,0:T(8,128)S(1)}, u32[]{:S(2)}, u32[]{:S(2)}) collective-permute-start(f32[256,128]{1,0:T(8,128)S(1)} %get-tuple-element.42.refs_1_), channel_id=1, source_target_pairs={{0,6},{2,4},{4,2},{6,0},{1,7},{3,5},{5,3},{7,1},{8,14},{10,12},{12... | collective-permute-start | bytes 393224 | tf_op jit(solution)/shard_map/ppermute | solution.py:286
  88.9 7.0 %collective-permute-start.8 = (bf16[4,256,128]{2,1,0:T(8,128)(2,1)S(1)}, bf16[4,256,128]{2,1,0:T(8,128)(2,1)S(1)}, u32[]{:S(2)}, u32[]{:S(2)}) collective-permute-start(bf16[4,256,128]{2,1,0:T(8,128)(2,1)S(1)} %bitcast.4), channel_id=1, source_target_pairs={{0,64},{64,0},{1,65},{65,1},{2,66},{66,2},{3,67},{67,3},{4,68},{68... | collective-permute-start | bytes 786440 | tf_op jit(solution)/shard_map/ppermute | solution.py:286
  95.9 17.2 %copy-start = (f32[256,128]{1,0:T(8,128)S(1)}, f32[256,128]{1,0:T(8,128)}, u32[]{:S(2)}) copy-start(f32[256,128]{1,0:T(8,128)} %dir_ref.3) | copy-start | bytes 393220
  95.9 17.2 %copy-start.1 = (f32[256,128]{1,0:T(8,128)S(1)}, f32[256,128]{1,0:T(8,128)}, u32[]{:S(2)}) copy-start(f32[256,128]{1,0:T(8,128)} %res_ref.3) | copy-start | bytes 393220
  96.6 9.3 %collective-permute-start.9 = (f32[256,128]{1,0:T(8,128)S(1)}, f32[256,128]{1,0:T(8,128)S(1)}, u32[]{:S(2)}, u32[]{:S(2)}) collective-permute-start(f32[256,128]{1,0:T(8,128)S(1)} %get-tuple-element.54), channel_id=1, source_target_pairs={{0,128},{128,0},{256,384},{384,256},{1,129},{129,1},{257,385},{385... | collective-permute-start | bytes 393224 | tf_op jit(solution)/shard_map/ppermute | solution.py:286
  99.5 13.6 %collective-permute-start.10 = (f32[256,128]{1,0:T(8,128)S(1)}, f32[256,128]{1,0:T(8,128)S(1)}, u32[]{:S(2)}, u32[]{:S(2)}) collective-permute-start(f32[256,128]{1,0:T(8,128)S(1)} %get-tuple-element.55), channel_id=1, source_target_pairs={{0,256},{128,384},{256,0},{384,128},{1,257},{129,385},{257,1},{385... | collective-permute-start | bytes 393224 | tf_op jit(solution)/shard_map/ppermute | solution.py:286
  102.8 10.3 %collective-permute-start.11 = (f32[256,128]{1,0:T(8,128)S(1)}, f32[256,128]{1,0:T(8,128)S(1)}, u32[]{:S(2)}, u32[]{:S(2)}) collective-permute-start(f32[256,128]{1,0:T(8,128)S(1)} %get-tuple-element.56), channel_id=1, source_target_pairs={{0,384},{128,256},{256,128},{384,0},{1,385},{129,257},{257,129},{3... | collective-permute-start | bytes 393224 | tf_op jit(solution)/shard_map/ppermute | solution.py:286
  147.1 12.5 %copy-start.4 = (f32[256,128]{1,0:T(8,128)S(1)}, f32[256,128]{1,0:T(8,128)}, u32[]{:S(2)}) copy-start(f32[256,128]{1,0:T(8,128)} %sol_ref.1) | copy-start | bytes 393220

commit v4 on v3

--- a/solution.py
+++ b/solution.py
@@ -18,14 +18,13 @@
 SCALE = math.sqrt(2.0 / FEATURES)
 ROUNDER = 12582912.0
 PACK = 272
-GRAM = 384
+GRAM = 512
 
 AXES = ("z2", "z1", "core", "y4", "y2", "y1", "x2", "x1", "zhi")
 DP = ("z2", "z1", "core")
 RING_X = ("x2", "x1")
 RING_Y = ("y4", "y2", "y1")
 RING_Z = ("zhi", "z2", "z1")
-CHIP_X = ("x2", "x1", "core")
 
 
 def vmem():
@@ -146,7 +145,7 @@
 
 def sum_copies_kernel(in_ref, out_ref):
     total = total_of(in_ref)
-    for i in range(8):
+    for i in range(out_ref.shape[0]):
         out_ref[i] = total
 
 
@@ -166,16 +165,24 @@
         outs[s][...] = total
 
 
-def their_back(ids_ref, first_ref, near_ref, far_ref, low_ref, a0, a1, a2, a3, *outs):
-    for s, part in enumerate((a0, a1, a2, a3)):
+def their_far_back(ids_ref, far_ref, low_ref, a2, a3, *outs):
+    for s, part in enumerate((a2, a3)):
         total = part[...]
         for q in range(4):
-            cols = slice(q * 256, (q + 1) * 256)
-            feats = (first_ref, near_ref, far_ref.at[0], far_ref.at[1])[s][:, cols]
+            feats = far_ref[s, :, q * 256 : (q + 1) * 256]
             total += jnp.dot(feats, low_ref[ids_ref[0] ^ q], preferred_element_type=f32)
         outs[s][...] = total
 
 
+def their_near_back(ids_ref, first_ref, near_ref, low_ref, a0, a1, after_ref, *outs):
+    for s, (ref, part) in enumerate(((first_ref, a0), (near_ref, a1))):
+        total = part[...]
+        for q in range(4):
+            feats = ref[:, q * 256 : (q + 1) * 256]
+            total += jnp.dot(feats, low_ref[ids_ref[0] ^ q], preferred_element_type=f32)
+        outs[s][...] = total
+
+
 def fdot(a, b):
     return jnp.dot(a, b, precision=highest, preferred_element_type=f32)
 
@@ -184,26 +191,23 @@
     return 0.5 * (m + m.T)
 
 
-def places():
-    n = 128
-    return lax.broadcasted_iota(jnp.int32, (n, n), 0), lax.broadcasted_iota(jnp.int32, (n, n), 1)
-
-
-def gram_kernel(p0, p1, p2, p3, dir_ref, res_ref, applied_ref, gram_ref):
-    total = (p0[...] + p1[...]) + (p2[...] + p3[...])
+def two_sum(a, b, out_ref):
+    out_ref[...] = a[...] + b[...]
+
+
+def gram_kernel(far, own, near, dir_ref, res_ref, applied_ref, gram_ref):
+    total = far[...] + (own[...] + near[...])
     applied = total + penalty * dir_ref[...]
     applied_ref[...] = applied
     applied_t = applied.T
-    dir_gram = sym(fdot(applied_t, dir_ref[...]))
-    applied_gram = fdot(applied_t, applied)
-    res_gram = sym(fdot(res_ref[...].T, res_ref[...]))
-    at_row, at_col = places()
-    diag = jnp.sum(jnp.where(at_row == at_col, applied_gram, 0.0), axis=1, keepdims=True)
-    gram_ref[0:128, :] = jnp.where(at_col >= at_row, dir_gram, applied_gram)
-    gram_ref[128:256, :] = fdot(applied_t, res_ref[...])
-    gram_ref[256:384, :] = jnp.where(
-        at_col >= at_row, res_gram, jnp.where(at_col == 0, diag, diag[0:1, 0:1])
-    )
+    grams = (
+        fdot(applied_t, dir_ref[...]),
+        fdot(applied_t, res_ref[...]),
+        fdot(applied_t, applied),
+        fdot(res_ref[...].T, res_ref[...]),
+    )
+    for i, g in enumerate(grams):
+        gram_ref[128 * i : 128 * i + 128, :] = g
 
 
 def inverse_factors(mats):
@@ -262,13 +266,10 @@
 
 
 def final_kernel(gram_ref, applied_ref, dir_ref, res_ref, sol_ref, sol_out, res_out, dir_out):
-    at_row, at_col = places()
-    first, cross, third = (gram_ref[128 * i : 128 * i + 128, :] for i in range(3))
-    first_t, third_t = first.T, third.T
-    dir_gram = jnp.where(at_col >= at_row, first, first_t)
-    res_gram = jnp.where(at_col >= at_row, third, third_t)
-    diag = jnp.where(at_row == 0, third[127:128, 1:2], third[:, 0:1])
-    applied_gram = jnp.where(at_col < at_row, first, jnp.where(at_col == at_row, diag, first_t))
+    dir_gram = sym(gram_ref[0:128, :])
+    cross = gram_ref[128:256, :]
+    applied_gram = gram_ref[256:384, :]
+    res_gram = sym(gram_ref[384:512, :])
     (m_d, n_d), (m_r, n_r) = inverse_factors([dir_gram, res_gram])
     step = fdot(m_d.T, fdot(n_d, res_gram))
     step_t = step.T
@@ -360,18 +361,31 @@
     low = exchange(low, RING_X + RING_Y).reshape(4, 256, 128)
     other_low = swap(low, core, 1)
     parts = call(own_back, [part] * 4, own_first, *own_rest, low, flops=work // 5, ids=ids)
+    far_parts = call(
+        their_far_back, [part] * 2, their_far, other_low, *parts[2:], flops=work // 10, ids=ids
+    )
     parts = call(
-        their_back, [part] * 4, their_first, their_near, their_far, other_low, *parts, flops=work // 5, ids=ids
-    )
-    parts = [parts[0]] + [swap(parts[s], z_lo, s) for s in (1, 2, 3)]
+        their_near_back,
+        [part] * 2,
+        their_first,
+        their_near,
+        other_low,
+        *parts[:2],
+        after=far_parts[1],
+        flops=work // 10,
+        ids=ids,
+    )
+    parts = [*parts, *far_parts]
+    received = [swap(parts[s], z_lo, s) for s in (1, 2, 3)]
+    far_sum = call(two_sum, part, received[1], received[2])
     applied, gram = call(
-        gram_kernel, [struct((256, 128)), struct((GRAM, 128))], *parts, direction, residual
-    )
-    chunk = GRAM // 8
-    piece = exchange(gram.reshape(8, chunk, 128), CHIP_X)
-    for axes in (RING_Y, RING_Z, CHIP_X):
-        piece = call(sum_copies_kernel, struct((8, chunk, 128)), piece)
-        piece = exchange(piece, axes)
+        gram_kernel, [struct((256, 128)), struct((GRAM, 128))], far_sum, parts[0], received[0], direction, residual
+    )
+    plane, column = RING_X + RING_Y, RING_Z + ("core",)
+    chunk = GRAM // 32
+    piece = exchange(gram.reshape(32, chunk, 128), plane)
+    piece = exchange(call(sum_copies_kernel, struct((16, chunk, 128)), piece), column)
+    piece = exchange(call(sum_copies_kernel, struct((32, chunk, 128)), piece), plane)
     return call(
         final_kernel,
         [struct((256, 128))] * 3,

time: 168 us -> 167 us (level)
    all_to_all x6 -> x5, blocking collectives: 84.6 us -> 83.2 us  [exchange(): return lax.all_to_all(value, axes, 0, 0)]
    pallas_call x18 -> x19, Pallas kernels: 20.6 us -> 20.8 us  [call(): pl.pallas_call(kernel, out_shape=outs, in_specs=specs, out_specs=jax.tree...]
  transfers between devices with their start and end apart: 12 -> 12, of which waited for: 5 -> 6; matrix products, arithmetic and copies ran while one was open for 0% -> 0% of each run, Pallas kernels for 6% -> 7%
where the time goes in v4:
time: 167 us; the launch traced here: 166 us
  blocking collectives  83.2 us (50%)
  starting transfers between devices  45 us (27%)
  Pallas kernels  22.5 us (13%)
  waiting for transfers between devices  13 us (8%)
    all_to_all x5, blocking collectives, exchange(): return lax.all_to_all(value, axes, 0, 0)  83.2 us
    ppermute x12, starting transfers between devices, swap(): return lax.ppermute(value, axes, [(i, i ^ s) for i in range(n)])  45 us
    pallas_call x19, Pallas kernels, call(): pl.pallas_call(kernel, out_shape=outs, in_specs=specs, out_specs=jax.tree...  20.8 us
    ppermute x12, waiting for transfers between devices, swap(): return lax.ppermute(value, axes, [(i, i ^ s) for i in range(n)])  13 us
  transfers between devices with their start and end apart: 12, of which 6 were waited for; matrix products, arithmetic and copies ran while one was open for 0% of the time, Pallas kernels for 7%

profile of v4, /device:TPU:1, one launch (start us, length us, event | category | flops | bytes accessed | tf_op | source)
XLA Modules:
  0.0 165.6 jit_solution(15959863863459405575)
XLA Ops:
  0.6 8.9 %collective-permute-start = (bf16[1024,128]{1,0:T(8,128)(2,1)}, bf16[1024,128]{1,0:T(8,128)(2,1)S(1)}, u32[]{:S(2)}, u32[]{:S(2)}) collective-permute-start(bf16[1024,128]{1,0:T(8,128)(2,1)} %samples_ref.1), channel_id=1, source_target_pairs={{0,64},{64,0},{1,65},{65,1},{2,66},{66,2},{3,67},{67,3},{4,68},{68... | collective-permute-start | bytes 786440 | tf_op jit(solution)/shard_map/ppermute | solution.py:287
  9.6 1.7 %shard_map.85.pack_ref = bf16[272,256]{1,0:T(8,128)(2,1)} custom-call(bf16[128,256]{1,0:T(8,128)(2,1)} %proj_in.1, bf16[1,256]{1,0:T(2,128)(2,1)} %shift_in.1, f32[256,128]{1,0:T(8,128)} %dir_ref.3), custom_call_target="tpu_custom_call" | custom-call | tf_op jit(solution)/shard_map/pallas_call | solution.py:297
  11.3 2.2 %collective-permute-start.3 = (bf16[272,256]{1,0:T(8,128)(2,1)}, bf16[272,256]{1,0:T(8,128)(2,1)S(1)}, u32[]{:S(2)}, u32[]{:S(2)}) collective-permute-start(bf16[272,256]{1,0:T(8,128)(2,1)} %shard_map.85.pack_ref), channel_id=1, source_target_pairs={{0,384},{128,256},{256,128},{384,0},{1,385},{129,257},{257,129},{3... | collective-permute-start | bytes 417800 | tf_op jit(solution)/shard_map/ppermute | solution.py:287
  13.5 1.9 %collective-permute-start.2 = (bf16[272,256]{1,0:T(8,128)(2,1)}, bf16[272,256]{1,0:T(8,128)(2,1)S(1)}, u32[]{:S(2)}, u32[]{:S(2)}) collective-permute-start(bf16[272,256]{1,0:T(8,128)(2,1)} %shard_map.85.pack_ref), channel_id=1, source_target_pairs={{0,256},{128,384},{256,0},{384,128},{1,257},{129,385},{257,1},{385... | collective-permute-start | bytes 417800 | tf_op jit(solution)/shard_map/ppermute | solution.py:287
  15.4 5.1 %collective-permute-start.1 = (bf16[272,256]{1,0:T(8,128)(2,1)}, bf16[272,256]{1,0:T(8,128)(2,1)S(1)}, u32[]{:S(2)}, u32[]{:S(2)}) collective-permute-start(bf16[272,256]{1,0:T(8,128)(2,1)} %shard_map.85.pack_ref), channel_id=1, source_target_pairs={{0,128},{128,0},{256,384},{384,256},{1,129},{129,1},{257,385},{385... | collective-permute-start | bytes 417800 | tf_op jit(solution)/shard_map/ppermute | solution.py:287
  24.3 2.8 %collective-permute-done.1.p1 = bf16[272,256]{1,0:T(8,128)(2,1)S(1)} collective-permute-done((bf16[272,256]{1,0:T(8,128)(2,1)}, bf16[272,256]{1,0:T(8,128)(2,1)S(1)}, u32[]{:S(2)}, u32[]{:S(2)}) %collective-permute-start.1) | collective-permute-done | bytes 139296 | tf_op jit(solution)/shard_map/ppermute | solution.py:287
  28.5 2.6 %shard_map.89 = (bf16[2,256,1024]{2,1,0:T(8,128)(2,1)S(1)}, f32[1024,128]{1,0:T(8,128)S(1)}) custom-call(bf16[128,1024]{1,0:T(8,128)(2,1)S(1)} %get-tuple-element.31.rows_t, f32[128,1024]{1,0:T(8,128)S(1)} %get-tuple-element.34.acc_in, bf16[272,256]{1,0:T(8,128)(2,1)S(1)} %collective-permute-done.2.p2, bf16[272,256]{1,0:T(8,128)(2,1)S(1)} %collective-permute-done.3.p3), custom_call_target="tpu_custom_call" | custom-call | flops 2684354560 | tf_op jit(solution)/shard_map/pallas_call | solution.py:39
  31.2 3.0 %collective-permute-start.4 = (f32[1024,128]{1,0:T(8,128)S(1)}, f32[1024,128]{1,0:T(8,128)S(1)}, u32[]{:S(2)}, u32[]{:S(2)}) collective-permute-start(f32[1024,128]{1,0:T(8,128)S(1)} %get-tuple-element.37.refs_0_), channel_id=1, source_target_pairs={{0,64},{64,0},{1,65},{65,1},{2,66},{66,2},{3,67},{67,3},{4,68},{68... | collective-permute-start | bytes 1572872 | tf_op jit(solution)/shard_map/ppermute | solution.py:287
  35.7 3.0 %collective-permute-start.6 = (f32[256,128]{1,0:T(8,128)S(1)}, f32[256,128]{1,0:T(8,128)S(1)}, u32[]{:S(2)}, u32[]{:S(2)}) collective-permute-start(f32[256,128]{1,0:T(8,128)S(1)} %shard_map.91.refs_1_), channel_id=1, source_target_pairs={{0,4},{2,6},{4,0},{6,2},{1,5},{3,7},{5,1},{7,3},{8,12},{10,14},{12... | collective-permute-start | bytes 393224 | tf_op jit(solution)/shard_map/ppermute | solution.py:287
  39.8 2.2 %collective-permute-start.5 = (f32[256,128]{1,0:T(8,128)S(1)}, f32[256,128]{1,0:T(8,128)S(1)}, u32[]{:S(2)}, u32[]{:S(2)}) collective-permute-start(f32[256,128]{1,0:T(8,128)S(1)} %get-tuple-element.39.refs_1_), channel_id=1, source_target_pairs={{0,2},{2,0},{4,6},{6,4},{1,3},{3,1},{5,7},{7,5},{8,10},{10,8},{12,... | collective-permute-start | bytes 393224 | tf_op jit(solution)/shard_map/ppermute | solution.py:287
  43.0 3.8 %collective-permute-start.7 = (f32[256,128]{1,0:T(8,128)S(1)}, f32[256,128]{1,0:T(8,128)S(1)}, u32[]{:S(2)}, u32[]{:S(2)}) collective-permute-start(f32[256,128]{1,0:T(8,128)S(1)} %get-tuple-element.40.refs_1_), channel_id=1, source_target_pairs={{0,6},{2,4},{4,2},{6,0},{1,7},{3,5},{5,3},{7,1},{8,14},{10,12},{12... | collective-permute-start | bytes 393224 | tf_op jit(solution)/shard_map/ppermute | solution.py:287
  47.8 2.1 %collective-permute-done.7.d = f32[256,128]{1,0:T(8,128)S(1)} collective-permute-done((f32[256,128]{1,0:T(8,128)S(1)}, f32[256,128]{1,0:T(8,128)S(1)}, u32[]{:S(2)}, u32[]{:S(2)}) %collective-permute-start.7) | collective-permute-done | bytes 131104 | tf_op jit(solution)/shard_map/ppermute | solution.py:287
  49.9 24.7 %all_to_all.25.in_ref = f32[16,32,128]{2,1,0:T(8,128)S(1)} all-to-all(f32[16,32,128]{2,1,0:T(8,128)S(1)} %shard_map.95), channel_id=1, replica_groups=mesh['z2'=2,'z1'=2,'core'=2,'y4'=2,'y2'=2,'y1'=2,'x2'=2,'x1'=2,'zhi'=2] ..., dimensions={0} | all-to-all | bytes 524288 | tf_op jit(solution)/shard_map/all_to_all | solution.py:291
  74.6 14.3 %all_to_all.26 = bf16[32,32,128]{2,1,0:T(8,128)(2,1)S(1)} all-to-all(bf16[32,32,128]{2,1,0:T(8,128)(2,1)S(1)} %shard_map.96), channel_id=1, replica_groups=mesh['z2'=2,'z1'=2,'core'=2,'y4'=2,'y2'=2,'y1'=2,'x2'=2,'x1'=2,'zhi'=2] ..., dimensions={0} | all-to-all | bytes 524288 | tf_op jit(solution)/shard_map/all_to_all | solution.py:291
  88.9 5.9 %collective-permute-start.8 = (bf16[4,256,128]{2,1,0:T(8,128)(2,1)S(1)}, bf16[4,256,128]{2,1,0:T(8,128)(2,1)S(1)}, u32[]{:S(2)}, u32[]{:S(2)}) collective-permute-start(bf16[4,256,128]{2,1,0:T(8,128)(2,1)S(1)} %bitcast.4), channel_id=1, source_target_pairs={{0,64},{64,0},{1,65},{65,1},{2,66},{66,2},{3,67},{67,3},{4,68},{68... | collective-permute-start | bytes 786440 | tf_op jit(solution)/shard_map/ppermute | solution.py:287
  96.3 3.1 %collective-permute-start.9 = (f32[256,128]{1,0:T(8,128)S(1)}, f32[256,128]{1,0:T(8,128)S(1)}, u32[]{:S(2)}, u32[]{:S(2)}) collective-permute-start(f32[256,128]{1,0:T(8,128)S(1)} %get-tuple-element.49), channel_id=1, source_target_pairs={{0,256},{128,384},{256,0},{384,128},{1,257},{129,385},{257,1},{385... | collective-permute-start | bytes 393224 | tf_op jit(solution)/shard_map/ppermute | solution.py:287
  99.5 3.7 %collective-permute-start.10 = (f32[256,128]{1,0:T(8,128)S(1)}, f32[256,128]{1,0:T(8,128)S(1)}, u32[]{:S(2)}, u32[]{:S(2)}) collective-permute-start(f32[256,128]{1,0:T(8,128)S(1)} %get-tuple-element.50.after_ref), channel_id=1, source_target_pairs={{0,384},{128,256},{256,128},{384,0},{1,385},{129,257},{257,129},{3... | collective-permute-start | bytes 393224 | tf_op jit(solution)/shard_map/ppermute | solution.py:287
  103.7 2.1 %collective-permute-start.11 = (f32[256,128]{1,0:T(8,128)S(1)}, f32[256,128]{1,0:T(8,128)S(1)}, u32[]{:S(2)}, u32[]{:S(2)}) collective-permute-start(f32[256,128]{1,0:T(8,128)S(1)} %get-tuple-element.56), channel_id=1, source_target_pairs={{0,128},{128,0},{256,384},{384,256},{1,129},{129,1},{257,385},{385... | collective-permute-start | bytes 393224 | tf_op jit(solution)/shard_map/ppermute | solution.py:287
  105.8 3.7 %collective-permute-done.9.a = f32[256,128]{1,0:T(8,128)S(1)} collective-permute-done((f32[256,128]{1,0:T(8,128)S(1)}, f32[256,128]{1,0:T(8,128)S(1)}, u32[]{:S(2)}, u32[]{:S(2)}) %collective-permute-start.9) | collective-permute-done | bytes 131104 | tf_op jit(solution)/shard_map/ppermute | solution.py:287
  109.5 3.4 %collective-permute-done.11.near = f32[256,128]{1,0:T(8,128)S(1)} collective-permute-done((f32[256,128]{1,0:T(8,128)S(1)}, f32[256,128]{1,0:T(8,128)S(1)}, u32[]{:S(2)}, u32[]{:S(2)}) %collective-permute-start.11) | collective-permute-done | bytes 131104 | tf_op jit(solution)/shard_map/ppermute | solution.py:287
  113.6 13.4 %all_to_all.27.in_ref = f32[32,16,128]{2,1,0:T(8,128)S(1)} all-to-all(f32[32,16,128]{2,1,0:T(8,128)S(1)} %bitcast.7), channel_id=1, replica_groups=mesh['z2'=2,'z1'=2,'core'=2,'y4'=2,'y2'=2,'y1'=2,'x2'=2,'x1'=2,'zhi'=2] ..., dimensions={0} | all-to-all | bytes 524288 | tf_op jit(solution)/shard_map/all_to_all | solution.py:291
  127.0 16.0 %all_to_all.28.in_ref = f32[16,16,128]{2,1,0:T(8,128)S(1)} all-to-all(f32[16,16,128]{2,1,0:T(8,128)S(1)} %shard_map.102), channel_id=1, replica_groups=mesh['z2'=2,'z1'=2,'core'=2,'y4'=2,'y2'=2,'y1'=2,'x2'=2,'x1'=2,'zhi'=2] ..., dimensions={0} | all-to-all | bytes 262144 | tf_op jit(solution)/shard_map/all_to_all | solution.py:291
  143.1 14.8 %all_to_all.29 = f32[32,16,128]{2,1,0:T(8,128)S(1)} all-to-all(f32[32,16,128]{2,1,0:T(8,128)S(1)} %shard_map.103), channel_id=1, replica_groups=mesh['z2'=2,'z1'=2,'core'=2,'y4'=2,'y2'=2,'y1'=2,'x2'=2,'x1'=2,'zhi'=2] ..., dimensions={0} | all-to-all | bytes 524288 | tf_op jit(solution)/shard_map/all_to_all | solution.py:291
  157.9 7.7 %shard_map.104 = (f32[256,128]{1,0:T(8,128)}, f32[256,128]{1,0:T(8,128)}, f32[256,128]{1,0:T(8,128)}) custom-call(f32[512,128]{1,0:T(8,128)S(1)} %bitcast.6, f32[256,128]{1,0:T(8,128)S(1)} %get-tuple-element.58.applied_ref, f32[256,128]{1,0:T(8,128)S(1)} %copy-done, f32[256,128]{1,0:T(8,128)S(1)} %copy-done.1, f32[256,128]{1,0:T(8,128)S(1)} %copy-done.4), custom_call_target="tpu_custom_call" | custom-call | tf_op jit(solution)/shard_map/pallas_call | solution.py:39
  (37 shorter events, 12.4 us)
Async XLA Ops:
  0.6 19.9 %copy-start.5 = (bf16[1024,128]{1,0:T(8,128)(2,1)S(1)}, bf16[1024,128]{1,0:T(8,128)(2,1)}, u32[]{:S(2)}) copy-start(bf16[1024,128]{1,0:T(8,128)(2,1)} %samples_ref.1) | copy-start | bytes 786436
  0.6 22.3 %collective-permute-start = (bf16[1024,128]{1,0:T(8,128)(2,1)}, bf16[1024,128]{1,0:T(8,128)(2,1)S(1)}, u32[]{:S(2)}, u32[]{:S(2)}) collective-permute-start(bf16[1024,128]{1,0:T(8,128)(2,1)} %samples_ref.1), channel_id=1, source_target_pairs={{0,64},{64,0},{1,65},{65,1},{2,66},{66,2},{3,67},{67,3},{4,68},{68... | collective-permute-start | bytes 786440 | tf_op jit(solution)/shard_map/ppermute | solution.py:287
  11.3 17.3 %collective-permute-start.3 = (bf16[272,256]{1,0:T(8,128)(2,1)}, bf16[272,256]{1,0:T(8,128)(2,1)S(1)}, u32[]{:S(2)}, u32[]{:S(2)}) collective-permute-start(bf16[272,256]{1,0:T(8,128)(2,1)} %shard_map.85.pack_ref), channel_id=1, source_target_pairs={{0,384},{128,256},{256,128},{384,0},{1,385},{129,257},{257,129},{3... | collective-permute-start | bytes 417800 | tf_op jit(solution)/shard_map/ppermute | solution.py:287
  13.5 15.0 %collective-permute-start.2 = (bf16[272,256]{1,0:T(8,128)(2,1)}, bf16[272,256]{1,0:T(8,128)(2,1)S(1)}, u32[]{:S(2)}, u32[]{:S(2)}) collective-permute-start(bf16[272,256]{1,0:T(8,128)(2,1)} %shard_map.85.pack_ref), channel_id=1, source_target_pairs={{0,256},{128,384},{256,0},{384,128},{1,257},{129,385},{257,1},{385... | collective-permute-start | bytes 417800 | tf_op jit(solution)/shard_map/ppermute | solution.py:287
  15.4 11.7 %collective-permute-start.1 = (bf16[272,256]{1,0:T(8,128)(2,1)}, bf16[272,256]{1,0:T(8,128)(2,1)S(1)}, u32[]{:S(2)}, u32[]{:S(2)}) collective-permute-start(bf16[272,256]{1,0:T(8,128)(2,1)} %shard_map.85.pack_ref), channel_id=1, source_target_pairs={{0,128},{128,0},{256,384},{384,256},{1,129},{129,1},{257,385},{385... | collective-permute-start | bytes 417800 | tf_op jit(solution)/shard_map/ppermute | solution.py:287
  20.6 0.9 copy-start.2
  21.5 1.4 copy-start.3
  31.2 4.5 %collective-permute-start.4 = (f32[1024,128]{1,0:T(8,128)S(1)}, f32[1024,128]{1,0:T(8,128)S(1)}, u32[]{:S(2)}, u32[]{:S(2)}) collective-permute-start(f32[1024,128]{1,0:T(8,128)S(1)} %get-tuple-element.37.refs_0_), channel_id=1, source_target_pairs={{0,64},{64,0},{1,65},{65,1},{2,66},{66,2},{3,67},{67,3},{4,68},{68... | collective-permute-start | bytes 1572872 | tf_op jit(solution)/shard_map/ppermute | solution.py:287
  35.7 12.0 %collective-permute-start.6 = (f32[256,128]{1,0:T(8,128)S(1)}, f32[256,128]{1,0:T(8,128)S(1)}, u32[]{:S(2)}, u32[]{:S(2)}) collective-permute-start(f32[256,128]{1,0:T(8,128)S(1)} %shard_map.91.refs_1_), channel_id=1, source_target_pairs={{0,4},{2,6},{4,0},{6,2},{1,5},{3,7},{5,1},{7,3},{8,12},{10,14},{12... | collective-permute-start | bytes 393224 | tf_op jit(solution)/shard_map/ppermute | solution.py:287
  39.8 8.0 %collective-permute-start.5 = (f32[256,128]{1,0:T(8,128)S(1)}, f32[256,128]{1,0:T(8,128)S(1)}, u32[]{:S(2)}, u32[]{:S(2)}) collective-permute-start(f32[256,128]{1,0:T(8,128)S(1)} %get-tuple-element.39.refs_1_), channel_id=1, source_target_pairs={{0,2},{2,0},{4,6},{6,4},{1,3},{3,1},{5,7},{7,5},{8,10},{10,8},{12,... | collective-permute-start | bytes 393224 | tf_op jit(solution)/shard_map/ppermute | solution.py:287
  43.0 6.9 %collective-permute-start.7 = (f32[256,128]{1,0:T(8,128)S(1)}, f32[256,128]{1,0:T(8,128)S(1)}, u32[]{:S(2)}, u32[]{:S(2)}) collective-permute-start(f32[256,128]{1,0:T(8,128)S(1)} %get-tuple-element.40.refs_1_), channel_id=1, source_target_pairs={{0,6},{2,4},{4,2},{6,0},{1,7},{3,5},{5,3},{7,1},{8,14},{10,12},{12... | collective-permute-start | bytes 393224 | tf_op jit(solution)/shard_map/ppermute | solution.py:287
  88.9 7.0 %collective-permute-start.8 = (bf16[4,256,128]{2,1,0:T(8,128)(2,1)S(1)}, bf16[4,256,128]{2,1,0:T(8,128)(2,1)S(1)}, u32[]{:S(2)}, u32[]{:S(2)}) collective-permute-start(bf16[4,256,128]{2,1,0:T(8,128)(2,1)S(1)} %bitcast.4), channel_id=1, source_target_pairs={{0,64},{64,0},{1,65},{65,1},{2,66},{66,2},{3,67},{67,3},{4,68},{68... | collective-permute-start | bytes 786440 | tf_op jit(solution)/shard_map/ppermute | solution.py:287
  96.3 13.2 %collective-permute-start.9 = (f32[256,128]{1,0:T(8,128)S(1)}, f32[256,128]{1,0:T(8,128)S(1)}, u32[]{:S(2)}, u32[]{:S(2)}) collective-permute-start(f32[256,128]{1,0:T(8,128)S(1)} %get-tuple-element.49), channel_id=1, source_target_pairs={{0,256},{128,384},{256,0},{384,128},{1,257},{129,385},{257,1},{385... | collective-permute-start | bytes 393224 | tf_op jit(solution)/shard_map/ppermute | solution.py:287
  99.5 10.0 %collective-permute-start.10 = (f32[256,128]{1,0:T(8,128)S(1)}, f32[256,128]{1,0:T(8,128)S(1)}, u32[]{:S(2)}, u32[]{:S(2)}) collective-permute-start(f32[256,128]{1,0:T(8,128)S(1)} %get-tuple-element.50.after_ref), channel_id=1, source_target_pairs={{0,384},{128,256},{256,128},{384,0},{1,385},{129,257},{257,129},{3... | collective-permute-start | bytes 393224 | tf_op jit(solution)/shard_map/ppermute | solution.py:287
  103.7 9.3 %copy-start = (f32[256,128]{1,0:T(8,128)S(1)}, f32[256,128]{1,0:T(8,128)}, u32[]{:S(2)}) copy-start(f32[256,128]{1,0:T(8,128)} %dir_ref.3) | copy-start | bytes 393220
  103.7 9.2 %copy-start.1 = (f32[256,128]{1,0:T(8,128)S(1)}, f32[256,128]{1,0:T(8,128)}, u32[]{:S(2)}) copy-start(f32[256,128]{1,0:T(8,128)} %res_ref.3) | copy-start | bytes 393220
  103.7 9.2 %collective-permute-start.11 = (f32[256,128]{1,0:T(8,128)S(1)}, f32[256,128]{1,0:T(8,128)S(1)}, u32[]{:S(2)}, u32[]{:S(2)}) collective-permute-start(f32[256,128]{1,0:T(8,128)S(1)} %get-tuple-element.56), channel_id=1, source_target_pairs={{0,128},{128,0},{256,384},{384,256},{1,129},{129,1},{257,385},{385... | collective-permute-start | bytes 393224 | tf_op jit(solution)/shard_map/ppermute | solution.py:287
  143.0 14.8 %copy-start.4 = (f32[256,128]{1,0:T(8,128)S(1)}, f32[256,128]{1,0:T(8,128)}, u32[]{:S(2)}) copy-start(f32[256,128]{1,0:T(8,128)} %sol_ref.1) | copy-start | bytes 393220

commit v5 on v4

--- a/solution.py
+++ b/solution.py
@@ -18,7 +18,7 @@
 SCALE = math.sqrt(2.0 / FEATURES)
 ROUNDER = 12582912.0
 PACK = 272
-GRAM = 512
+GRAM = 384
 
 AXES = ("z2", "z1", "core", "y4", "y2", "y1", "x2", "x1", "zhi")
 DP = ("z2", "z1", "core")
@@ -191,6 +191,11 @@
     return 0.5 * (m + m.T)
 
 
+def places():
+    n = 128
+    return lax.broadcasted_iota(jnp.int32, (n, n), 0), lax.broadcasted_iota(jnp.int32, (n, n), 1)
+
+
 def two_sum(a, b, out_ref):
     out_ref[...] = a[...] + b[...]
 
@@ -200,14 +205,16 @@
     applied = total + penalty * dir_ref[...]
     applied_ref[...] = applied
     applied_t = applied.T
-    grams = (
-        fdot(applied_t, dir_ref[...]),
-        fdot(applied_t, res_ref[...]),
-        fdot(applied_t, applied),
-        fdot(res_ref[...].T, res_ref[...]),
-    )
-    for i, g in enumerate(grams):
-        gram_ref[128 * i : 128 * i + 128, :] = g
+    dir_gram = sym(fdot(applied_t, dir_ref[...]))
+    applied_gram = fdot(applied_t, applied)
+    res_gram = sym(fdot(res_ref[...].T, res_ref[...]))
+    at_row, at_col = places()
+    diag = jnp.sum(jnp.where(at_row == at_col, applied_gram, 0.0), axis=1, keepdims=True)
+    gram_ref[0:128, :] = jnp.where(at_col >= at_row, dir_gram, applied_gram)
+    gram_ref[128:256, :] = fdot(applied_t, res_ref[...])
+    gram_ref[256:384, :] = jnp.where(
+        at_col >= at_row, res_gram, jnp.where(at_col == 0, diag, diag[0:1, 0:1])
+    )
 
 
 def inverse_factors(mats):
@@ -266,10 +273,13 @@
 
 
 def final_kernel(gram_ref, applied_ref, dir_ref, res_ref, sol_ref, sol_out, res_out, dir_out):
-    dir_gram = sym(gram_ref[0:128, :])
-    cross = gram_ref[128:256, :]
-    applied_gram = gram_ref[256:384, :]
-    res_gram = sym(gram_ref[384:512, :])
+    at_row, at_col = places()
+    first, cross, third = (gram_ref[128 * i : 128 * i + 128, :] for i in range(3))
+    first_t, third_t = first.T, third.T
+    dir_gram = jnp.where(at_col >= at_row, first, first_t)
+    res_gram = jnp.where(at_col >= at_row, third, third_t)
+    diag = jnp.where(at_row == 0, third[127:128, 1:2], third[:, 0:1])
+    applied_gram = jnp.where(at_col < at_row, first, jnp.where(at_col == at_row, diag, first_t))
     (m_d, n_d), (m_r, n_r) = inverse_factors([dir_gram, res_gram])
     step = fdot(m_d.T, fdot(n_d, res_gram))
     step_t = step.T
@@ -381,11 +391,11 @@
     applied, gram = call(
         gram_kernel, [struct((256, 128)), struct((GRAM, 128))], far_sum, parts[0], received[0], direction, residual
     )
-    plane, column = RING_X + RING_Y, RING_Z + ("core",)
-    chunk = GRAM // 32
-    piece = exchange(gram.reshape(32, chunk, 128), plane)
-    piece = exchange(call(sum_copies_kernel, struct((16, chunk, 128)), piece), column)
-    piece = exchange(call(sum_copies_kernel, struct((32, chunk, 128)), piece), plane)
+    near, far = RING_X + ("core", "y1"), ("y4", "y2") + RING_Z
+    chunk = GRAM // 16
+    piece = exchange(gram.reshape(16, chunk, 128), near)
+    piece = exchange(call(sum_copies_kernel, struct((32, chunk, 128)), piece), far)
+    piece = exchange(call(sum_copies_kernel, struct((16, chunk, 128)), piece), near)
     return call(
         final_kernel,
         [struct((256, 128))] * 3,

time: 167 us -> 164 us (0.982)
  blocking collectives: 83.2 us -> 80.4 us
    all_to_all x5, blocking collectives: 83.2 us -> 80.4 us  [exchange(): return lax.all_to_all(value, axes, 0, 0)]
where the time goes in v5:
time: 164 us; the launch traced here: 163 us
  blocking collectives  80.4 us (49%)
  starting transfers between devices  45 us (27%)
  Pallas kernels  22.5 us (14%)
  waiting for transfers between devices  13 us (8%)
    all_to_all x5, blocking collectives, exchange(): return lax.all_to_all(value, axes, 0, 0)  80.4 us
    ppermute x12, starting transfers between devices, swap(): return lax.ppermute(value, axes, [(i, i ^ s) for i in range(n)])  45 us
    pallas_call x19, Pallas kernels, call(): pl.pallas_call(kernel, out_shape=outs, in_specs=specs, out_specs=jax.tree...  20.8 us
    ppermute x12, waiting for transfers between devices, swap(): return lax.ppermute(value, axes, [(i, i ^ s) for i in range(n)])  13 us
  transfers between devices with their start and end apart: 12, of which 6 were waited for; matrix products, arithmetic and copies ran while one was open for 0% of the time, Pallas kernels for 7%

profile of v5, /device:TPU:1, one launch (start us, length us, event | category | flops | bytes accessed | tf_op | source)
XLA Modules:
  0.0 162.9 jit_solution(7320934197136108166)
XLA Ops:
  0.6 8.9 %collective-permute-start = (bf16[1024,128]{1,0:T(8,128)(2,1)}, bf16[1024,128]{1,0:T(8,128)(2,1)S(1)}, u32[]{:S(2)}, u32[]{:S(2)}) collective-permute-start(bf16[1024,128]{1,0:T(8,128)(2,1)} %samples_ref.1), channel_id=1, source_target_pairs={{0,64},{64,0},{1,65},{65,1},{2,66},{66,2},{3,67},{67,3},{4,68},{68... | collective-permute-start | bytes 786440 | tf_op jit(solution)/shard_map/ppermute | solution.py:297
  9.6 1.7 %shard_map.85.pack_ref = bf16[272,256]{1,0:T(8,128)(2,1)} custom-call(bf16[128,256]{1,0:T(8,128)(2,1)} %proj_in.1, bf16[1,256]{1,0:T(2,128)(2,1)} %shift_in.1, f32[256,128]{1,0:T(8,128)} %dir_ref.3), custom_call_target="tpu_custom_call" | custom-call | tf_op jit(solution)/shard_map/pallas_call | solution.py:307
  11.3 2.2 %collective-permute-start.3 = (bf16[272,256]{1,0:T(8,128)(2,1)}, bf16[272,256]{1,0:T(8,128)(2,1)S(1)}, u32[]{:S(2)}, u32[]{:S(2)}) collective-permute-start(bf16[272,256]{1,0:T(8,128)(2,1)} %shard_map.85.pack_ref), channel_id=1, source_target_pairs={{0,384},{128,256},{256,128},{384,0},{1,385},{129,257},{257,129},{3... | collective-permute-start | bytes 417800 | tf_op jit(solution)/shard_map/ppermute | solution.py:297
  13.5 1.9 %collective-permute-start.2 = (bf16[272,256]{1,0:T(8,128)(2,1)}, bf16[272,256]{1,0:T(8,128)(2,1)S(1)}, u32[]{:S(2)}, u32[]{:S(2)}) collective-permute-start(bf16[272,256]{1,0:T(8,128)(2,1)} %shard_map.85.pack_ref), channel_id=1, source_target_pairs={{0,256},{128,384},{256,0},{384,128},{1,257},{129,385},{257,1},{385... | collective-permute-start | bytes 417800 | tf_op jit(solution)/shard_map/ppermute | solution.py:297
  15.4 5.1 %collective-permute-start.1 = (bf16[272,256]{1,0:T(8,128)(2,1)}, bf16[272,256]{1,0:T(8,128)(2,1)S(1)}, u32[]{:S(2)}, u32[]{:S(2)}) collective-permute-start(bf16[272,256]{1,0:T(8,128)(2,1)} %shard_map.85.pack_ref), channel_id=1, source_target_pairs={{0,128},{128,0},{256,384},{384,256},{1,129},{129,1},{257,385},{385... | collective-permute-start | bytes 417800 | tf_op jit(solution)/shard_map/ppermute | solution.py:297
  24.3 2.8 %collective-permute-done.1.p1 = bf16[272,256]{1,0:T(8,128)(2,1)S(1)} collective-permute-done((bf16[272,256]{1,0:T(8,128)(2,1)}, bf16[272,256]{1,0:T(8,128)(2,1)S(1)}, u32[]{:S(2)}, u32[]{:S(2)}) %collective-permute-start.1) | collective-permute-done | bytes 139296 | tf_op jit(solution)/shard_map/ppermute | solution.py:297
  28.5 2.6 %shard_map.89 = (bf16[2,256,1024]{2,1,0:T(8,128)(2,1)S(1)}, f32[1024,128]{1,0:T(8,128)S(1)}) custom-call(bf16[128,1024]{1,0:T(8,128)(2,1)S(1)} %get-tuple-element.31.rows_t, f32[128,1024]{1,0:T(8,128)S(1)} %get-tuple-element.34.acc_in, bf16[272,256]{1,0:T(8,128)(2,1)S(1)} %collective-permute-done.2.p2, bf16[272,256]{1,0:T(8,128)(2,1)S(1)} %collective-permute-done.3.p3), custom_call_target="tpu_custom_call" | custom-call | flops 2684354560 | tf_op jit(solution)/shard_map/pallas_call | solution.py:39
  31.2 3.0 %collective-permute-start.4 = (f32[1024,128]{1,0:T(8,128)S(1)}, f32[1024,128]{1,0:T(8,128)S(1)}, u32[]{:S(2)}, u32[]{:S(2)}) collective-permute-start(f32[1024,128]{1,0:T(8,128)S(1)} %get-tuple-element.37.refs_0_), channel_id=1, source_target_pairs={{0,64},{64,0},{1,65},{65,1},{2,66},{66,2},{3,67},{67,3},{4,68},{68... | collective-permute-start | bytes 1572872 | tf_op jit(solution)/shard_map/ppermute | solution.py:297
  35.7 3.0 %collective-permute-start.6 = (f32[256,128]{1,0:T(8,128)S(1)}, f32[256,128]{1,0:T(8,128)S(1)}, u32[]{:S(2)}, u32[]{:S(2)}) collective-permute-start(f32[256,128]{1,0:T(8,128)S(1)} %shard_map.91.refs_1_), channel_id=1, source_target_pairs={{0,4},{2,6},{4,0},{6,2},{1,5},{3,7},{5,1},{7,3},{8,12},{10,14},{12... | collective-permute-start | bytes 393224 | tf_op jit(solution)/shard_map/ppermute | solution.py:297
  39.8 2.2 %collective-permute-start.5 = (f32[256,128]{1,0:T(8,128)S(1)}, f32[256,128]{1,0:T(8,128)S(1)}, u32[]{:S(2)}, u32[]{:S(2)}) collective-permute-start(f32[256,128]{1,0:T(8,128)S(1)} %get-tuple-element.39.refs_1_), channel_id=1, source_target_pairs={{0,2},{2,0},{4,6},{6,4},{1,3},{3,1},{5,7},{7,5},{8,10},{10,8},{12,... | collective-permute-start | bytes 393224 | tf_op jit(solution)/shard_map/ppermute | solution.py:297
  43.0 3.8 %collective-permute-start.7 = (f32[256,128]{1,0:T(8,128)S(1)}, f32[256,128]{1,0:T(8,128)S(1)}, u32[]{:S(2)}, u32[]{:S(2)}) collective-permute-start(f32[256,128]{1,0:T(8,128)S(1)} %get-tuple-element.40.refs_1_), channel_id=1, source_target_pairs={{0,6},{2,4},{4,2},{6,0},{1,7},{3,5},{5,3},{7,1},{8,14},{10,12},{12... | collective-permute-start | bytes 393224 | tf_op jit(solution)/shard_map/ppermute | solution.py:297
  47.8 2.1 %collective-permute-done.7.d = f32[256,128]{1,0:T(8,128)S(1)} collective-permute-done((f32[256,128]{1,0:T(8,128)S(1)}, f32[256,128]{1,0:T(8,128)S(1)}, u32[]{:S(2)}, u32[]{:S(2)}) %collective-permute-start.7) | collective-permute-done | bytes 131104 | tf_op jit(solution)/shard_map/ppermute | solution.py:297
  49.9 24.7 %all_to_all.25.in_ref = f32[16,32,128]{2,1,0:T(8,128)S(1)} all-to-all(f32[16,32,128]{2,1,0:T(8,128)S(1)} %shard_map.95), channel_id=1, replica_groups=mesh['z2'=2,'z1'=2,'core'=2,'y4'=2,'y2'=2,'y1'=2,'x2'=2,'x1'=2,'zhi'=2] ..., dimensions={0} | all-to-all | bytes 524288 | tf_op jit(solution)/shard_map/all_to_all | solution.py:301
  74.6 14.3 %all_to_all.26 = bf16[32,32,128]{2,1,0:T(8,128)(2,1)S(1)} all-to-all(bf16[32,32,128]{2,1,0:T(8,128)(2,1)S(1)} %shard_map.96), channel_id=1, replica_groups=mesh['z2'=2,'z1'=2,'core'=2,'y4'=2,'y2'=2,'y1'=2,'x2'=2,'x1'=2,'zhi'=2] ..., dimensions={0} | all-to-all | bytes 524288 | tf_op jit(solution)/shard_map/all_to_all | solution.py:301
  88.9 5.9 %collective-permute-start.8 = (bf16[4,256,128]{2,1,0:T(8,128)(2,1)S(1)}, bf16[4,256,128]{2,1,0:T(8,128)(2,1)S(1)}, u32[]{:S(2)}, u32[]{:S(2)}) collective-permute-start(bf16[4,256,128]{2,1,0:T(8,128)(2,1)S(1)} %bitcast.4), channel_id=1, source_target_pairs={{0,64},{64,0},{1,65},{65,1},{2,66},{66,2},{3,67},{67,3},{4,68},{68... | collective-permute-start | bytes 786440 | tf_op jit(solution)/shard_map/ppermute | solution.py:297
  96.3 3.1 %collective-permute-start.9 = (f32[256,128]{1,0:T(8,128)S(1)}, f32[256,128]{1,0:T(8,128)S(1)}, u32[]{:S(2)}, u32[]{:S(2)}) collective-permute-start(f32[256,128]{1,0:T(8,128)S(1)} %get-tuple-element.49), channel_id=1, source_target_pairs={{0,256},{128,384},{256,0},{384,128},{1,257},{129,385},{257,1},{385... | collective-permute-start | bytes 393224 | tf_op jit(solution)/shard_map/ppermute | solution.py:297
  99.5 3.7 %collective-permute-start.10 = (f32[256,128]{1,0:T(8,128)S(1)}, f32[256,128]{1,0:T(8,128)S(1)}, u32[]{:S(2)}, u32[]{:S(2)}) collective-permute-start(f32[256,128]{1,0:T(8,128)S(1)} %get-tuple-element.50.after_ref), channel_id=1, source_target_pairs={{0,384},{128,256},{256,128},{384,0},{1,385},{129,257},{257,129},{3... | collective-permute-start | bytes 393224 | tf_op jit(solution)/shard_map/ppermute | solution.py:297
  103.7 2.1 %collective-permute-start.11 = (f32[256,128]{1,0:T(8,128)S(1)}, f32[256,128]{1,0:T(8,128)S(1)}, u32[]{:S(2)}, u32[]{:S(2)}) collective-permute-start(f32[256,128]{1,0:T(8,128)S(1)} %get-tuple-element.56), channel_id=1, source_target_pairs={{0,128},{128,0},{256,384},{384,256},{1,129},{129,1},{257,385},{385... | collective-permute-start | bytes 393224 | tf_op jit(solution)/shard_map/ppermute | solution.py:297
  105.8 3.7 %collective-permute-done.9.a = f32[256,128]{1,0:T(8,128)S(1)} collective-permute-done((f32[256,128]{1,0:T(8,128)S(1)}, f32[256,128]{1,0:T(8,128)S(1)}, u32[]{:S(2)}, u32[]{:S(2)}) %collective-permute-start.9) | collective-permute-done | bytes 131104 | tf_op jit(solution)/shard_map/ppermute | solution.py:297
  109.5 3.4 %collective-permute-done.11.near = f32[256,128]{1,0:T(8,128)S(1)} collective-permute-done((f32[256,128]{1,0:T(8,128)S(1)}, f32[256,128]{1,0:T(8,128)S(1)}, u32[]{:S(2)}, u32[]{:S(2)}) %collective-permute-start.11) | collective-permute-done | bytes 131104 | tf_op jit(solution)/shard_map/ppermute | solution.py:297
  113.6 10.7 %all_to_all.27.in_ref = f32[16,24,128]{2,1,0:T(8,128)S(1)} all-to-all(f32[16,24,128]{2,1,0:T(8,128)S(1)} %bitcast.7), channel_id=1, replica_groups=mesh['z2'=2,'z1'=2,'core'=2,'y4'=2,'y2'=2,'y1'=2,'x2'=2,'x1'=2,'zhi'=2] ..., dimensions={0} | all-to-all | bytes 393216 | tf_op jit(solution)/shard_map/all_to_all | solution.py:301
  124.4 18.1 %all_to_all.28.in_ref = f32[32,24,128]{2,1,0:T(8,128)S(1)} all-to-all(f32[32,24,128]{2,1,0:T(8,128)S(1)} %shard_map.102), channel_id=1, replica_groups=mesh['z2'=2,'z1'=2,'core'=2,'y4'=2,'y2'=2,'y1'=2,'x2'=2,'x1'=2,'zhi'=2] ..., dimensions={0} | all-to-all | bytes 786432 | tf_op jit(solution)/shard_map/all_to_all | solution.py:301
  142.5 12.7 %all_to_all.29 = f32[16,24,128]{2,1,0:T(8,128)S(1)} all-to-all(f32[16,24,128]{2,1,0:T(8,128)S(1)} %shard_map.103), channel_id=1, replica_groups=mesh['z2'=2,'z1'=2,'core'=2,'y4'=2,'y2'=2,'y1'=2,'x2'=2,'x1'=2,'zhi'=2] ..., dimensions={0} | all-to-all | bytes 393216 | tf_op jit(solution)/shard_map/all_to_all | solution.py:301
  155.1 7.7 %shard_map.104 = (f32[256,128]{1,0:T(8,128)}, f32[256,128]{1,0:T(8,128)}, f32[256,128]{1,0:T(8,128)}) custom-call(f32[384,128]{1,0:T(8,128)S(1)} %bitcast.6, f32[256,128]{1,0:T(8,128)S(1)} %get-tuple-element.58.applied_ref, f32[256,128]{1,0:T(8,128)S(1)} %copy-done, f32[256,128]{1,0:T(8,128)S(1)} %copy-done.1, f32[256,128]{1,0:T(8,128)S(1)} %copy-done.4), custom_call_target="tpu_custom_call" | custom-call | tf_op jit(solution)/shard_map/pallas_call | solution.py:39
  (37 shorter events, 12.4 us)
Async XLA Ops:
  0.6 19.9 %copy-start.5 = (bf16[1024,128]{1,0:T(8,128)(2,1)S(1)}, bf16[1024,128]{1,0:T(8,128)(2,1)}, u32[]{:S(2)}) copy-start(bf16[1024,128]{1,0:T(8,128)(2,1)} %samples_ref.1) | copy-start | bytes 786436
  0.6 22.3 %collective-permute-start = (bf16[1024,128]{1,0:T(8,128)(2,1)}, bf16[1024,128]{1,0:T(8,128)(2,1)S(1)}, u32[]{:S(2)}, u32[]{:S(2)}) collective-permute-start(bf16[1024,128]{1,0:T(8,128)(2,1)} %samples_ref.1), channel_id=1, source_target_pairs={{0,64},{64,0},{1,65},{65,1},{2,66},{66,2},{3,67},{67,3},{4,68},{68... | collective-permute-start | bytes 786440 | tf_op jit(solution)/shard_map/ppermute | solution.py:297
  11.3 17.3 %collective-permute-start.3 = (bf16[272,256]{1,0:T(8,128)(2,1)}, bf16[272,256]{1,0:T(8,128)(2,1)S(1)}, u32[]{:S(2)}, u32[]{:S(2)}) collective-permute-start(bf16[272,256]{1,0:T(8,128)(2,1)} %shard_map.85.pack_ref), channel_id=1, source_target_pairs={{0,384},{128,256},{256,128},{384,0},{1,385},{129,257},{257,129},{3... | collective-permute-start | bytes 417800 | tf_op jit(solution)/shard_map/ppermute | solution.py:297
  13.5 15.0 %collective-permute-start.2 = (bf16[272,256]{1,0:T(8,128)(2,1)}, bf16[272,256]{1,0:T(8,128)(2,1)S(1)}, u32[]{:S(2)}, u32[]{:S(2)}) collective-permute-start(bf16[272,256]{1,0:T(8,128)(2,1)} %shard_map.85.pack_ref), channel_id=1, source_target_pairs={{0,256},{128,384},{256,0},{384,128},{1,257},{129,385},{257,1},{385... | collective-permute-start | bytes 417800 | tf_op jit(solution)/shard_map/ppermute | solution.py:297
  15.4 11.7 %collective-permute-start.1 = (bf16[272,256]{1,0:T(8,128)(2,1)}, bf16[272,256]{1,0:T(8,128)(2,1)S(1)}, u32[]{:S(2)}, u32[]{:S(2)}) collective-permute-start(bf16[272,256]{1,0:T(8,128)(2,1)} %shard_map.85.pack_ref), channel_id=1, source_target_pairs={{0,128},{128,0},{256,384},{384,256},{1,129},{129,1},{257,385},{385... | collective-permute-start | bytes 417800 | tf_op jit(solution)/shard_map/ppermute | solution.py:297
  20.6 0.9 copy-start.2
  21.5 1.4 copy-start.3
  31.2 4.5 %collective-permute-start.4 = (f32[1024,128]{1,0:T(8,128)S(1)}, f32[1024,128]{1,0:T(8,128)S(1)}, u32[]{:S(2)}, u32[]{:S(2)}) collective-permute-start(f32[1024,128]{1,0:T(8,128)S(1)} %get-tuple-element.37.refs_0_), channel_id=1, source_target_pairs={{0,64},{64,0},{1,65},{65,1},{2,66},{66,2},{3,67},{67,3},{4,68},{68... | collective-permute-start | bytes 1572872 | tf_op jit(solution)/shard_map/ppermute | solution.py:297
  35.7 12.0 %collective-permute-start.6 = (f32[256,128]{1,0:T(8,128)S(1)}, f32[256,128]{1,0:T(8,128)S(1)}, u32[]{:S(2)}, u32[]{:S(2)}) collective-permute-start(f32[256,128]{1,0:T(8,128)S(1)} %shard_map.91.refs_1_), channel_id=1, source_target_pairs={{0,4},{2,6},{4,0},{6,2},{1,5},{3,7},{5,1},{7,3},{8,12},{10,14},{12... | collective-permute-start | bytes 393224 | tf_op jit(solution)/shard_map/ppermute | solution.py:297
  39.8 8.0 %collective-permute-start.5 = (f32[256,128]{1,0:T(8,128)S(1)}, f32[256,128]{1,0:T(8,128)S(1)}, u32[]{:S(2)}, u32[]{:S(2)}) collective-permute-start(f32[256,128]{1,0:T(8,128)S(1)} %get-tuple-element.39.refs_1_), channel_id=1, source_target_pairs={{0,2},{2,0},{4,6},{6,4},{1,3},{3,1},{5,7},{7,5},{8,10},{10,8},{12,... | collective-permute-start | bytes 393224 | tf_op jit(solution)/shard_map/ppermute | solution.py:297
  43.0 6.9 %collective-permute-start.7 = (f32[256,128]{1,0:T(8,128)S(1)}, f32[256,128]{1,0:T(8,128)S(1)}, u32[]{:S(2)}, u32[]{:S(2)}) collective-permute-start(f32[256,128]{1,0:T(8,128)S(1)} %get-tuple-element.40.refs_1_), channel_id=1, source_target_pairs={{0,6},{2,4},{4,2},{6,0},{1,7},{3,5},{5,3},{7,1},{8,14},{10,12},{12... | collective-permute-start | bytes 393224 | tf_op jit(solution)/shard_map/ppermute | solution.py:297
  88.9 7.0 %collective-permute-start.8 = (bf16[4,256,128]{2,1,0:T(8,128)(2,1)S(1)}, bf16[4,256,128]{2,1,0:T(8,128)(2,1)S(1)}, u32[]{:S(2)}, u32[]{:S(2)}) collective-permute-start(bf16[4,256,128]{2,1,0:T(8,128)(2,1)S(1)} %bitcast.4), channel_id=1, source_target_pairs={{0,64},{64,0},{1,65},{65,1},{2,66},{66,2},{3,67},{67,3},{4,68},{68... | collective-permute-start | bytes 786440 | tf_op jit(solution)/shard_map/ppermute | solution.py:297
  96.3 13.2 %collective-permute-start.9 = (f32[256,128]{1,0:T(8,128)S(1)}, f32[256,128]{1,0:T(8,128)S(1)}, u32[]{:S(2)}, u32[]{:S(2)}) collective-permute-start(f32[256,128]{1,0:T(8,128)S(1)} %get-tuple-element.49), channel_id=1, source_target_pairs={{0,256},{128,384},{256,0},{384,128},{1,257},{129,385},{257,1},{385... | collective-permute-start | bytes 393224 | tf_op jit(solution)/shard_map/ppermute | solution.py:297
  99.5 10.0 %collective-permute-start.10 = (f32[256,128]{1,0:T(8,128)S(1)}, f32[256,128]{1,0:T(8,128)S(1)}, u32[]{:S(2)}, u32[]{:S(2)}) collective-permute-start(f32[256,128]{1,0:T(8,128)S(1)} %get-tuple-element.50.after_ref), channel_id=1, source_target_pairs={{0,384},{128,256},{256,128},{384,0},{1,385},{129,257},{257,129},{3... | collective-permute-start | bytes 393224 | tf_op jit(solution)/shard_map/ppermute | solution.py:297
  103.7 9.3 %copy-start = (f32[256,128]{1,0:T(8,128)S(1)}, f32[256,128]{1,0:T(8,128)}, u32[]{:S(2)}) copy-start(f32[256,128]{1,0:T(8,128)} %dir_ref.3) | copy-start | bytes 393220
  103.7 9.2 %copy-start.1 = (f32[256,128]{1,0:T(8,128)S(1)}, f32[256,128]{1,0:T(8,128)}, u32[]{:S(2)}) copy-start(f32[256,128]{1,0:T(8,128)} %res_ref.3) | copy-start | bytes 393220
  103.7 9.2 %collective-permute-start.11 = (f32[256,128]{1,0:T(8,128)S(1)}, f32[256,128]{1,0:T(8,128)S(1)}, u32[]{:S(2)}, u32[]{:S(2)}) collective-permute-start(f32[256,128]{1,0:T(8,128)S(1)} %get-tuple-element.56), channel_id=1, source_target_pairs={{0,128},{128,0},{256,384},{384,256},{1,129},{129,1},{257,385},{385... | collective-permute-start | bytes 393224 | tf_op jit(solution)/shard_map/ppermute | solution.py:297
  142.5 12.7 %copy-start.4 = (f32[256,128]{1,0:T(8,128)S(1)}, f32[256,128]{1,0:T(8,128)}, u32[]{:S(2)}) copy-start(f32[256,128]{1,0:T(8,128)} %sol_ref.1) | copy-start | bytes 393220

commit v6 on v4

--- a/solution.py
+++ b/solution.py
@@ -381,7 +381,7 @@
     applied, gram = call(
         gram_kernel, [struct((256, 128)), struct((GRAM, 128))], far_sum, parts[0], received[0], direction, residual
     )
-    plane, column = RING_X + RING_Y, RING_Z + ("core",)
+    plane, column = RING_X + ("core", "y1", "z1"), ("y4", "y2", "zhi", "z2")
     chunk = GRAM // 32
     piece = exchange(gram.reshape(32, chunk, 128), plane)
     piece = exchange(call(sum_copies_kernel, struct((16, chunk, 128)), piece), column)

time: 167 us -> 163 us (0.976)
  blocking collectives: 83.2 us -> 79.4 us
    all_to_all x5, blocking collectives: 83.2 us -> 79.4 us  [exchange(): return lax.all_to_all(value, axes, 0, 0)]
where the time goes in v6:
time: 163 us; the launch traced here: 162 us
  blocking collectives  79.4 us (49%)
  starting transfers between devices  45 us (28%)
  Pallas kernels  22.5 us (14%)
  waiting for transfers between devices  13 us (8%)
    all_to_all x5, blocking collectives, exchange(): return lax.all_to_all(value, axes, 0, 0)  79.4 us
    ppermute x12, starting transfers between devices, swap(): return lax.ppermute(value, axes, [(i, i ^ s) for i in range(n)])  45 us
    pallas_call x19, Pallas kernels, call(): pl.pallas_call(kernel, out_shape=outs, in_specs=specs, out_specs=jax.tree...  20.8 us
    ppermute x12, waiting for transfers between devices, swap(): return lax.ppermute(value, axes, [(i, i ^ s) for i in range(n)])  13 us
  transfers between devices with their start and end apart: 12, of which 6 were waited for; matrix products, arithmetic and copies ran while one was open for 0% of the time, Pallas kernels for 7%

profile of v6, /device:TPU:1, one launch (start us, length us, event | category | flops | bytes accessed | tf_op | source)
XLA Modules:
  0.0 161.9 jit_solution(8517380297303736157)
XLA Ops:
  0.6 8.9 %collective-permute-start = (bf16[1024,128]{1,0:T(8,128)(2,1)}, bf16[1024,128]{1,0:T(8,128)(2,1)S(1)}, u32[]{:S(2)}, u32[]{:S(2)}) collective-permute-start(bf16[1024,128]{1,0:T(8,128)(2,1)} %samples_ref.1), channel_id=1, source_target_pairs={{0,64},{64,0},{1,65},{65,1},{2,66},{66,2},{3,67},{67,3},{4,68},{68... | collective-permute-start | bytes 786440 | tf_op jit(solution)/shard_map/ppermute | solution.py:287
  9.6 1.7 %shard_map.85.pack_ref = bf16[272,256]{1,0:T(8,128)(2,1)} custom-call(bf16[128,256]{1,0:T(8,128)(2,1)} %proj_in.1, bf16[1,256]{1,0:T(2,128)(2,1)} %shift_in.1, f32[256,128]{1,0:T(8,128)} %dir_ref.3), custom_call_target="tpu_custom_call" | custom-call | tf_op jit(solution)/shard_map/pallas_call | solution.py:297
  11.3 2.2 %collective-permute-start.3 = (bf16[272,256]{1,0:T(8,128)(2,1)}, bf16[272,256]{1,0:T(8,128)(2,1)S(1)}, u32[]{:S(2)}, u32[]{:S(2)}) collective-permute-start(bf16[272,256]{1,0:T(8,128)(2,1)} %shard_map.85.pack_ref), channel_id=1, source_target_pairs={{0,384},{128,256},{256,128},{384,0},{1,385},{129,257},{257,129},{3... | collective-permute-start | bytes 417800 | tf_op jit(solution)/shard_map/ppermute | solution.py:287
  13.5 1.9 %collective-permute-start.2 = (bf16[272,256]{1,0:T(8,128)(2,1)}, bf16[272,256]{1,0:T(8,128)(2,1)S(1)}, u32[]{:S(2)}, u32[]{:S(2)}) collective-permute-start(bf16[272,256]{1,0:T(8,128)(2,1)} %shard_map.85.pack_ref), channel_id=1, source_target_pairs={{0,256},{128,384},{256,0},{384,128},{1,257},{129,385},{257,1},{385... | collective-permute-start | bytes 417800 | tf_op jit(solution)/shard_map/ppermute | solution.py:287
  15.4 5.1 %collective-permute-start.1 = (bf16[272,256]{1,0:T(8,128)(2,1)}, bf16[272,256]{1,0:T(8,128)(2,1)S(1)}, u32[]{:S(2)}, u32[]{:S(2)}) collective-permute-start(bf16[272,256]{1,0:T(8,128)(2,1)} %shard_map.85.pack_ref), channel_id=1, source_target_pairs={{0,128},{128,0},{256,384},{384,256},{1,129},{129,1},{257,385},{385... | collective-permute-start | bytes 417800 | tf_op jit(solution)/shard_map/ppermute | solution.py:287
  24.3 2.8 %collective-permute-done.1.p1 = bf16[272,256]{1,0:T(8,128)(2,1)S(1)} collective-permute-done((bf16[272,256]{1,0:T(8,128)(2,1)}, bf16[272,256]{1,0:T(8,128)(2,1)S(1)}, u32[]{:S(2)}, u32[]{:S(2)}) %collective-permute-start.1) | collective-permute-done | bytes 139296 | tf_op jit(solution)/shard_map/ppermute | solution.py:287
  28.5 2.6 %shard_map.89 = (bf16[2,256,1024]{2,1,0:T(8,128)(2,1)S(1)}, f32[1024,128]{1,0:T(8,128)S(1)}) custom-call(bf16[128,1024]{1,0:T(8,128)(2,1)S(1)} %get-tuple-element.31.rows_t, f32[128,1024]{1,0:T(8,128)S(1)} %get-tuple-element.34.acc_in, bf16[272,256]{1,0:T(8,128)(2,1)S(1)} %collective-permute-done.2.p2, bf16[272,256]{1,0:T(8,128)(2,1)S(1)} %collective-permute-done.3.p3), custom_call_target="tpu_custom_call" | custom-call | flops 2684354560 | tf_op jit(solution)/shard_map/pallas_call | solution.py:39
  31.2 3.0 %collective-permute-start.4 = (f32[1024,128]{1,0:T(8,128)S(1)}, f32[1024,128]{1,0:T(8,128)S(1)}, u32[]{:S(2)}, u32[]{:S(2)}) collective-permute-start(f32[1024,128]{1,0:T(8,128)S(1)} %get-tuple-element.37.refs_0_), channel_id=1, source_target_pairs={{0,64},{64,0},{1,65},{65,1},{2,66},{66,2},{3,67},{67,3},{4,68},{68... | collective-permute-start | bytes 1572872 | tf_op jit(solution)/shard_map/ppermute | solution.py:287
  35.7 3.0 %collective-permute-start.6 = (f32[256,128]{1,0:T(8,128)S(1)}, f32[256,128]{1,0:T(8,128)S(1)}, u32[]{:S(2)}, u32[]{:S(2)}) collective-permute-start(f32[256,128]{1,0:T(8,128)S(1)} %shard_map.91.refs_1_), channel_id=1, source_target_pairs={{0,4},{2,6},{4,0},{6,2},{1,5},{3,7},{5,1},{7,3},{8,12},{10,14},{12... | collective-permute-start | bytes 393224 | tf_op jit(solution)/shard_map/ppermute | solution.py:287
  39.8 2.2 %collective-permute-start.5 = (f32[256,128]{1,0:T(8,128)S(1)}, f32[256,128]{1,0:T(8,128)S(1)}, u32[]{:S(2)}, u32[]{:S(2)}) collective-permute-start(f32[256,128]{1,0:T(8,128)S(1)} %get-tuple-element.39.refs_1_), channel_id=1, source_target_pairs={{0,2},{2,0},{4,6},{6,4},{1,3},{3,1},{5,7},{7,5},{8,10},{10,8},{12,... | collective-permute-start | bytes 393224 | tf_op jit(solution)/shard_map/ppermute | solution.py:287
  43.0 3.8 %collective-permute-start.7 = (f32[256,128]{1,0:T(8,128)S(1)}, f32[256,128]{1,0:T(8,128)S(1)}, u32[]{:S(2)}, u32[]{:S(2)}) collective-permute-start(f32[256,128]{1,0:T(8,128)S(1)} %get-tuple-element.40.refs_1_), channel_id=1, source_target_pairs={{0,6},{2,4},{4,2},{6,0},{1,7},{3,5},{5,3},{7,1},{8,14},{10,12},{12... | collective-permute-start | bytes 393224 | tf_op jit(solution)/shard_map/ppermute | solution.py:287
  47.8 2.1 %collective-permute-done.7.d = f32[256,128]{1,0:T(8,128)S(1)} collective-permute-done((f32[256,128]{1,0:T(8,128)S(1)}, f32[256,128]{1,0:T(8,128)S(1)}, u32[]{:S(2)}, u32[]{:S(2)}) %collective-permute-start.7) | collective-permute-done | bytes 131104 | tf_op jit(solution)/shard_map/ppermute | solution.py:287
  49.9 24.7 %all_to_all.25.in_ref = f32[16,32,128]{2,1,0:T(8,128)S(1)} all-to-all(f32[16,32,128]{2,1,0:T(8,128)S(1)} %shard_map.95), channel_id=1, replica_groups=mesh['z2'=2,'z1'=2,'core'=2,'y4'=2,'y2'=2,'y1'=2,'x2'=2,'x1'=2,'zhi'=2] ..., dimensions={0} | all-to-all | bytes 524288 | tf_op jit(solution)/shard_map/all_to_all | solution.py:291
  74.6 14.3 %all_to_all.26 = bf16[32,32,128]{2,1,0:T(8,128)(2,1)S(1)} all-to-all(bf16[32,32,128]{2,1,0:T(8,128)(2,1)S(1)} %shard_map.96), channel_id=1, replica_groups=mesh['z2'=2,'z1'=2,'core'=2,'y4'=2,'y2'=2,'y1'=2,'x2'=2,'x1'=2,'zhi'=2] ..., dimensions={0} | all-to-all | bytes 524288 | tf_op jit(solution)/shard_map/all_to_all | solution.py:291
  88.9 5.9 %collective-permute-start.8 = (bf16[4,256,128]{2,1,0:T(8,128)(2,1)S(1)}, bf16[4,256,128]{2,1,0:T(8,128)(2,1)S(1)}, u32[]{:S(2)}, u32[]{:S(2)}) collective-permute-start(bf16[4,256,128]{2,1,0:T(8,128)(2,1)S(1)} %bitcast.4), channel_id=1, source_target_pairs={{0,64},{64,0},{1,65},{65,1},{2,66},{66,2},{3,67},{67,3},{4,68},{68... | collective-permute-start | bytes 786440 | tf_op jit(solution)/shard_map/ppermute | solution.py:287
  96.3 3.1 %collective-permute-start.9 = (f32[256,128]{1,0:T(8,128)S(1)}, f32[256,128]{1,0:T(8,128)S(1)}, u32[]{:S(2)}, u32[]{:S(2)}) collective-permute-start(f32[256,128]{1,0:T(8,128)S(1)} %get-tuple-element.49), channel_id=1, source_target_pairs={{0,256},{128,384},{256,0},{384,128},{1,257},{129,385},{257,1},{385... | collective-permute-start | bytes 393224 | tf_op jit(solution)/shard_map/ppermute | solution.py:287
  99.5 3.7 %collective-permute-start.10 = (f32[256,128]{1,0:T(8,128)S(1)}, f32[256,128]{1,0:T(8,128)S(1)}, u32[]{:S(2)}, u32[]{:S(2)}) collective-permute-start(f32[256,128]{1,0:T(8,128)S(1)} %get-tuple-element.50.after_ref), channel_id=1, source_target_pairs={{0,384},{128,256},{256,128},{384,0},{1,385},{129,257},{257,129},{3... | collective-permute-start | bytes 393224 | tf_op jit(solution)/shard_map/ppermute | solution.py:287
  103.7 2.1 %collective-permute-start.11 = (f32[256,128]{1,0:T(8,128)S(1)}, f32[256,128]{1,0:T(8,128)S(1)}, u32[]{:S(2)}, u32[]{:S(2)}) collective-permute-start(f32[256,128]{1,0:T(8,128)S(1)} %get-tuple-element.56), channel_id=1, source_target_pairs={{0,128},{128,0},{256,384},{384,256},{1,129},{129,1},{257,385},{385... | collective-permute-start | bytes 393224 | tf_op jit(solution)/shard_map/ppermute | solution.py:287
  105.8 3.7 %collective-permute-done.9.a = f32[256,128]{1,0:T(8,128)S(1)} collective-permute-done((f32[256,128]{1,0:T(8,128)S(1)}, f32[256,128]{1,0:T(8,128)S(1)}, u32[]{:S(2)}, u32[]{:S(2)}) %collective-permute-start.9) | collective-permute-done | bytes 131104 | tf_op jit(solution)/shard_map/ppermute | solution.py:287
  109.5 3.4 %collective-permute-done.11.near = f32[256,128]{1,0:T(8,128)S(1)} collective-permute-done((f32[256,128]{1,0:T(8,128)S(1)}, f32[256,128]{1,0:T(8,128)S(1)}, u32[]{:S(2)}, u32[]{:S(2)}) %collective-permute-start.11) | collective-permute-done | bytes 131104 | tf_op jit(solution)/shard_map/ppermute | solution.py:287
  113.6 11.9 %all_to_all.27.in_ref = f32[32,16,128]{2,1,0:T(8,128)S(1)} all-to-all(f32[32,16,128]{2,1,0:T(8,128)S(1)} %bitcast.7), channel_id=1, replica_groups=mesh['z2'=2,'z1'=2,'core'=2,'y4'=2,'y2'=2,'y1'=2,'x2'=2,'x1'=2,'zhi'=2] ..., dimensions={0} | all-to-all | bytes 524288 | tf_op jit(solution)/shard_map/all_to_all | solution.py:291
  125.5 15.3 %all_to_all.28.in_ref = f32[16,16,128]{2,1,0:T(8,128)S(1)} all-to-all(f32[16,16,128]{2,1,0:T(8,128)S(1)} %shard_map.102), channel_id=1, replica_groups=mesh['z2'=2,'z1'=2,'core'=2,'y4'=2,'y2'=2,'y1'=2,'x2'=2,'x1'=2,'zhi'=2] ..., dimensions={0} | all-to-all | bytes 262144 | tf_op jit(solution)/shard_map/all_to_all | solution.py:291
  140.8 13.3 %all_to_all.29 = f32[32,16,128]{2,1,0:T(8,128)S(1)} all-to-all(f32[32,16,128]{2,1,0:T(8,128)S(1)} %shard_map.103), channel_id=1, replica_groups=mesh['z2'=2,'z1'=2,'core'=2,'y4'=2,'y2'=2,'y1'=2,'x2'=2,'x1'=2,'zhi'=2] ..., dimensions={0} | all-to-all | bytes 524288 | tf_op jit(solution)/shard_map/all_to_all | solution.py:291
  154.1 7.7 %shard_map.104 = (f32[256,128]{1,0:T(8,128)}, f32[256,128]{1,0:T(8,128)}, f32[256,128]{1,0:T(8,128)}) custom-call(f32[512,128]{1,0:T(8,128)S(1)} %bitcast.6, f32[256,128]{1,0:T(8,128)S(1)} %get-tuple-element.58.applied_ref, f32[256,128]{1,0:T(8,128)S(1)} %copy-done, f32[256,128]{1,0:T(8,128)S(1)} %copy-done.1, f32[256,128]{1,0:T(8,128)S(1)} %copy-done.4), custom_call_target="tpu_custom_call" | custom-call | tf_op jit(solution)/shard_map/pallas_call | solution.py:39
  (37 shorter events, 12.4 us)
Async XLA Ops:
  0.6 19.9 %copy-start.5 = (bf16[1024,128]{1,0:T(8,128)(2,1)S(1)}, bf16[1024,128]{1,0:T(8,128)(2,1)}, u32[]{:S(2)}) copy-start(bf16[1024,128]{1,0:T(8,128)(2,1)} %samples_ref.1) | copy-start | bytes 786436
  0.6 22.3 %collective-permute-start = (bf16[1024,128]{1,0:T(8,128)(2,1)}, bf16[1024,128]{1,0:T(8,128)(2,1)S(1)}, u32[]{:S(2)}, u32[]{:S(2)}) collective-permute-start(bf16[1024,128]{1,0:T(8,128)(2,1)} %samples_ref.1), channel_id=1, source_target_pairs={{0,64},{64,0},{1,65},{65,1},{2,66},{66,2},{3,67},{67,3},{4,68},{68... | collective-permute-start | bytes 786440 | tf_op jit(solution)/shard_map/ppermute | solution.py:287
  11.3 17.3 %collective-permute-start.3 = (bf16[272,256]{1,0:T(8,128)(2,1)}, bf16[272,256]{1,0:T(8,128)(2,1)S(1)}, u32[]{:S(2)}, u32[]{:S(2)}) collective-permute-start(bf16[272,256]{1,0:T(8,128)(2,1)} %shard_map.85.pack_ref), channel_id=1, source_target_pairs={{0,384},{128,256},{256,128},{384,0},{1,385},{129,257},{257,129},{3... | collective-permute-start | bytes 417800 | tf_op jit(solution)/shard_map/ppermute | solution.py:287
  13.5 15.0 %collective-permute-start.2 = (bf16[272,256]{1,0:T(8,128)(2,1)}, bf16[272,256]{1,0:T(8,128)(2,1)S(1)}, u32[]{:S(2)}, u32[]{:S(2)}) collective-permute-start(bf16[272,256]{1,0:T(8,128)(2,1)} %shard_map.85.pack_ref), channel_id=1, source_target_pairs={{0,256},{128,384},{256,0},{384,128},{1,257},{129,385},{257,1},{385... | collective-permute-start | bytes 417800 | tf_op jit(solution)/shard_map/ppermute | solution.py:287
  15.4 11.7 %collective-permute-start.1 = (bf16[272,256]{1,0:T(8,128)(2,1)}, bf16[272,256]{1,0:T(8,128)(2,1)S(1)}, u32[]{:S(2)}, u32[]{:S(2)}) collective-permute-start(bf16[272,256]{1,0:T(8,128)(2,1)} %shard_map.85.pack_ref), channel_id=1, source_target_pairs={{0,128},{128,0},{256,384},{384,256},{1,129},{129,1},{257,385},{385... | collective-permute-start | bytes 417800 | tf_op jit(solution)/shard_map/ppermute | solution.py:287
  20.6 0.9 copy-start.2
  21.5 1.4 copy-start.3
  31.2 4.5 %collective-permute-start.4 = (f32[1024,128]{1,0:T(8,128)S(1)}, f32[1024,128]{1,0:T(8,128)S(1)}, u32[]{:S(2)}, u32[]{:S(2)}) collective-permute-start(f32[1024,128]{1,0:T(8,128)S(1)} %get-tuple-element.37.refs_0_), channel_id=1, source_target_pairs={{0,64},{64,0},{1,65},{65,1},{2,66},{66,2},{3,67},{67,3},{4,68},{68... | collective-permute-start | bytes 1572872 | tf_op jit(solution)/shard_map/ppermute | solution.py:287
  35.7 12.0 %collective-permute-start.6 = (f32[256,128]{1,0:T(8,128)S(1)}, f32[256,128]{1,0:T(8,128)S(1)}, u32[]{:S(2)}, u32[]{:S(2)}) collective-permute-start(f32[256,128]{1,0:T(8,128)S(1)} %shard_map.91.refs_1_), channel_id=1, source_target_pairs={{0,4},{2,6},{4,0},{6,2},{1,5},{3,7},{5,1},{7,3},{8,12},{10,14},{12... | collective-permute-start | bytes 393224 | tf_op jit(solution)/shard_map/ppermute | solution.py:287
  39.8 8.0 %collective-permute-start.5 = (f32[256,128]{1,0:T(8,128)S(1)}, f32[256,128]{1,0:T(8,128)S(1)}, u32[]{:S(2)}, u32[]{:S(2)}) collective-permute-start(f32[256,128]{1,0:T(8,128)S(1)} %get-tuple-element.39.refs_1_), channel_id=1, source_target_pairs={{0,2},{2,0},{4,6},{6,4},{1,3},{3,1},{5,7},{7,5},{8,10},{10,8},{12,... | collective-permute-start | bytes 393224 | tf_op jit(solution)/shard_map/ppermute | solution.py:287
  43.0 6.9 %collective-permute-start.7 = (f32[256,128]{1,0:T(8,128)S(1)}, f32[256,128]{1,0:T(8,128)S(1)}, u32[]{:S(2)}, u32[]{:S(2)}) collective-permute-start(f32[256,128]{1,0:T(8,128)S(1)} %get-tuple-element.40.refs_1_), channel_id=1, source_target_pairs={{0,6},{2,4},{4,2},{6,0},{1,7},{3,5},{5,3},{7,1},{8,14},{10,12},{12... | collective-permute-start | bytes 393224 | tf_op jit(solution)/shard_map/ppermute | solution.py:287
  88.9 7.0 %collective-permute-start.8 = (bf16[4,256,128]{2,1,0:T(8,128)(2,1)S(1)}, bf16[4,256,128]{2,1,0:T(8,128)(2,1)S(1)}, u32[]{:S(2)}, u32[]{:S(2)}) collective-permute-start(bf16[4,256,128]{2,1,0:T(8,128)(2,1)S(1)} %bitcast.4), channel_id=1, source_target_pairs={{0,64},{64,0},{1,65},{65,1},{2,66},{66,2},{3,67},{67,3},{4,68},{68... | collective-permute-start | bytes 786440 | tf_op jit(solution)/shard_map/ppermute | solution.py:287
  96.3 13.2 %collective-permute-start.9 = (f32[256,128]{1,0:T(8,128)S(1)}, f32[256,128]{1,0:T(8,128)S(1)}, u32[]{:S(2)}, u32[]{:S(2)}) collective-permute-start(f32[256,128]{1,0:T(8,128)S(1)} %get-tuple-element.49), channel_id=1, source_target_pairs={{0,256},{128,384},{256,0},{384,128},{1,257},{129,385},{257,1},{385... | collective-permute-start | bytes 393224 | tf_op jit(solution)/shard_map/ppermute | solution.py:287
  99.5 10.0 %collective-permute-start.10 = (f32[256,128]{1,0:T(8,128)S(1)}, f32[256,128]{1,0:T(8,128)S(1)}, u32[]{:S(2)}, u32[]{:S(2)}) collective-permute-start(f32[256,128]{1,0:T(8,128)S(1)} %get-tuple-element.50.after_ref), channel_id=1, source_target_pairs={{0,384},{128,256},{256,128},{384,0},{1,385},{129,257},{257,129},{3... | collective-permute-start | bytes 393224 | tf_op jit(solution)/shard_map/ppermute | solution.py:287
  103.7 9.3 %copy-start = (f32[256,128]{1,0:T(8,128)S(1)}, f32[256,128]{1,0:T(8,128)}, u32[]{:S(2)}) copy-start(f32[256,128]{1,0:T(8,128)} %dir_ref.3) | copy-start | bytes 393220
  103.7 9.2 %copy-start.1 = (f32[256,128]{1,0:T(8,128)S(1)}, f32[256,128]{1,0:T(8,128)}, u32[]{:S(2)}) copy-start(f32[256,128]{1,0:T(8,128)} %res_ref.3) | copy-start | bytes 393220
  103.7 9.2 %collective-permute-start.11 = (f32[256,128]{1,0:T(8,128)S(1)}, f32[256,128]{1,0:T(8,128)S(1)}, u32[]{:S(2)}, u32[]{:S(2)}) collective-permute-start(f32[256,128]{1,0:T(8,128)S(1)} %get-tuple-element.56), channel_id=1, source_target_pairs={{0,128},{128,0},{256,384},{384,256},{1,129},{129,1},{257,385},{385... | collective-permute-start | bytes 393224 | tf_op jit(solution)/shard_map/ppermute | solution.py:287
  140.8 13.3 %copy-start.4 = (f32[256,128]{1,0:T(8,128)S(1)}, f32[256,128]{1,0:T(8,128)}, u32[]{:S(2)}) copy-start(f32[256,128]{1,0:T(8,128)} %sol_ref.1) | copy-start | bytes 393220

commit v7 on v6

--- a/solution.py
+++ b/solution.py
@@ -233,7 +233,7 @@
             r = [jnp.where(inside, jnp.where(lane == k + i, 1.0, 0.0), rows[i]) for i in range(w)]
             inv, low = [], {}
             for j in range(w):
-                inv.append(1.0 / p[j, j])
+                inv.append(pl.reciprocal(p[j, j], approx=False))
                 for i in range(j + 1, w):
                     low[i, j] = p[i, j] * inv[j]
                 for i in range(j + 1, w):

time: 163 us -> 163 us (level)
  no operation moved by 1% of the time
where the time goes in v7:
time: 163 us; the launch traced here: 162 us
  blocking collectives  79.4 us (49%)
  starting transfers between devices  45 us (28%)
  Pallas kernels  22.5 us (14%)
  waiting for transfers between devices  13 us (8%)
    all_to_all x5, blocking collectives, exchange(): return lax.all_to_all(value, axes, 0, 0)  79.4 us
    ppermute x12, starting transfers between devices, swap(): return lax.ppermute(value, axes, [(i, i ^ s) for i in range(n)])  45 us
    pallas_call x19, Pallas kernels, call(): pl.pallas_call(kernel, out_shape=outs, in_specs=specs, out_specs=jax.tree...  20.8 us
    ppermute x12, waiting for transfers between devices, swap(): return lax.ppermute(value, axes, [(i, i ^ s) for i in range(n)])  13 us
  transfers between devices with their start and end apart: 12, of which 6 were waited for; matrix products, arithmetic and copies ran while one was open for 0% of the time, Pallas kernels for 7%

profile of v7, /device:TPU:1, one launch (start us, length us, event | category | flops | bytes accessed | tf_op | source)
XLA Modules:
  0.0 161.9 jit_solution(8517380297303736157)
XLA Ops:
  0.6 8.9 %collective-permute-start = (bf16[1024,128]{1,0:T(8,128)(2,1)}, bf16[1024,128]{1,0:T(8,128)(2,1)S(1)}, u32[]{:S(2)}, u32[]{:S(2)}) collective-permute-start(bf16[1024,128]{1,0:T(8,128)(2,1)} %samples_ref.1), channel_id=1, source_target_pairs={{0,64},{64,0},{1,65},{65,1},{2,66},{66,2},{3,67},{67,3},{4,68},{68... | collective-permute-start | bytes 786440 | tf_op jit(solution)/shard_map/ppermute | solution.py:287
  9.6 1.7 %shard_map.85.pack_ref = bf16[272,256]{1,0:T(8,128)(2,1)} custom-call(bf16[128,256]{1,0:T(8,128)(2,1)} %proj_in.1, bf16[1,256]{1,0:T(2,128)(2,1)} %shift_in.1, f32[256,128]{1,0:T(8,128)} %dir_ref.3), custom_call_target="tpu_custom_call" | custom-call | tf_op jit(solution)/shard_map/pallas_call | solution.py:297
  11.3 2.2 %collective-permute-start.3 = (bf16[272,256]{1,0:T(8,128)(2,1)}, bf16[272,256]{1,0:T(8,128)(2,1)S(1)}, u32[]{:S(2)}, u32[]{:S(2)}) collective-permute-start(bf16[272,256]{1,0:T(8,128)(2,1)} %shard_map.85.pack_ref), channel_id=1, source_target_pairs={{0,384},{128,256},{256,128},{384,0},{1,385},{129,257},{257,129},{3... | collective-permute-start | bytes 417800 | tf_op jit(solution)/shard_map/ppermute | solution.py:287
  13.5 1.9 %collective-permute-start.2 = (bf16[272,256]{1,0:T(8,128)(2,1)}, bf16[272,256]{1,0:T(8,128)(2,1)S(1)}, u32[]{:S(2)}, u32[]{:S(2)}) collective-permute-start(bf16[272,256]{1,0:T(8,128)(2,1)} %shard_map.85.pack_ref), channel_id=1, source_target_pairs={{0,256},{128,384},{256,0},{384,128},{1,257},{129,385},{257,1},{385... | collective-permute-start | bytes 417800 | tf_op jit(solution)/shard_map/ppermute | solution.py:287
  15.4 5.1 %collective-permute-start.1 = (bf16[272,256]{1,0:T(8,128)(2,1)}, bf16[272,256]{1,0:T(8,128)(2,1)S(1)}, u32[]{:S(2)}, u32[]{:S(2)}) collective-permute-start(bf16[272,256]{1,0:T(8,128)(2,1)} %shard_map.85.pack_ref), channel_id=1, source_target_pairs={{0,128},{128,0},{256,384},{384,256},{1,129},{129,1},{257,385},{385... | collective-permute-start | bytes 417800 | tf_op jit(solution)/shard_map/ppermute | solution.py:287
  24.3 2.8 %collective-permute-done.1.p1 = bf16[272,256]{1,0:T(8,128)(2,1)S(1)} collective-permute-done((bf16[272,256]{1,0:T(8,128)(2,1)}, bf16[272,256]{1,0:T(8,128)(2,1)S(1)}, u32[]{:S(2)}, u32[]{:S(2)}) %collective-permute-start.1) | collective-permute-done | bytes 139296 | tf_op jit(solution)/shard_map/ppermute | solution.py:287
  28.5 2.6 %shard_map.89 = (bf16[2,256,1024]{2,1,0:T(8,128)(2,1)S(1)}, f32[1024,128]{1,0:T(8,128)S(1)}) custom-call(bf16[128,1024]{1,0:T(8,128)(2,1)S(1)} %get-tuple-element.31.rows_t, f32[128,1024]{1,0:T(8,128)S(1)} %get-tuple-element.34.acc_in, bf16[272,256]{1,0:T(8,128)(2,1)S(1)} %collective-permute-done.2.p2, bf16[272,256]{1,0:T(8,128)(2,1)S(1)} %collective-permute-done.3.p3), custom_call_target="tpu_custom_call" | custom-call | flops 2684354560 | tf_op jit(solution)/shard_map/pallas_call | solution.py:39
  31.2 3.0 %collective-permute-start.4 = (f32[1024,128]{1,0:T(8,128)S(1)}, f32[1024,128]{1,0:T(8,128)S(1)}, u32[]{:S(2)}, u32[]{:S(2)}) collective-permute-start(f32[1024,128]{1,0:T(8,128)S(1)} %get-tuple-element.37.refs_0_), channel_id=1, source_target_pairs={{0,64},{64,0},{1,65},{65,1},{2,66},{66,2},{3,67},{67,3},{4,68},{68... | collective-permute-start | bytes 1572872 | tf_op jit(solution)/shard_map/ppermute | solution.py:287
  35.7 3.0 %collective-permute-start.6 = (f32[256,128]{1,0:T(8,128)S(1)}, f32[256,128]{1,0:T(8,128)S(1)}, u32[]{:S(2)}, u32[]{:S(2)}) collective-permute-start(f32[256,128]{1,0:T(8,128)S(1)} %shard_map.91.refs_1_), channel_id=1, source_target_pairs={{0,4},{2,6},{4,0},{6,2},{1,5},{3,7},{5,1},{7,3},{8,12},{10,14},{12... | collective-permute-start | bytes 393224 | tf_op jit(solution)/shard_map/ppermute | solution.py:287
  39.8 2.2 %collective-permute-start.5 = (f32[256,128]{1,0:T(8,128)S(1)}, f32[256,128]{1,0:T(8,128)S(1)}, u32[]{:S(2)}, u32[]{:S(2)}) collective-permute-start(f32[256,128]{1,0:T(8,128)S(1)} %get-tuple-element.39.refs_1_), channel_id=1, source_target_pairs={{0,2},{2,0},{4,6},{6,4},{1,3},{3,1},{5,7},{7,5},{8,10},{10,8},{12,... | collective-permute-start | bytes 393224 | tf_op jit(solution)/shard_map/ppermute | solution.py:287
  43.0 3.8 %collective-permute-start.7 = (f32[256,128]{1,0:T(8,128)S(1)}, f32[256,128]{1,0:T(8,128)S(1)}, u32[]{:S(2)}, u32[]{:S(2)}) collective-permute-start(f32[256,128]{1,0:T(8,128)S(1)} %get-tuple-element.40.refs_1_), channel_id=1, source_target_pairs={{0,6},{2,4},{4,2},{6,0},{1,7},{3,5},{5,3},{7,1},{8,14},{10,12},{12... | collective-permute-start | bytes 393224 | tf_op jit(solution)/shard_map/ppermute | solution.py:287
  47.8 2.1 %collective-permute-done.7.d = f32[256,128]{1,0:T(8,128)S(1)} collective-permute-done((f32[256,128]{1,0:T(8,128)S(1)}, f32[256,128]{1,0:T(8,128)S(1)}, u32[]{:S(2)}, u32[]{:S(2)}) %collective-permute-start.7) | collective-permute-done | bytes 131104 | tf_op jit(solution)/shard_map/ppermute | solution.py:287
  49.9 24.7 %all_to_all.25.in_ref = f32[16,32,128]{2,1,0:T(8,128)S(1)} all-to-all(f32[16,32,128]{2,1,0:T(8,128)S(1)} %shard_map.95), channel_id=1, replica_groups=mesh['z2'=2,'z1'=2,'core'=2,'y4'=2,'y2'=2,'y1'=2,'x2'=2,'x1'=2,'zhi'=2] ..., dimensions={0} | all-to-all | bytes 524288 | tf_op jit(solution)/shard_map/all_to_all | solution.py:291
  74.6 14.3 %all_to_all.26 = bf16[32,32,128]{2,1,0:T(8,128)(2,1)S(1)} all-to-all(bf16[32,32,128]{2,1,0:T(8,128)(2,1)S(1)} %shard_map.96), channel_id=1, replica_groups=mesh['z2'=2,'z1'=2,'core'=2,'y4'=2,'y2'=2,'y1'=2,'x2'=2,'x1'=2,'zhi'=2] ..., dimensions={0} | all-to-all | bytes 524288 | tf_op jit(solution)/shard_map/all_to_all | solution.py:291
  88.9 5.9 %collective-permute-start.8 = (bf16[4,256,128]{2,1,0:T(8,128)(2,1)S(1)}, bf16[4,256,128]{2,1,0:T(8,128)(2,1)S(1)}, u32[]{:S(2)}, u32[]{:S(2)}) collective-permute-start(bf16[4,256,128]{2,1,0:T(8,128)(2,1)S(1)} %bitcast.4), channel_id=1, source_target_pairs={{0,64},{64,0},{1,65},{65,1},{2,66},{66,2},{3,67},{67,3},{4,68},{68... | collective-permute-start | bytes 786440 | tf_op jit(solution)/shard_map/ppermute | solution.py:287
  96.3 3.1 %collective-permute-start.9 = (f32[256,128]{1,0:T(8,128)S(1)}, f32[256,128]{1,0:T(8,128)S(1)}, u32[]{:S(2)}, u32[]{:S(2)}) collective-permute-start(f32[256,128]{1,0:T(8,128)S(1)} %get-tuple-element.49), channel_id=1, source_target_pairs={{0,256},{128,384},{256,0},{384,128},{1,257},{129,385},{257,1},{385... | collective-permute-start | bytes 393224 | tf_op jit(solution)/shard_map/ppermute | solution.py:287
  99.5 3.7 %collective-permute-start.10 = (f32[256,128]{1,0:T(8,128)S(1)}, f32[256,128]{1,0:T(8,128)S(1)}, u32[]{:S(2)}, u32[]{:S(2)}) collective-permute-start(f32[256,128]{1,0:T(8,128)S(1)} %get-tuple-element.50.after_ref), channel_id=1, source_target_pairs={{0,384},{128,256},{256,128},{384,0},{1,385},{129,257},{257,129},{3... | collective-permute-start | bytes 393224 | tf_op jit(solution)/shard_map/ppermute | solution.py:287
  103.7 2.1 %collective-permute-start.11 = (f32[256,128]{1,0:T(8,128)S(1)}, f32[256,128]{1,0:T(8,128)S(1)}, u32[]{:S(2)}, u32[]{:S(2)}) collective-permute-start(f32[256,128]{1,0:T(8,128)S(1)} %get-tuple-element.56), channel_id=1, source_target_pairs={{0,128},{128,0},{256,384},{384,256},{1,129},{129,1},{257,385},{385... | collective-permute-start | bytes 393224 | tf_op jit(solution)/shard_map/ppermute | solution.py:287
  105.8 3.7 %collective-permute-done.9.a = f32[256,128]{1,0:T(8,128)S(1)} collective-permute-done((f32[256,128]{1,0:T(8,128)S(1)}, f32[256,128]{1,0:T(8,128)S(1)}, u32[]{:S(2)}, u32[]{:S(2)}) %collective-permute-start.9) | collective-permute-done | bytes 131104 | tf_op jit(solution)/shard_map/ppermute | solution.py:287
  109.5 3.4 %collective-permute-done.11.near = f32[256,128]{1,0:T(8,128)S(1)} collective-permute-done((f32[256,128]{1,0:T(8,128)S(1)}, f32[256,128]{1,0:T(8,128)S(1)}, u32[]{:S(2)}, u32[]{:S(2)}) %collective-permute-start.11) | collective-permute-done | bytes 131104 | tf_op jit(solution)/shard_map/ppermute | solution.py:287
  113.6 11.9 %all_to_all.27.in_ref = f32[32,16,128]{2,1,0:T(8,128)S(1)} all-to-all(f32[32,16,128]{2,1,0:T(8,128)S(1)} %bitcast.7), channel_id=1, replica_groups=mesh['z2'=2,'z1'=2,'core'=2,'y4'=2,'y2'=2,'y1'=2,'x2'=2,'x1'=2,'zhi'=2] ..., dimensions={0} | all-to-all | bytes 524288 | tf_op jit(solution)/shard_map/all_to_all | solution.py:291
  125.5 15.3 %all_to_all.28.in_ref = f32[16,16,128]{2,1,0:T(8,128)S(1)} all-to-all(f32[16,16,128]{2,1,0:T(8,128)S(1)} %shard_map.102), channel_id=1, replica_groups=mesh['z2'=2,'z1'=2,'core'=2,'y4'=2,'y2'=2,'y1'=2,'x2'=2,'x1'=2,'zhi'=2] ..., dimensions={0} | all-to-all | bytes 262144 | tf_op jit(solution)/shard_map/all_to_all | solution.py:291
  140.8 13.3 %all_to_all.29 = f32[32,16,128]{2,1,0:T(8,128)S(1)} all-to-all(f32[32,16,128]{2,1,0:T(8,128)S(1)} %shard_map.103), channel_id=1, replica_groups=mesh['z2'=2,'z1'=2,'core'=2,'y4'=2,'y2'=2,'y1'=2,'x2'=2,'x1'=2,'zhi'=2] ..., dimensions={0} | all-to-all | bytes 524288 | tf_op jit(solution)/shard_map/all_to_all | solution.py:291
  154.1 7.7 %shard_map.104 = (f32[256,128]{1,0:T(8,128)}, f32[256,128]{1,0:T(8,128)}, f32[256,128]{1,0:T(8,128)}) custom-call(f32[512,128]{1,0:T(8,128)S(1)} %bitcast.6, f32[256,128]{1,0:T(8,128)S(1)} %get-tuple-element.58.applied_ref, f32[256,128]{1,0:T(8,128)S(1)} %copy-done, f32[256,128]{1,0:T(8,128)S(1)} %copy-done.1, f32[256,128]{1,0:T(8,128)S(1)} %copy-done.4), custom_call_target="tpu_custom_call" | custom-call | tf_op jit(solution)/shard_map/pallas_call | solution.py:39
  (37 shorter events, 12.4 us)
Async XLA Ops:
  0.6 19.9 %copy-start.5 = (bf16[1024,128]{1,0:T(8,128)(2,1)S(1)}, bf16[1024,128]{1,0:T(8,128)(2,1)}, u32[]{:S(2)}) copy-start(bf16[1024,128]{1,0:T(8,128)(2,1)} %samples_ref.1) | copy-start | bytes 786436
  0.6 22.3 %collective-permute-start = (bf16[1024,128]{1,0:T(8,128)(2,1)}, bf16[1024,128]{1,0:T(8,128)(2,1)S(1)}, u32[]{:S(2)}, u32[]{:S(2)}) collective-permute-start(bf16[1024,128]{1,0:T(8,128)(2,1)} %samples_ref.1), channel_id=1, source_target_pairs={{0,64},{64,0},{1,65},{65,1},{2,66},{66,2},{3,67},{67,3},{4,68},{68... | collective-permute-start | bytes 786440 | tf_op jit(solution)/shard_map/ppermute | solution.py:287
  11.3 17.3 %collective-permute-start.3 = (bf16[272,256]{1,0:T(8,128)(2,1)}, bf16[272,256]{1,0:T(8,128)(2,1)S(1)}, u32[]{:S(2)}, u32[]{:S(2)}) collective-permute-start(bf16[272,256]{1,0:T(8,128)(2,1)} %shard_map.85.pack_ref), channel_id=1, source_target_pairs={{0,384},{128,256},{256,128},{384,0},{1,385},{129,257},{257,129},{3... | collective-permute-start | bytes 417800 | tf_op jit(solution)/shard_map/ppermute | solution.py:287
  13.5 15.0 %collective-permute-start.2 = (bf16[272,256]{1,0:T(8,128)(2,1)}, bf16[272,256]{1,0:T(8,128)(2,1)S(1)}, u32[]{:S(2)}, u32[]{:S(2)}) collective-permute-start(bf16[272,256]{1,0:T(8,128)(2,1)} %shard_map.85.pack_ref), channel_id=1, source_target_pairs={{0,256},{128,384},{256,0},{384,128},{1,257},{129,385},{257,1},{385... | collective-permute-start | bytes 417800 | tf_op jit(solution)/shard_map/ppermute | solution.py:287
  15.4 11.7 %collective-permute-start.1 = (bf16[272,256]{1,0:T(8,128)(2,1)}, bf16[272,256]{1,0:T(8,128)(2,1)S(1)}, u32[]{:S(2)}, u32[]{:S(2)}) collective-permute-start(bf16[272,256]{1,0:T(8,128)(2,1)} %shard_map.85.pack_ref), channel_id=1, source_target_pairs={{0,128},{128,0},{256,384},{384,256},{1,129},{129,1},{257,385},{385... | collective-permute-start | bytes 417800 | tf_op jit(solution)/shard_map/ppermute | solution.py:287
  20.6 0.9 copy-start.2
  21.5 1.4 copy-start.3
  31.2 4.5 %collective-permute-start.4 = (f32[1024,128]{1,0:T(8,128)S(1)}, f32[1024,128]{1,0:T(8,128)S(1)}, u32[]{:S(2)}, u32[]{:S(2)}) collective-permute-start(f32[1024,128]{1,0:T(8,128)S(1)} %get-tuple-element.37.refs_0_), channel_id=1, source_target_pairs={{0,64},{64,0},{1,65},{65,1},{2,66},{66,2},{3,67},{67,3},{4,68},{68... | collective-permute-start | bytes 1572872 | tf_op jit(solution)/shard_map/ppermute | solution.py:287
  35.7 12.0 %collective-permute-start.6 = (f32[256,128]{1,0:T(8,128)S(1)}, f32[256,128]{1,0:T(8,128)S(1)}, u32[]{:S(2)}, u32[]{:S(2)}) collective-permute-start(f32[256,128]{1,0:T(8,128)S(1)} %shard_map.91.refs_1_), channel_id=1, source_target_pairs={{0,4},{2,6},{4,0},{6,2},{1,5},{3,7},{5,1},{7,3},{8,12},{10,14},{12... | collective-permute-start | bytes 393224 | tf_op jit(solution)/shard_map/ppermute | solution.py:287
  39.8 8.0 %collective-permute-start.5 = (f32[256,128]{1,0:T(8,128)S(1)}, f32[256,128]{1,0:T(8,128)S(1)}, u32[]{:S(2)}, u32[]{:S(2)}) collective-permute-start(f32[256,128]{1,0:T(8,128)S(1)} %get-tuple-element.39.refs_1_), channel_id=1, source_target_pairs={{0,2},{2,0},{4,6},{6,4},{1,3},{3,1},{5,7},{7,5},{8,10},{10,8},{12,... | collective-permute-start | bytes 393224 | tf_op jit(solution)/shard_map/ppermute | solution.py:287
  43.0 6.9 %collective-permute-start.7 = (f32[256,128]{1,0:T(8,128)S(1)}, f32[256,128]{1,0:T(8,128)S(1)}, u32[]{:S(2)}, u32[]{:S(2)}) collective-permute-start(f32[256,128]{1,0:T(8,128)S(1)} %get-tuple-element.40.refs_1_), channel_id=1, source_target_pairs={{0,6},{2,4},{4,2},{6,0},{1,7},{3,5},{5,3},{7,1},{8,14},{10,12},{12... | collective-permute-start | bytes 393224 | tf_op jit(solution)/shard_map/ppermute | solution.py:287
  88.9 7.0 %collective-permute-start.8 = (bf16[4,256,128]{2,1,0:T(8,128)(2,1)S(1)}, bf16[4,256,128]{2,1,0:T(8,128)(2,1)S(1)}, u32[]{:S(2)}, u32[]{:S(2)}) collective-permute-start(bf16[4,256,128]{2,1,0:T(8,128)(2,1)S(1)} %bitcast.4), channel_id=1, source_target_pairs={{0,64},{64,0},{1,65},{65,1},{2,66},{66,2},{3,67},{67,3},{4,68},{68... | collective-permute-start | bytes 786440 | tf_op jit(solution)/shard_map/ppermute | solution.py:287
  96.3 13.2 %collective-permute-start.9 = (f32[256,128]{1,0:T(8,128)S(1)}, f32[256,128]{1,0:T(8,128)S(1)}, u32[]{:S(2)}, u32[]{:S(2)}) collective-permute-start(f32[256,128]{1,0:T(8,128)S(1)} %get-tuple-element.49), channel_id=1, source_target_pairs={{0,256},{128,384},{256,0},{384,128},{1,257},{129,385},{257,1},{385... | collective-permute-start | bytes 393224 | tf_op jit(solution)/shard_map/ppermute | solution.py:287
  99.5 10.0 %collective-permute-start.10 = (f32[256,128]{1,0:T(8,128)S(1)}, f32[256,128]{1,0:T(8,128)S(1)}, u32[]{:S(2)}, u32[]{:S(2)}) collective-permute-start(f32[256,128]{1,0:T(8,128)S(1)} %get-tuple-element.50.after_ref), channel_id=1, source_target_pairs={{0,384},{128,256},{256,128},{384,0},{1,385},{129,257},{257,129},{3... | collective-permute-start | bytes 393224 | tf_op jit(solution)/shard_map/ppermute | solution.py:287
  103.7 9.3 %copy-start = (f32[256,128]{1,0:T(8,128)S(1)}, f32[256,128]{1,0:T(8,128)}, u32[]{:S(2)}) copy-start(f32[256,128]{1,0:T(8,128)} %dir_ref.3) | copy-start | bytes 393220
  103.7 9.2 %copy-start.1 = (f32[256,128]{1,0:T(8,128)S(1)}, f32[256,128]{1,0:T(8,128)}, u32[]{:S(2)}) copy-start(f32[256,128]{1,0:T(8,128)} %res_ref.3) | copy-start | bytes 393220
  103.7 9.2 %collective-permute-start.11 = (f32[256,128]{1,0:T(8,128)S(1)}, f32[256,128]{1,0:T(8,128)S(1)}, u32[]{:S(2)}, u32[]{:S(2)}) collective-permute-start(f32[256,128]{1,0:T(8,128)S(1)} %get-tuple-element.56), channel_id=1, source_target_pairs={{0,128},{128,0},{256,384},{384,256},{1,129},{129,1},{257,385},{385... | collective-permute-start | bytes 393224 | tf_op jit(solution)/shard_map/ppermute | solution.py:287
  140.8 13.3 %copy-start.4 = (f32[256,128]{1,0:T(8,128)S(1)}, f32[256,128]{1,0:T(8,128)}, u32[]{:S(2)}) copy-start(f32[256,128]{1,0:T(8,128)} %sol_ref.1) | copy-start | bytes 393220
